TPU v7x, 32 devices: a whole 2x2x4 slice. The times are simulated.
32 devices in a mesh: seq: 8 (over y, x, core), head: 4 (over z).
Axes of the slice: x: 2, y: 2, z: 4, core: 2. Of those that a mesh axis runs over, the one named last changes fastest.
Arguments:
- x_in: bfloat16 [12288, 768], P(('seq', 'head')), may hold values from -6 to 6
- lengths: int32 [8], P('seq'), may hold values from 1 to 1536, 6144 in all
- cotangent: bfloat16 [12288, 768], P(('seq', 'head')), may hold values from -6 to 6
- w_in: float32 [768, 3224], P('seq', 'head'), may hold values from -0.21875 to 0.21875
- w_out: float32 [1536, 768], P('head', 'seq'), may hold values from -0.15625 to 0.15625
- small_params: float32 [10696], replicated, may hold values from -8 to 1.5, as said below
- row_in: float32 [768], P('seq'), may hold values from 2457.6 to 9830.4
- col_in: float32 [3224], P('head'), may hold values from 2457.6 to 9830.4
- row_out: float32 [1536], P('head'), may hold values from 6144 to 24576
- col_out: float32 [768], P('seq'), may hold values from 6144 to 24576
- small_second: float32 [10696], replicated, may hold values from 245.76 to 12288
Outputs:
- out: bfloat16 [12288, 768], P(('seq', 'head'))
- grad_x: float32 [12288, 768], P(('seq', 'head'))
- grad_in: float32 [768, 3224], P('seq', 'head')
- row_in_new: float32 [768], P('seq')
- col_in_new: float32 [3224], P('head')
- w_in_new: float32 [768, 3224], P('seq', 'head')
- grad_out: float32 [1536, 768], P('head', 'seq')
- row_out_new: float32 [1536], P('head')
- col_out_new: float32 [768], P('seq')
- w_out_new: float32 [1536, 768], P('head', 'seq')
- small_grad: float32 [10696], replicated
- small_second_new: float32 [10696], replicated
- small_new: float32 [10696], replicated
Inputs may be any that keep to these rules, and one draw needn't show every extreme that they name: `small_params`: step biases lie in -8 to -3, log rates in 0 to 1.5, skip gains and both norm gains in 0.5 to 1.5, convolution taps within 0.9 and its bias within 0.5 of zero.
All inputs are finite; a program needn't handle non-finite values. No bound on the sum of `lengths` on one device may be relied on, other than what follows from the above.
Results may differ from a plain program's by a relative error of at most 0.0023.
The roundings to bfloat16 on the way count: a program that leaves them out, or rounds other values in their place, can miss the bound.
Values may be sent and summed in bfloat16 or wider, within the bound.
A program may use at most 128 MiB of HBM per device.

v0:
```python
import jax
import jax.numpy as jnp
from jax import lax
from jax.sharding import PartitionSpec as P

D = 768
HEADS = 24
HEAD_DIM = 64
STATE = 64
CONV = 4
SPAN = 128
STEP = 8
INNER = 1536
CONV_CH = 1664
PROJ = 3224


EPS = 1e-05
EPS_SQUARE = 1e-30
LEARN_RATE = 0.3
LEARN_SMALL = 3.0
CLIP_RMS = 0.1
PRECISE = lax.Precision.HIGHEST


def shifted(value, axis, steps):
    count = lax.axis_size(axis)
    first, last = (max(0, -steps), min(count, count - steps))
    return lax.ppermute(value, axis, [(source, source + steps) for source in range(first, last)])


def silu_gate(value):
    return value * jax.nn.sigmoid(value)


def unpack(small):
    first = D
    norm_gain = small[:first]
    conv_weight = small[first : first + CONV * CONV_CH].reshape(CONV, CONV_CH)
    first = first + CONV * CONV_CH
    conv_bias = small[first : first + CONV_CH]
    first = first + CONV_CH
    step_bias = small[first : first + HEADS]
    log_rates = small[first + HEADS : first + 2 * HEADS]
    skip_gain = small[first + 2 * HEADS : first + 3 * HEADS]
    out_gain = small[first + 3 * HEADS : first + 3 * HEADS + INNER]
    return (norm_gain, conv_weight, conv_bias, step_bias, log_rates, skip_gain, out_gain)


def norm_rows(values, gain):
    return values * lax.rsqrt(jnp.mean(values * values, axis=1, keepdims=True) + EPS) * gain


def gate_rows(heads_in, gate_vals, gain):
    gated = heads_in * silu_gate(gate_vals)
    return gated * lax.rsqrt(jnp.mean(gated * gated, axis=1, keepdims=True) + EPS) * gain


def conv_rows(padded, weight, bias):
    row_count = padded.shape[0] - (CONV - 1)
    total = jnp.zeros((row_count, padded.shape[1]), jnp.float32) + bias[None, :]
    for offset in range(CONV):
        total = total + weight[offset][None, :] * padded[offset : offset + row_count]
    return silu_gate(total)


def direction_scan(xheads, steps, rates, bmaps, cmaps):
    length = xheads.shape[0]
    head_count = xheads.shape[1]
    head_size = xheads.shape[2]
    state_size = bmaps.shape[1]
    blocks = length // SPAN
    x_blocks = xheads.reshape(blocks, SPAN, head_count, head_size)
    step_blocks = steps.reshape(blocks, SPAN, head_count)
    b_blocks = bmaps.reshape(blocks, SPAN, state_size)
    c_blocks = cmaps.reshape(blocks, SPAN, state_size)
    causal_mask = jnp.arange(SPAN)[:, None] >= jnp.arange(SPAN)[None, :]
    log_decay = jnp.cumsum(step_blocks * rates[None, None, :], axis=1)
    decay_heads = log_decay.transpose(0, 2, 1)
    log_gaps = decay_heads[:, :, :, None] - decay_heads[:, :, None, :]
    decay_table = jnp.exp(jnp.where(causal_mask[None, None], log_gaps, -10000.0))
    intersection = jnp.einsum("ktn,ksn->kts", c_blocks, b_blocks, precision=PRECISE)
    mixing = intersection[:, None] * decay_table * step_blocks.transpose(0, 2, 1)[:, :, None, :]
    within = jnp.einsum("khts,kshp->kthp", mixing, x_blocks, precision=PRECISE)
    tail_weight = jnp.exp(log_decay[:, -1:, :] - log_decay) * step_blocks
    block_states = jnp.einsum(
        "ksh,kshp,ksn->khpn", tail_weight, x_blocks, b_blocks, precision=PRECISE
    )
    block_decay = jnp.exp(log_decay[:, -1, :])

    def advance(carried_state, block_data):
        decay_part, fresh = block_data
        return (carried_state * decay_part[:, None, None] + fresh, carried_state)

    state_init = jnp.zeros((head_count, head_size, state_size), jnp.float32)
    _, entering = lax.scan(advance, state_init, (block_decay, block_states))
    carried = (
        jnp.einsum("ktn,khpn->kthp", c_blocks, entering, precision=PRECISE)
        * jnp.exp(log_decay)[:, :, :, None]
    )
    return (within + carried).reshape(length, head_count, head_size)


def mixer_heads(xheads, raw_steps, bmaps, cmaps, step_bias, log_rates, skip_gain, valid_rows):
    steps = jax.nn.softplus(raw_steps + step_bias[None, :]) * valid_rows[:, None]
    rates = -jnp.exp(log_rates)
    forward_part = direction_scan(xheads, steps, rates, bmaps, cmaps)
    backward_part = direction_scan(xheads[::-1], steps[::-1], rates, bmaps[::-1], cmaps[::-1])[::-1]
    return forward_part + backward_part + skip_gain[None, :, None] * xheads


def contract_rows(left, right):
    return lax.dot_general(
        left, right, (((0,), (0,)), ((), ())), preferred_element_type=jnp.float32
    )


def contract_cols(left, right):
    return lax.dot_general(
        left, right, (((1,), (1,)), ((), ())), preferred_element_type=jnp.float32
    )


def on_device(
    x_in,
    lengths,
    cotangent,
    w_in,
    w_out,
    small_params,
    row_in,
    col_in,
    row_out,
    col_out,
    small_second,
):
    seq_count = lax.axis_size("seq")
    head_count = lax.axis_size("head")
    seq_index = lax.axis_index("seq")
    head_index = lax.axis_index("head")
    tok_rows = x_in.shape[0]
    heads_dev = HEADS // head_count
    head_width = heads_dev * HEAD_DIM
    seq_rows = tok_rows * head_count
    side_width = heads_dev + 2 * STATE
    in_part, out_part = (
        lax.all_gather(w_in.astype(jnp.bfloat16), "seq", axis=0, tiled=True),
        lax.all_gather(w_out.astype(jnp.bfloat16), "seq", axis=1, tiled=True),
    )
    in_full, out_full = (
        lax.all_gather(in_part, "head", axis=1, tiled=True),
        lax.all_gather(out_part, "head", axis=0, tiled=True),
    )
    norm_gain, conv_weight, conv_bias, step_bias, log_rates, skip_gain, out_gain = unpack(
        small_params
    )
    seq_length = lengths[0]
    valid_rows = (head_index * tok_rows + jnp.arange(tok_rows) < seq_length).astype(jnp.float32)
    seq_valid = (jnp.arange(seq_rows) < seq_length).astype(jnp.float32)
    inputs = x_in.astype(jnp.float32)
    normed, norm_pull = jax.vjp(norm_rows, inputs, norm_gain)
    normed_low = normed.astype(jnp.bfloat16)
    projected = jnp.dot(normed_low, in_full, preferred_element_type=jnp.float32).astype(
        jnp.bfloat16
    )
    gate_in = projected[:, :INNER]
    conv_in = projected[:, INNER : INNER + CONV_CH]
    raw_steps = projected[:, INNER + CONV_CH :]
    edge_rows = shifted(conv_in[tok_rows - (CONV - 1) :], "head", 1)
    padded = jnp.concatenate([edge_rows, conv_in], axis=0).astype(jnp.float32)
    convolved, conv_pull = jax.vjp(conv_rows, padded, conv_weight, conv_bias)
    conv_low = convolved.astype(jnp.bfloat16)
    x_send = conv_low[:, :INNER].reshape(tok_rows, head_count, head_width)
    maps_low = conv_low[:, INNER:]
    side_send = jnp.concatenate(
        [
            raw_steps.reshape(tok_rows, head_count, heads_dev),
            jnp.broadcast_to(maps_low[:, None, :], (tok_rows, head_count, 2 * STATE)),
        ],
        axis=2,
    )
    x_heads, side_heads = (
        lax.all_to_all(x_send, "head", split_axis=1, concat_axis=0, tiled=True),
        lax.all_to_all(side_send, "head", split_axis=1, concat_axis=0, tiled=True),
    )
    head_start = head_index * heads_dev
    bias_part = lax.dynamic_slice_in_dim(step_bias, head_start, heads_dev)
    rate_part = lax.dynamic_slice_in_dim(log_rates, head_start, heads_dev)
    skip_part = lax.dynamic_slice_in_dim(skip_gain, head_start, heads_dev)

    def ssd_local(xheads, raw_part, bmaps, cmaps, bias_in, rate_in, skip_in):
        mixed_part = mixer_heads(
            xheads, raw_part, bmaps, cmaps, bias_in, rate_in, skip_in, seq_valid
        )
        return mixed_part.reshape(seq_rows, head_width)

    side_float = side_heads[:, 0, :].astype(jnp.float32)
    mixed, ssd_pull = jax.vjp(
        ssd_local,
        x_heads.reshape(seq_rows, heads_dev, HEAD_DIM).astype(jnp.float32),
        side_float[:, :heads_dev],
        side_float[:, heads_dev : heads_dev + STATE],
        side_float[:, heads_dev + STATE :],
        bias_part,
        rate_part,
        skip_part,
    )
    heads_out = lax.all_to_all(
        mixed.astype(jnp.bfloat16).reshape(seq_rows, 1, head_width),
        "head",
        split_axis=0,
        concat_axis=1,
        tiled=True,
    ).reshape(tok_rows, INNER)
    gate_normed, gate_pull = jax.vjp(
        gate_rows, heads_out.astype(jnp.float32), gate_in.astype(jnp.float32), out_gain
    )
    gate_low = gate_normed.astype(jnp.bfloat16)
    branch = jnp.dot(gate_low, out_full, preferred_element_type=jnp.float32)
    result = (inputs + valid_rows[:, None] * branch).astype(jnp.bfloat16)
    back_in = cotangent.astype(jnp.float32)
    branch_grad = (valid_rows[:, None] * back_in).astype(jnp.bfloat16)
    grad_wout = contract_rows(gate_low, branch_grad)
    gate_grad = contract_cols(branch_grad, out_full)
    heads_grad, gate_in_grad, out_gain_grad = gate_pull(gate_grad)
    heads_send = heads_grad.astype(jnp.bfloat16).reshape(tok_rows, head_count, head_width)
    heads_back = lax.all_to_all(
        heads_send, "head", split_axis=1, concat_axis=0, tiled=True
    ).reshape(seq_rows, head_width)
    x_grad, raw_grad, bmap_grad, cmap_grad, bias_grad, rate_grad, skip_grad = ssd_pull(
        heads_back.astype(jnp.float32)
    )
    back_side = jnp.concatenate([raw_grad, bmap_grad, cmap_grad], axis=1).reshape(
        seq_rows, 1, side_width
    )
    tok_x_grad, tok_side_grad = (
        lax.all_to_all(
            x_grad.reshape(seq_rows, 1, head_width), "head", split_axis=0, concat_axis=1, tiled=True
        ),
        lax.all_to_all(back_side, "head", split_axis=0, concat_axis=1, tiled=True),
    )
    conv_grad = jnp.concatenate(
        [tok_x_grad.reshape(tok_rows, INNER), jnp.sum(tok_side_grad[:, :, heads_dev:], axis=1)],
        axis=1,
    )
    steps_grad = tok_side_grad[:, :, :heads_dev].reshape(tok_rows, HEADS)
    padded_grad, conv_weight_grad, conv_bias_grad = conv_pull(conv_grad)
    spill_grad = shifted(padded_grad[: CONV - 1], "head", -1)
    conv_in_grad = padded_grad[CONV - 1 :].at[tok_rows - (CONV - 1) :].add(spill_grad)
    proj_grad = jnp.concatenate([gate_in_grad, conv_in_grad, steps_grad], axis=1).astype(
        jnp.bfloat16
    )
    grad_win = contract_rows(normed_low, proj_grad)
    normed_grad = contract_cols(proj_grad, in_full)
    input_grad, norm_gain_grad = norm_pull(normed_grad)
    grad_x = back_in + input_grad
    zero_heads = jnp.zeros((HEADS,), jnp.float32)
    small_part = jnp.concatenate(
        [
            norm_gain_grad,
            conv_weight_grad.reshape(-1),
            conv_bias_grad,
            lax.dynamic_update_slice_in_dim(zero_heads, bias_grad, head_start, 0),
            lax.dynamic_update_slice_in_dim(zero_heads, rate_grad, head_start, 0),
            lax.dynamic_update_slice_in_dim(zero_heads, skip_grad, head_start, 0),
            out_gain_grad,
        ]
    )
    head_in, head_out = (
        lax.psum_scatter(grad_win, "head", scatter_dimension=1, tiled=True),
        lax.psum_scatter(grad_wout, "head", scatter_dimension=0, tiled=True),
    )
    grad_in, grad_out = (
        lax.psum_scatter(head_in, "seq", scatter_dimension=0, tiled=True),
        lax.psum_scatter(head_out, "seq", scatter_dimension=1, tiled=True),
    )
    square_in = grad_in * grad_in
    square_out = grad_out * grad_out
    rows_in = grad_in.shape[0]
    cols_in = grad_in.shape[1]
    rows_out = grad_out.shape[0]
    cols_out = grad_out.shape[1]
    row_in_part = lax.dynamic_update_slice_in_dim(
        jnp.zeros((D,), jnp.float32), jnp.sum(square_in, axis=1), seq_index * rows_in, 0
    )
    col_in_part = lax.dynamic_update_slice_in_dim(
        jnp.zeros((PROJ,), jnp.float32), jnp.sum(square_in, axis=0), head_index * cols_in, 0
    )
    row_out_part = lax.dynamic_update_slice_in_dim(
        jnp.zeros((INNER,), jnp.float32), jnp.sum(square_out, axis=1), head_index * rows_out, 0
    )
    col_out_part = lax.dynamic_update_slice_in_dim(
        jnp.zeros((D,), jnp.float32), jnp.sum(square_out, axis=0), seq_index * cols_out, 0
    )
    old_totals = jnp.stack([jnp.sum(row_in) / head_count, jnp.sum(row_out) / seq_count])
    small_grad, row_in_total, col_in_total, row_out_total, col_out_total, old_total = lax.psum(
        (small_part, row_in_part, col_in_part, row_out_part, col_out_part, old_totals),
        ("seq", "head"),
    )
    decay = 1.0 - STEP ** (-0.8)
    row_in_new = decay * row_in + (1.0 - decay) * (
        lax.dynamic_slice_in_dim(row_in_total, seq_index * rows_in, rows_in) / PROJ + EPS_SQUARE
    )
    col_in_new = decay * col_in + (1.0 - decay) * (
        lax.dynamic_slice_in_dim(col_in_total, head_index * cols_in, cols_in) / D + EPS_SQUARE
    )
    mean_in = decay * old_total[0] / D + (1.0 - decay) * (
        jnp.sum(row_in_total) / (D * PROJ) + EPS_SQUARE
    )
    row_out_new = decay * row_out + (1.0 - decay) * (
        lax.dynamic_slice_in_dim(row_out_total, head_index * rows_out, rows_out) / D + EPS_SQUARE
    )
    col_out_new = decay * col_out + (1.0 - decay) * (
        lax.dynamic_slice_in_dim(col_out_total, seq_index * cols_out, cols_out) / INNER + EPS_SQUARE
    )
    mean_out = decay * old_total[1] / INNER + (1.0 - decay) * (
        jnp.sum(row_out_total) / (INNER * D) + EPS_SQUARE
    )
    scaled_in = grad_in * lax.rsqrt(row_in_new[:, None] * col_in_new[None, :] / mean_in)
    scaled_out = grad_out * lax.rsqrt(row_out_new[:, None] * col_out_new[None, :] / mean_out)
    update_sums = lax.psum(
        jnp.stack([jnp.sum(scaled_in * scaled_in), jnp.sum(scaled_out * scaled_out)]),
        ("seq", "head"),
    )
    spread_in = jnp.sqrt(update_sums[0] / (D * PROJ))
    spread_out = jnp.sqrt(update_sums[1] / (INNER * D))
    w_in_new = w_in - LEARN_RATE * scaled_in / jnp.maximum(1.0, spread_in / CLIP_RMS)
    w_out_new = w_out - LEARN_RATE * scaled_out / jnp.maximum(1.0, spread_out / CLIP_RMS)
    small_second_new = decay * small_second + (1.0 - decay) * (small_grad * small_grad + EPS_SQUARE)
    scaled_small = small_grad * lax.rsqrt(small_second_new)
    spread_small = jnp.sqrt(jnp.mean(scaled_small * scaled_small))
    small_new = small_params - LEARN_SMALL * scaled_small / jnp.maximum(
        1.0, spread_small / CLIP_RMS
    )
    return (
        result,
        grad_x,
        grad_in,
        row_in_new,
        col_in_new,
        w_in_new,
        grad_out,
        row_out_new,
        col_out_new,
        w_out_new,
        small_grad,
        small_second_new,
        small_new,
    )


def solution(mesh):
    placed = (
        P(("seq", "head"), None),
        P("seq"),
        P(("seq", "head"), None),
        P("seq", "head"),
        P("head", "seq"),
        P(),
        P("seq"),
        P("head"),
        P("head"),
        P("seq"),
        P(),
    )
    return jax.shard_map(
        on_device,
        mesh=mesh,
        in_specs=placed,
        out_specs=(
            P(("seq", "head"), None),
            P(("seq", "head"), None),
            P("seq", "head"),
            P("seq"),
            P("head"),
            P("seq", "head"),
            P("head", "seq"),
            P("head"),
            P("seq"),
            P("head", "seq"),
            P(),
            P(),
            P(),
        ),
        check_vma=False,
    )
```

profile of v0, /device:TPU:0, one launch (start us, length us, event | category | flops | bytes accessed | tf_op | source)
XLA Modules:
  0.0 1462.9 jit_solution(8876727985200835231)
XLA Ops:
  9.0 29.1 %all-gather.5.cloned.1.call-done = bf16[768,806]{1,0:T(8,128)(2,1)} async-done(((bf16[96,806]{1,0:T(8,128)(2,1)}), bf16[768,806]{1,0:T(8,128)(2,1)}) %all-gather.5.cloned.1.call-update) | async-done | bytes 1238032 | tf_op jit(solution)/shard_map/all_gather | solution.py:147
  40.9 93.4 %all-gather.9.cloned.1.call-done = bf16[4,806,768]{2,1,0:T(8,128)(2,1)} async-done(((bf16[1,806,768]{2,1,0:T(8,128)(2,1)}), bf16[4,806,768]{2,1,0:T(8,128)(2,1)}) %all-gather.9.cloned.1.call-update) | async-done | bytes 4952080 | tf_op jit(solution)/shard_map/all_gather | solution.py:151
  170.0 11.1 all_gather.14
  264.2 62.7 %while.69 = (s32[]{:T(128)}, f32[6,64,64]{2,1,0:T(8,128)}, f32[12,6,64,64]{3,2,1,0:T(8,128)}, f32[12,6,1,1]{1,3,2,0:T(1,128)}, f32[12,6]{1,0:T(8,128)}, /*index=5*/f32[12,6,64,64]{3,2,1,0:T(8,128)}, s32[]{:T(128)}, s32[]{:T(128)}) while((s32[]{:T(128)}, f32[6,64,64]{2,1,0:T(8,128)}, f32[12,6,64,64]{3,2,1,0:T(8,128)}, ...), condition=%wide.region_3.4_spmd.clone, body=%wide.region_2.3_spmd.clone.sunk | while | flops 98307 | bytes 689344 | solution.py:96
  334.9 8.4 rev.30
  351.0 62.8 %while.70 = (s32[]{:T(128)}, f32[6,64,64]{2,1,0:T(8,128)}, f32[12,6,64,64]{3,2,1,0:T(8,128)}, f32[12,6,1,1]{1,3,2,0:T(1,128)}, f32[12,6]{1,0:T(8,128)}, /*index=5*/f32[12,6,64,64]{3,2,1,0:T(8,128)}, s32[]{:T(128)}, s32[]{:T(128)}) while((s32[]{:T(128)}, f32[6,64,64]{2,1,0:T(8,128)}, f32[12,6,64,64]{3,2,1,0:T(8,128)}, ...), condition=%wide.region_6.7_spmd.clone, body=%wide.region_5.6_spmd.clone.sunk | while | flops 98307 | bytes 689344 | solution.py:96
  418.0 9.5 fusion.42
  429.3 8.6 rev.34
  464.2 27.2 %all-to-all-done.2 = bf16[4,2,73728]{2,1,0:T(2,128)(2,1)} async-done(((bf16[4,2,73728]{2,1,0:T(2,128)(2,1)}), bf16[4,2,73728]{2,1,0:T(2,128)(2,1)}, u32[]{:S(2)}, u32[]{:S(2)}) %all-to-all-start.2) | async-done | bytes 1179680 | tf_op jit(solution)/shard_map/all_to_all | solution.py:208
  525.3 24.6 %all-to-all-done.3 = bf16[384,4,384]{0,2,1:T(8,128)(2,1)} async-done(((bf16[384,4,384]{0,2,1:T(8,128)(2,1)}), bf16[384,4,384]{0,2,1:T(8,128)(2,1)}, u32[]{:S(2)}, u32[]{:S(2)}) %all-to-all-start.3) | async-done | bytes 1179680 | tf_op jit(solution)/shard_map/all_to_all | solution.py:227
  570.1 71.0 %while.72 = (s32[]{:T(128)}, f32[6,64,64]{2,1,0:T(8,128)}, f32[12,6]{1,0:T(8,128)}, f32[12,6,64,64]{3,2,1,0:T(8,128)}, f32[12,6,64,64]{3,2,1,0:T(8,128)}, /*inde...) while((s32[]{:T(128)}, f32[6,64,64]{2,1,0:T(8,128)}, ...), condition=%wide.region_14.15_spmd.clone, body=%wide.region_12.14_spmd.clone.sunk | while | flops 147454 | bytes 786724 | solution.py:96
  659.0 8.5 rev.35
  682.0 71.3 %while.71 = (s32[]{:T(128)}, f32[6,64,64]{2,1,0:T(8,128)}, f32[12,6]{1,0:T(8,128)}, f32[12,6,64,64]{3,2,1,0:T(8,128)}, f32[12,6,64,64]{3,2,1,0:T(8,128)}, /*inde...) while((s32[]{:T(128)}, f32[6,64,64]{2,1,0:T(8,128)}, ...), condition=%wide.region_11.12_spmd.clone, body=%wide.region_9.11_spmd.clone.sunk | while | flops 147454 | bytes 786724 | solution.py:96
  780.3 11.6 fusion.37
  799.2 8.2 rev.36
  807.5 11.0 fusion.24
  905.2 22.1 %all-to-all-done.5 = f32[1536,1,134]{2,1,0:T(1,128)} async-done(((f32[1536,1,134]{2,1,0:T(1,128)}), f32[1536,1,134]{2,1,0:T(1,128)}, u32[]{:S(2)}, u32[]{:S(2)}) %all-to-all-start.5) | async-done | bytes 823328 | tf_op jit(solution)/shard_map/all_to_all | solution.py:240
  947.7 100.2 %all-to-all-done.4 = f32[1536,1,384]{2,1,0:T(1,128)} async-done(((f32[1536,1,384]{2,1,0:T(1,128)}), f32[1536,1,384]{2,1,0:T(1,128)}, u32[]{:S(2)}, u32[]{:S(2)}) %all-to-all-start.4) | async-done | bytes 2359328 | tf_op jit(solution)/shard_map/all_to_all | solution.py:237
  1085.0 8.3 fusion.121
  1093.3 164.3 %fusion = f32[768,808]{0,1:T(8,128)S(1)} fusion(f32[768,3224]{0,1:T(8,128)} %fusion.121), kind=kCustom, calls=%all-reduce-scatter | all-reduce-scatter fusion | flops 2482177 | bytes 12386816
  1294.8 20.9 %reduce-scatter.12.cloned.1.call-done = f32[96,806]{1,0:T(8,128)} async-done(((f32[768,806]{1,0:T(8,128)}), f32[96,806]{1,0:T(8,128)}) %reduce-scatter.12.cloned.1.call-update) | async-done | bytes 309520
  1317.6 38.9 %reduce-scatter.14.cloned.1.call-done = f32[96,384]{1,0:T(8,128)} async-done(((f32[768,384]{1,0:T(8,128)}), f32[96,384]{1,0:T(8,128)}) %reduce-scatter.14.cloned.1.call-update) | async-done | bytes 147472
  1358.2 39.9 %all-reduce.15 = (f32[768]{0:T(1024)S(1)}, f32[3224]{0:T(1024)S(1)}, f32[2]{0:T(128)S(1)}, f32[1536]{0:T(1024)S(1)}, f32[768]{0:T(1024)S(1)}) all-reduce(f32[768]{0:T(1024)S(1)} %dynamic_update_slice.72, f32[3224]{0:T(1024)S(1)} %dynamic_update_slice.73, ...), channel_id=1, replica_groups=mesh['seq'=8,'head'=4] {'seq','head'}, use_global_device_ids=true, to_apply=%region_34.35 | all-reduce | flops 6298 | bytes 50384 | tf_op jit(solution)/shard_map/psum | solution.py:296
  1408.4 41.4 %all-reduce.14 = (f32[2]{0:T(128)S(1)}, f32[10696]{0:T(1024)S(1)}) all-reduce(f32[2]{0:T(128)S(1)} %pad_maximum_fusion.6, f32[10696]{0:T(1024)S(1)} %concatenate.26), channel_id=1, replica_groups=mesh['seq'=8,'head'=4] {'seq','head'}, use_global_device_ids=true, to_apply=%region_50.51 | all-reduce | flops 10698 | bytes 85584 | tf_op jit(solution)/shard_map/psum | solution.py:321
  (697 shorter events, 751.9 us)
Async XLA Ops:
  7.2 30.9 %all-gather.5.cloned.1.call-start = ((), (), s32[]{:S(2)}) async-start(), calls=%async_computation.9 | async-start | bytes 1548288 | tf_op jit(solution)/shard_map/all_gather | solution.py:147
  9.0 125.3 %all-gather.9.cloned.1.call-start = ((), (), s32[]{:S(2)}) async-start(), calls=%async_computation.12 | async-start | bytes 6205440 | tf_op jit(solution)/shard_map/all_gather | solution.py:151
  40.7 99.6 %copy-start.65 = (f32[768]{0:T(1024)}, f32[768]{0:T(1024)S(1)}, u32[]{:S(2)}) copy-start(f32[768]{0:T(1024)S(1)} %slice.138) | copy-start | bytes 9220
  40.9 99.4 %copy-start.98 = (f32[384]{0:T(512)}, f32[384]{0:T(512)S(1)}, u32[]{:S(2)}) copy-start(f32[384]{0:T(512)S(1)} %fusion.108) | copy-start | bytes 4612
  40.9 99.4 %copy-start.74 = (f32[384]{0:T(512)}, f32[384]{0:T(512)S(1)}, u32[]{:S(2)}) copy-start(f32[384]{0:T(512)S(1)} %fusion.177) | copy-start | bytes 4612
  145.8 10.8 collective-permute-start
  165.1 20.6 %all-to-all-start.1 = ((bf16[384,4,134]{0,2,1:T(8,128)(2,1)}), bf16[384,4,134]{0,2,1:T(8,128)(2,1)}, u32[]{:S(2)}, u32[]{:S(2)}) async-start(bf16[384,4,134]{0,2,1:T(8,128)(2,1)} %pad_maximum_fusion.4), calls=%async_computation.1 | async-start | bytes 835584 | tf_op jit(solution)/shard_map/all_to_all | solution.py:184
  170.0 337.6 %all-gather.7.cloned.1.call-start = ((), (), s32[]{:S(2)}) async-start(), calls=%async_computation.10 | async-start | bytes 2949120 | tf_op jit(solution)/shard_map/all_gather | solution.py:152
  185.7 65.2 %all-to-all-start = ((bf16[384,4,384]{0,2,1:T(8,128)(2,1)}), bf16[384,4,384]{0,2,1:T(8,128)(2,1)}, u32[]{:S(2)}, u32[]{:S(2)}) async-start(bf16[384,4,384]{0,2,1:T(8,128)(2,1)} %bitcast.431), calls=%async_computation | async-start | bytes 2359296 | tf_op jit(solution)/shard_map/all_to_all | solution.py:183
  458.0 33.5 %all-to-all-start.2 = ((bf16[4,2,73728]{2,1,0:T(2,128)(2,1)}), bf16[4,2,73728]{2,1,0:T(2,128)(2,1)}, u32[]{:S(2)}, u32[]{:S(2)}) async-start(bf16[4,2,73728]{2,1,0:T(2,128)(2,1)} %reshape.437), calls=%async_computation.2 | async-start | bytes 2359296 | tf_op jit(solution)/shard_map/all_to_all | solution.py:208
  517.1 32.8 %all-to-all-start.3 = ((bf16[384,4,384]{0,2,1:T(8,128)(2,1)}), bf16[384,4,384]{0,2,1:T(8,128)(2,1)}, u32[]{:S(2)}, u32[]{:S(2)}) async-start(bf16[384,4,384]{0,2,1:T(8,128)(2,1)} %bitcast.433), calls=%async_computation.3 | async-start | bytes 2359296 | tf_op jit(solution)/shard_map/all_to_all | solution.py:227
  886.4 40.9 %all-to-all-start.5 = ((f32[1536,1,134]{2,1,0:T(1,128)}), f32[1536,1,134]{2,1,0:T(1,128)}, u32[]{:S(2)}, u32[]{:S(2)}) async-start(f32[1536,1,134]{2,1,0:T(1,128)} %copy.541), calls=%async_computation.5 | async-start | bytes 3145728 | tf_op jit(solution)/shard_map/all_to_all | solution.py:240
  927.2 120.7 %all-to-all-start.4 = ((f32[1536,1,384]{2,1,0:T(1,128)}), f32[1536,1,384]{2,1,0:T(1,128)}, u32[]{:S(2)}, u32[]{:S(2)}) async-start(f32[1536,1,384]{2,1,0:T(1,128)} %copy.509), calls=%async_computation.4 | async-start | bytes 4718592 | tf_op jit(solution)/shard_map/all_to_all | solution.py:237
  931.8 350.8 %reduce-scatter.10.cloned.1.call-start = ((), (), s32[]{:S(2)}) async-start(), calls=%async_computation.11 | async-start | bytes 5898240 | tf_op jit(solution)/shard_map/reduce_scatter | solution.py:271
  937.7 378.0 %reduce-scatter.12.cloned.1.call-start = ((), (), s32[]{:S(2)}) async-start(), calls=%async_computation.13 | async-start | bytes 3096576
  1065.5 9.1 collective-permute-start.1
  1093.3 166.1 %copy-start.119 = (u32[32]{0:T(128)S(1)}, u32[32]{0:T(128)}, u32[]{:S(2)}) copy-start(u32[32]{0:T(128)} %constant.320) | copy-start | bytes 388
  1257.5 3.3 collective-permute-start.2
  1272.3 84.2 %reduce-scatter.14.cloned.1.call-start = ((), (), s32[]{:S(2)}) async-start(), calls=%async_computation.14 | async-start | bytes 1327104
  1288.9 112.4 %copy-start.111 = (f32[806]{0:T(1024)S(1)}, f32[806]{0:T(1024)}, u32[]{:S(2)}) copy-start(f32[806]{0:T(1024)} %param.28) | copy-start | bytes 9676
  1288.9 112.5 %copy-start.121 = (f32[96]{0:T(128)S(1)}, f32[96]{0:T(128)}, u32[]{:S(2)}) copy-start(f32[96]{0:T(128)} %param.30) | copy-start | bytes 1156
  1294.7 111.0 %copy-start.33 = (bf16[384,768]{1,0:T(8,128)(2,1)S(1)}, bf16[384,768]{1,0:T(8,128)(2,1)}, u32[]{:S(2)}) copy-start(bf16[384,768]{1,0:T(8,128)(2,1)} %param.23) | copy-start | bytes 1769476
  1357.5 94.2 %copy-start.36 = (f32[96,806]{0,1:T(8,128)S(1)}, f32[96,806]{0,1:T(8,128)}, u32[]{:S(2)}) copy-start(f32[96,806]{0,1:T(8,128)} %copy.546) | copy-start | bytes 928516
  1398.1 54.7 %copy-start.97 = (f32[384]{0:T(512)}, f32[384]{0:T(512)S(1)}, u32[]{:S(2)}) copy-start(f32[384]{0:T(512)S(1)} %multiply_add_fusion.3) | copy-start | bytes 4612
  (113 other events, 1052.9 us)
Sparse Core Ops, SparseCore 0:
  10.5 27.5 all-gather.4
  40.8 93.4 all-gather.8
  181.2 75.8 all-gather.6
  937.8 117.9 reduce-scatter.9
  1272.4 43.2 reduce-scatter.11
  1319.7 36.7 reduce-scatter.13
where the time goes:
time: 1480 us; the launch traced here: 1460 us
  waiting for transfers between devices  365 us (25%)
  local copies, waits for them, and re-layouts  352 us (24%)
  other arithmetic  284 us (19%)
  blocking collectives  257 us (17%)
  matrix products  148 us (10%)
  starting transfers between devices  33.8 us (2%)
  between operations  23.3 us (2%)
    unnamed x1, blocking collectives  164 us
    all_to_all x1, waiting for transfers between devices, on_device(): lax.all_to_all(x_grad.reshape(seq_rows, 1, head_width), 'head', split_axi...  100 us
    all_gather x1, waiting for transfers between devices, on_device(): lax.all_gather(in_part, 'head', axis=1, tiled=True)  93.4 us
    dynamic_update_slice x48, other arithmetic, direction_scan(): _, entering = lax.scan(advance, state_init, (block_decay, block_states))  74 us
    dynamic_update_slice x48, local copies, waits for them, and re-layouts, direction_scan(): _, entering = lax.scan(advance, state_init, (block_decay, block_states))  60.4 us
    unnamed x9, waiting for transfers between devices  60.1 us
    reduce_sum x24, other arithmetic, advance(): return (carried_state * decay_part[:, None, None] + fresh, carried_state)  58.5 us
    unnamed x267, local copies, waits for them, and re-layouts  54.8 us
  transfers between devices with their start and end apart: 15, of which 11 were waited for; matrix products, arithmetic and copies ran while one was open for 38% of the time, Pallas kernels for 0%

commit v1 on v0

v1 whole, which is shorter than its diff:
```python
import functools

import jax
import jax.numpy as jnp
import numpy as np
from jax import lax
from jax.experimental import pallas as pl
from jax.experimental.pallas import tpu as pltpu
from jax.sharding import PartitionSpec as P

D = 768
HEADS = 24
HEAD_DIM = 64
STATE = 64
CONV = 4
SPAN = 128
STEP = 8
INNER = 1536
CONV_CH = 1664
PROJ = 3224
WIDE = 3328
LANES = 128
HALO = 16

EPS = 1e-05
EPS_SQUARE = 1e-30
LEARN_RATE = 0.3
LEARN_SMALL = 3.0
CLIP_RMS = 0.1
DECAY = 1.0 - STEP ** (-0.8)
F32 = jnp.float32
BF16 = jnp.bfloat16
HIGHEST = lax.Precision.HIGHEST
MESH = pl.DeviceIdType.MESH
VMEM_BYTES = 60 << 20


def nn(left, right):
    return lax.dot_general(left, right, (((1,), (0,)), ((), ())), preferred_element_type=F32)


def nt(left, right):
    return lax.dot_general(left, right, (((1,), (1,)), ((), ())), preferred_element_type=F32)


def split(value):
    high = value.astype(BF16)
    return high, (value - high.astype(F32)).astype(BF16)


def nn_split(value, exact):
    high, low = split(value)
    return nn(high, exact) + nn(low, exact)


def expand(value, spread):
    return nn_split(value, spread)


def fold(value, spread):
    high, low = split(value)
    return nt(high, spread) + nt(low, spread)


def iota(shape, dim):
    return lax.broadcasted_iota(jnp.int32, shape, dim)


def tri_low():
    return (iota((SPAN, SPAN), 0) >= iota((SPAN, SPAN), 1)).astype(F32)


def tri_high():
    return (iota((SPAN, SPAN), 0) <= iota((SPAN, SPAN), 1)).astype(F32)


def precise(left, right):
    return lax.dot_general(
        left, right, (((1,), (0,)), ((), ())), precision=HIGHEST, preferred_element_type=F32
    )


def sigmoid(value):
    return 1.0 / (1.0 + jnp.exp(-value))


def tiles_of(per_part, index):
    return (per_part * index) // LANES, -(-(per_part * (index + 1)) // LANES)


def tile_count(per_part, parts):
    return max(e - s for s, e in (tiles_of(per_part, i) for i in range(parts)))


def gather_kernel(n_s, n_h, pay, full, lsem, zs, zr, ps, pr, cs, cr):
    s = lax.axis_index("seq")
    h = lax.axis_index("head")
    n_c = n_s // 2
    chip = s // 2
    core = lax.rem(s, 2)
    sib = chip * 2 + (1 - core)
    zpeer = [lax.rem(h + j, n_h) for j in range(1, n_h)]
    cpeer = [lax.rem(chip + j, n_c) for j in range(1, n_c)]
    bar = pltpu.get_barrier_semaphore()
    for z in zpeer:
        pl.semaphore_signal(bar, inc=1, device_id=(s, z), device_id_type=MESH)
    for c in cpeer:
        pl.semaphore_signal(bar, inc=1, device_id=(c * 2 + core, h), device_id_type=MESH)
    pl.semaphore_signal(bar, inc=1, device_id=(sib, h), device_id_type=MESH)
    pl.semaphore_wait(bar, n_h + n_c - 1)

    def rc(src, dst, ss, rs, dev):
        return pltpu.make_async_remote_copy(
            src_ref=src, dst_ref=dst, send_sem=ss, recv_sem=rs, device_id=dev, device_id_type=MESH
        )

    local = pltpu.make_async_copy(pay, full.at[h, s], lsem)
    local.start()
    sends = []

    def go(c):
        c.start()
        sends.append(c)

    for j, z in enumerate(zpeer):
        go(rc(pay, full.at[h, s], zs.at[j], zr.at[h], (s, z)))

    def plane(src, k, slot):
        for j, c in enumerate(cpeer):
            go(rc(src, full.at[k, s], ps.at[slot, j], pr.at[chip, k], (c * 2 + core, h)))
        go(rc(src, full.at[k, s], cs.at[slot, 0], cr.at[chip, k], (sib, h)))

    plane(pay, h, 0)
    order = [h] + zpeer

    def relay(kk, i):
        for j, c in enumerate(cpeer):
            o = c * 2 + core
            rc(pay, full.at[kk, o], zs.at[0], pr.at[c, kk], (s, zpeer[0])).wait_recv()
            go(rc(full.at[kk, o], full.at[kk, o], cs.at[i, j + 1], cr.at[c, kk], (sib, h)))

    for i, k in enumerate(zpeer):
        rc(pay, full.at[k, s], zs.at[i], zr.at[k], (s, k)).wait_recv()
        plane(full.at[k, s], k, i + 1)
        relay(order[i], i)
    relay(order[-1], n_h - 1)
    for kk in order:
        for c in [chip] + cpeer:
            rc(pay, full.at[kk, c * 2 + 1 - core], zs.at[0], cr.at[c, kk], (sib, h)).wait_recv()
    for c in sends:
        c.wait_send()
    local.wait()


def gather(pay, n_s, n_h):
    n_c = n_s // 2
    dma = pltpu.SemaphoreType.DMA
    return pl.pallas_call(
        functools.partial(gather_kernel, n_s, n_h),
        out_shape=jax.ShapeDtypeStruct((n_h, n_s) + pay.shape, pay.dtype),
        in_specs=[pl.BlockSpec(memory_space=pl.ANY)],
        out_specs=pl.BlockSpec(memory_space=pl.ANY),
        scratch_shapes=[
            dma,
            dma((n_h - 1,)),
            dma((n_h,)),
            dma((n_h, n_c - 1)),
            dma((n_c, n_h)),
            dma((n_h, n_c)),
            dma((n_c, n_h)),
        ],
        compiler_params=pltpu.CompilerParams(collective_id=0, has_side_effects=True),
        name="gather_weights",
    )(pay)


def chain_kernel(n_h, dev, dec, out, snd, us, ur, ds, dr):
    s = lax.axis_index("seq")
    h = lax.axis_index("head")
    up = lax.rem(h + 1, n_h)
    down = lax.rem(h + n_h - 1, n_h)
    bar = pltpu.get_barrier_semaphore()
    for z in (up, down):
        pl.semaphore_signal(bar, inc=1, device_id=(s, z), device_id_type=MESH)
    pl.semaphore_wait(bar, 2)
    parts = 4
    width = INNER // parts

    def rc(d, c, sem_s, sem_r, dev_h):
        cols = pl.ds(c * width, width)
        return pltpu.make_async_remote_copy(
            src_ref=snd.at[d, :, cols],
            dst_ref=out.at[d, :, cols],
            send_sem=sem_s.at[c],
            recv_sem=sem_r.at[c],
            device_id=(s, dev_h),
            device_id_type=MESH,
        )

    first = h == 0
    last = h == n_h - 1

    @pl.when(first)
    def _():
        out[0] = jnp.zeros((STATE, INNER), F32)
        snd[0] = dev[0]
        for c in range(parts):
            rc(0, c, us, ur, up).start()

    @pl.when(last)
    def _():
        out[1] = jnp.zeros((STATE, INNER), F32)
        snd[1] = dev[1]
        for c in range(parts):
            rc(1, c, ds, dr, down).start()

    for c in range(parts):
        cols = slice(c * width, (c + 1) * width)

        @pl.when(h > 0)
        def _():
            rc(0, c, us, ur, down).wait_recv()

        @pl.when(jnp.logical_and(h > 0, h < n_h - 1))
        def _():
            snd[0, :, cols] = out[0, :, cols] * dec[0:1, cols] + dev[0, :, cols]
            rc(0, c, us, ur, up).start()

        @pl.when(h < n_h - 1)
        def _():
            rc(1, c, ds, dr, up).wait_recv()

        @pl.when(jnp.logical_and(h > 0, h < n_h - 1))
        def _():
            snd[1, :, cols] = out[1, :, cols] * dec[0:1, cols] + dev[1, :, cols]
            rc(1, c, ds, dr, down).start()

    @pl.when(h < n_h - 1)
    def _():
        for c in range(parts):
            rc(0, c, us, ur, up).wait_send()

    @pl.when(h > 0)
    def _():
        for c in range(parts):
            rc(1, c, ds, dr, down).wait_send()


def chain(dev, dec, n_h, cid):
    dma = pltpu.SemaphoreType.DMA
    vm = pl.BlockSpec(memory_space=pltpu.VMEM)
    return pl.pallas_call(
        functools.partial(chain_kernel, n_h),
        out_shape=jax.ShapeDtypeStruct((2, STATE, INNER), F32),
        in_specs=[vm, vm],
        out_specs=vm,
        scratch_shapes=[pltpu.VMEM((2, STATE, INNER), F32), dma((4,)), dma((4,)), dma((4,)), dma((4,))],
        compiler_params=pltpu.CompilerParams(
            collective_id=cid, has_side_effects=True, vmem_limit_bytes=VMEM_BYTES
        ),
        name="state_chain",
    )(dev, dec)


def head_terms(steps, rates):
    logs = steps * rates
    incl = precise(tri_low(), logs)
    return incl, incl - logs, incl[SPAN - 1 : SPAN]


def front_kernel(
    n_h, cph, oph, wi,
    x, full, gain, taps, heads, left, spread,
    nlow, w_in, w_out, gate, conv_in, conv_low, slope, raw, steps, hst, gst, dev, decb, dec,
    nscr, cf,
):
    rows = nlow.shape[0]
    blocks = rows // SPAN

    def norm_body(i, _):
        at = pl.ds(pl.multiple_of(i * 16, 16), 16)
        v = x[at, :].astype(F32)
        n = v * lax.rsqrt(jnp.mean(v * v, axis=1, keepdims=True) + EPS) * gain[...]
        nscr[at, :] = n.astype(BF16)
        return 0

    lax.fori_loop(0, (rows + HALO) // 16, norm_body, 0)
    nlow[...] = nscr[HALO:, :]
    for per, width, base, dst in ((cph, WIDE, 0, w_in), (oph, INNER, wi, w_out)):
        for tile in range(width // LANES):
            parts = []
            for i in range(n_h):
                t0, t1 = tiles_of(per, i)
                if t0 <= tile < t1:
                    at = base + (tile - t0) * LANES
                    parts.append(full[i, :, at : at + LANES])
            v = parts[0] if len(parts) == 1 else parts[0] + parts[1]
            dst[:, tile * LANES : (tile + 1) * LANES] = v

    def gate_body(j, _):
        at = pl.ds(pl.multiple_of(j * 256, 256), 256)
        gate[:, at] = nn(nscr[HALO:, :], w_in[:, at]).astype(BF16)
        return 0

    lax.fori_loop(0, INNER // 256, gate_body, 0)

    def conv_body(j, _):
        at = pl.ds(pl.multiple_of(j * 256, 256), 256)
        v = nn(nscr[...], w_in[:, pl.ds(pl.multiple_of(INNER + j * 256, 256), 256)]).astype(BF16)
        conv_in[:, at] = v
        cf[:, at] = v.astype(F32)
        return 0

    lax.fori_loop(0, INNER // 256, conv_body, 0)
    v = nn(nscr[...], w_in[:, 2 * INNER : WIDE]).astype(BF16)
    conv_in[:, INNER:] = v[:, :LANES]
    cf[:, INNER:] = v[:, :LANES].astype(F32)
    raw[...] = v[HALO:, LANES:].astype(F32)

    def taps_body(j, _):
        at = pl.ds(pl.multiple_of(j * LANES, LANES), LANES)
        total = jnp.zeros((rows, LANES), F32) + taps[CONV : CONV + 1, at]
        for k in range(CONV):
            total = total + taps[k : k + 1, at] * cf[HALO - CONV + 1 + k : HALO - CONV + 1 + k + rows, at]
        sg = sigmoid(total)
        conv_low[:, at] = (total * sg).astype(BF16)
        slope[:, at] = sg * (1.0 + total * (1.0 - sg))
        return 0

    lax.fori_loop(0, CONV_CH // LANES, taps_body, 0)
    biased = raw[...] + heads[0:1, :]
    soft = jnp.maximum(biased, 0.0) + jnp.log1p(jnp.exp(-jnp.abs(biased)))
    keep = jnp.logical_and(iota((rows, LANES), 0) < left[0], iota((rows, LANES), 1) < HEADS)
    steps[...] = jnp.where(keep, soft, 0.0)
    rates = -jnp.exp(heads[1:2, :])
    for b in range(blocks):
        at = slice(b * SPAN, (b + 1) * SPAN)
        st = steps[at, :]
        incl, excl, total = head_terms(st, rates)
        wf = split(jnp.exp(total - incl) * st)
        wg = split(jnp.exp(excl) * st)
        bt = conv_low[at, INNER:].astype(F32).T[:STATE].astype(BF16)
        bt2 = jnp.concatenate([bt, bt], axis=1)
        tot = jnp.broadcast_to(jnp.exp(total), (8, LANES))
        for g in range(INNER // 256):
            cols = slice(g * 256, (g + 1) * 256)
            sp = spread[:, cols]
            xs = conv_low[at, cols].astype(F32)
            for w, dst in ((wf, hst), (wg, gst)):
                hi, lo = split((nn(w[0], sp) + nn(w[1], sp)) * xs)
                dst[b, :, cols] = nn(bt2, jnp.concatenate([hi, lo], axis=0))
            decb[b, :, cols] = expand(tot, sp)
    hv, gv, dv = hst[0], gst[blocks - 1], decb[0]
    for b in range(1, blocks):
        hv = hv * decb[b, 0:1, :] + hst[b]
        dv = dv * decb[b]
    for b in range(blocks - 2, -1, -1):
        gv = gv * decb[b, 0:1, :] + gst[b]
    dev[0] = hv
    dev[1] = gv
    dec[...] = dv


def front(x, full, gain, taps, heads, left, spread, n_h, cph, oph, wi):
    rows = x.shape[0] - HALO
    blocks = rows // SPAN
    vm = pl.BlockSpec(memory_space=pltpu.VMEM)
    sm = pl.BlockSpec(memory_space=pltpu.SMEM)
    sds = jax.ShapeDtypeStruct
    return pl.pallas_call(
        functools.partial(front_kernel, n_h, cph, oph, wi),
        out_shape=(
            sds((rows, D), BF16),
            sds((D, WIDE), BF16),
            sds((D, INNER), BF16),
            sds((rows, INNER), BF16),
            sds((rows + HALO, CONV_CH), BF16),
            sds((rows, CONV_CH), BF16),
            sds((rows, CONV_CH), F32),
            sds((rows, LANES), F32),
            sds((rows, LANES), F32),
            sds((blocks, STATE, INNER), F32),
            sds((blocks, STATE, INNER), F32),
            sds((2, STATE, INNER), F32),
            sds((blocks, 8, INNER), F32),
            sds((8, INNER), F32),
        ),
        in_specs=[vm, vm, vm, vm, vm, sm, vm],
        out_specs=(vm,) * 14,
        scratch_shapes=[pltpu.VMEM((rows + HALO, D), BF16), pltpu.VMEM((rows + HALO, CONV_CH), F32)],
        compiler_params=pltpu.CompilerParams(vmem_limit_bytes=VMEM_BYTES),
        name="front",
    )(x, full, gain, taps, heads, left, spread)


def half_masks(value):
    low = iota(value.shape, 1) < HEAD_DIM
    zero = jnp.zeros_like(value)
    return jnp.where(low, value, zero), jnp.where(low, zero, value)


def block_entries(blocks, dst, entering, local, decb, reverse):
    order = range(blocks - 1, -1, -1) if reverse else range(blocks)
    v = entering
    for b in order:
        dst[b] = v
        v = v * decb[b, 0:1, :] + local[b]


def middle_kernel(
    x, cot, gate, conv_low, steps, hst, gst, into, decb, w_out, heads, out_gain, left, spread,
    result, dgate, hgrad, gout, dgain, lst, mst, dev,
    hin, gin, el, eg, ho, gg_scr, glow,
):
    rows = x.shape[0]
    blocks = rows // SPAN
    rates = -jnp.exp(heads[1:2, :])
    block_entries(blocks, hin, into[0], hst, decb, False)
    block_entries(blocks, gin, into[1], gst, decb, True)
    row = iota((SPAN, SPAN), 0)
    col = iota((SPAN, SPAN), 1)
    after = row >= col
    twice = 1.0 + (row == col).astype(F32)
    skip8 = jnp.broadcast_to(heads[2:3, :], (8, LANES))

    def block_body(b, _):
        at = pl.ds(pl.multiple_of(b * SPAN, SPAN), SPAN)
        st = steps[at, :]
        incl, excl, total = head_terms(st, rates)
        incl_t, excl_t, st_t = incl.T, excl.T, st.T
        bc = conv_low[at, INNER:].astype(F32)
        cb = pltpu.roll(bc, STATE, 1)
        c_low = half_masks(cb)[0].astype(BF16)
        inter = nt(c_low, bc.astype(BF16)) * twice
        cc = cb[:, :STATE].astype(BF16)
        for dst, val in ((el, jnp.exp(incl)), (eg, jnp.exp(total - excl))):
            hi, lo = split(val)
            for g in range(INNER // 256):
                cols = slice(g * 256, (g + 1) * 256)
                dst[at, cols] = nn(hi, spread[:, cols]) + nn(lo, spread[:, cols])
        for pair in range(HEADS // 2):
            cols = slice(pair * LANES, (pair + 1) * LANES)
            xs = conv_low[at, cols]
            mix = []
            for h in (2 * pair, 2 * pair + 1):
                gap = jnp.where(
                    after,
                    incl[:, h : h + 1] - incl_t[h : h + 1, :],
                    excl_t[h : h + 1, :] - excl[:, h : h + 1],
                )
                mix.append(inter * jnp.exp(gap) * st_t[h : h + 1, :])
            x0, x1 = half_masks(xs)
            y = nn_split(jnp.concatenate(mix, axis=1), jnp.concatenate([x0, x1], axis=0))
            hh, hl = split(hin[b, :, cols])
            gh, gl = split(gin[b, :, cols])
            y = y + el[at, cols] * (nn(cc, hh) + nn(cc, hl))
            y = y + eg[at, cols] * (nn(cc, gh) + nn(cc, gl))
            y = y + expand(skip8, spread[:, cols])[0:1] * xs.astype(F32)
            ho[at, cols] = y.astype(BF16)
        return 0

    lax.fori_loop(0, blocks, block_body, 0)
    keep = (iota((rows, 1), 0) < left[0]).astype(F32)
    bgrad = (cot[...].astype(F32) * keep).astype(BF16)
    for g in range(INNER // 256):
        cols = slice(g * 256, (g + 1) * 256)
        gg_scr[:, cols] = nn(bgrad, w_out[:, cols])
    dgain[...] = jnp.zeros_like(dgain)

    def gate_body(i, _):
        at = pl.ds(pl.multiple_of(i * 16, 16), 16)
        z = gate[at, :].astype(F32)
        hv = ho[at, :].astype(F32)
        sg = sigmoid(z)
        sl = z * sg
        gated = hv * sl
        r = lax.rsqrt(jnp.mean(gated * gated, axis=1, keepdims=True) + EPS)
        unit = gated * r
        glow[at, :] = (unit * out_gain[...]).astype(BF16)
        gr = gg_scr[at, :]
        prod = gr * unit
        dgain[...] += prod[0:8] + prod[8:16]
        gg = gr * out_gain[...]
        dg = r * (gg - unit * jnp.mean(gg * unit, axis=1, keepdims=True))
        hgrad[at, :] = (dg * sl).astype(BF16)
        dgate[at, :] = (dg * hv * (sg * (1.0 + z * (1.0 - sg)))).astype(BF16)
        return 0

    lax.fori_loop(0, rows // 16, gate_body, 0)
    for g in range(D // 256):
        cols = slice(g * 256, (g + 1) * 256)
        branch = nt(glow[...], w_out[cols, :])
        result[:, cols] = (x[:, cols].astype(F32) + keep * branch).astype(BF16)
    bgt = bgrad.T
    for g in range(INNER // 256):
        cols = slice(g * 256, (g + 1) * 256)
        gout[:, cols] = nn(bgt, glow[:, cols])

    def state_body(b, _):
        at = pl.ds(pl.multiple_of(b * SPAN, SPAN), SPAN)
        ct = conv_low[at, INNER:].astype(F32).T[STATE:].astype(BF16)
        ct2 = jnp.concatenate([ct, ct], axis=1)
        for g in range(INNER // 256):
            cols = slice(g * 256, (g + 1) * 256)
            dy = hgrad[at, cols].astype(F32)
            for scale, dst in ((el, lst), (eg, mst)):
                hi, lo = split(scale[at, cols] * dy)
                dst[b, :, cols] = nn(ct2, jnp.concatenate([hi, lo], axis=0))
        return 0

    lax.fori_loop(0, blocks, state_body, 0)
    mv, lv = mst[0], lst[blocks - 1]
    for b in range(1, blocks):
        mv = mv * decb[b, 0:1, :] + mst[b]
    for b in range(blocks - 2, -1, -1):
        lv = lv * decb[b, 0:1, :] + lst[b]
    dev[0] = mv
    dev[1] = lv


def middle(x, cot, gate, conv_low, steps, hst, gst, into, decb, w_out, heads, out_gain, left, spread):
    rows = x.shape[0]
    blocks = rows // SPAN
    vm = pl.BlockSpec(memory_space=pltpu.VMEM)
    sm = pl.BlockSpec(memory_space=pltpu.SMEM)
    sds = jax.ShapeDtypeStruct
    big = pltpu.VMEM((rows, INNER), F32)
    low = pltpu.VMEM((rows, INNER), BF16)
    st = pltpu.VMEM((blocks, STATE, INNER), F32)
    return pl.pallas_call(
        middle_kernel,
        out_shape=(
            sds((rows, D), BF16),
            sds((rows, INNER), BF16),
            sds((rows, INNER), BF16),
            sds((D, INNER), F32),
            sds((8, INNER), F32),
            sds((blocks, STATE, INNER), F32),
            sds((blocks, STATE, INNER), F32),
            sds((2, STATE, INNER), F32),
        ),
        in_specs=[vm] * 12 + [sm, vm],
        out_specs=(vm,) * 8,
        scratch_shapes=[st, st, big, big, low, big, low],
        compiler_params=pltpu.CompilerParams(vmem_limit_bytes=VMEM_BYTES),
        name="middle",
    )(x, cot, gate, conv_low, steps, hst, gst, into, decb, w_out, heads, out_gain, left, spread)


def back_kernel(
    conv_low, hgrad, steps, raw, slope, conv_in, hst, gst, lst, mst, into, adj, decb, heads, left, spread,
    dpre, draw, dheads, dtaps,
    hin, gin, lend, mstart, at_f, at_g, cf,
):
    rows = hgrad.shape[0]
    blocks = rows // SPAN
    rates = -jnp.exp(heads[1:2, :])
    block_entries(blocks, hin, into[0], hst, decb, False)
    block_entries(blocks, gin, into[1], gst, decb, True)
    block_entries(blocks, mstart, adj[0], mst, decb, False)
    block_entries(blocks, lend, adj[1], lst, decb, True)
    row = iota((SPAN, SPAN), 0)
    col = iota((SPAN, SPAN), 1)
    later = col >= row
    twice = 1.0 + (row == col).astype(F32)
    skip8 = jnp.broadcast_to(heads[2:3, :], (8, LANES))
    dheads[...] = jnp.zeros_like(dheads)
    at_f[...] = jnp.zeros_like(at_f)
    at_g[...] = jnp.zeros_like(at_g)

    def block_body(b, _):
        at = pl.ds(pl.multiple_of(b * SPAN, SPAN), SPAN)
        st = steps[at, :]
        incl, excl, total = head_terms(st, rates)
        incl_t, excl_t = incl.T, excl.T
        bc = conv_low[at, INNER:].astype(F32)
        cb = pltpu.roll(bc, STATE, 1)
        b_low = half_masks(bc)[0].astype(BF16)
        inter = nt(b_low, cb.astype(BF16))
        inter2 = inter * twice
        bb = bc[:, :STATE].astype(BF16)
        cc = cb[:, :STATE].astype(BF16)
        scales = [split(v) for v in (st, jnp.exp(incl), jnp.exp(total - excl), jnp.exp(total - incl), jnp.exp(excl))]
        q_t = jnp.zeros((SPAN, SPAN), F32)
        back_f = jnp.zeros((SPAN, LANES), F32)
        back_g = jnp.zeros((SPAN, LANES), F32)
        red_f = jnp.zeros((SPAN, LANES), F32)
        red_g = jnp.zeros((SPAN, LANES), F32)
        red_s = jnp.zeros((SPAN, LANES), F32)
        red_k = jnp.zeros((SPAN, LANES), F32)
        cross_f = jnp.zeros((8, LANES), F32)
        cross_g = jnp.zeros((8, LANES), F32)
        dbc = jnp.zeros((SPAN, LANES), F32)
        zero_state = jnp.zeros((STATE, LANES), BF16)
        for pair in range(HEADS // 2):
            cols = slice(pair * LANES, (pair + 1) * LANES)
            sp = spread[:, cols]
            st_e, el, eg, tl, ex = [nn(hi, sp) + nn(lo, sp) for hi, lo in scales]
            xs = conv_low[at, cols].astype(F32)
            dyl = hgrad[at, cols]
            dy = dyl.astype(F32)
            xst = st_e * xs
            xh, xl = split(xst)
            xh0, xh1 = half_masks(xh)
            xl0, xl1 = half_masks(xl)
            dy2 = jnp.concatenate([dyl, dyl], axis=1)
            kern = []
            for h, xa, xb in ((2 * pair, xh0, xl0), (2 * pair + 1, xh1, xl1)):
                gap = jnp.where(
                    later,
                    incl_t[h : h + 1, :] - incl[:, h : h + 1],
                    excl[:, h : h + 1] - excl_t[h : h + 1, :],
                )
                decay = jnp.exp(gap)
                kern.append(inter2 * decay)
                weigh = nt(jnp.concatenate([xa, xb], axis=1), dy2) * decay
                q_t = q_t + weigh * twice
                pairs = weigh * inter
                up = jnp.where(col > row, pairs, 0.0)
                down = jnp.where(col < row, pairs, 0.0)
                at_f[h : h + 1, :] = jnp.sum(up, axis=0, keepdims=True)
                at_g[h : h + 1, :] = jnp.sum(down, axis=0, keepdims=True)
                here = iota((SPAN, LANES), 1) == h
                back_f = jnp.where(here, jnp.sum(up, axis=1, keepdims=True), back_f)
                back_g = jnp.where(here, jnp.sum(down, axis=1, keepdims=True), back_g)
            dy0, dy1 = half_masks(dyl)
            dxu = nn_split(jnp.concatenate(kern, axis=1), jnp.concatenate([dy0, dy1], axis=0))
            hs, gs, ls, ms = hin[b, :, cols], gin[b, :, cols], lend[b, :, cols], mstart[b, :, cols]
            (hh, hl), (gh, gl), (lh, ll), (mh, ml) = split(hs), split(gs), split(ls), split(ms)
            into_f = el * (nn(cc, hh) + nn(cc, hl))
            into_g = eg * (nn(cc, gh) + nn(cc, gl))
            out_f = tl * (nn(bb, lh) + nn(bb, ll))
            out_g = ex * (nn(bb, mh) + nn(bb, ml))
            dxu = dxu + out_f + out_g
            skip = expand(skip8, sp)[0:1]
            dx = st_e * dxu + skip * dy
            dpre[at, cols] = dx * slope[at, cols]
            red_f = red_f + fold(dy * into_f - xst * out_f, sp)
            red_g = red_g + fold(dy * into_g - xst * out_g, sp)
            red_s = red_s + fold(xs * dxu, sp)
            red_k = red_k + fold(xs * dy, sp)
            dtot = decb[b, :, cols]
            h_end = hs * dtot[0:1] + hst[b, :, cols]
            g_start = gs * dtot[0:1] + gst[b, :, cols]
            cf_row = jnp.sum(ls * h_end, axis=0, keepdims=True)
            cg_row = jnp.sum(ms * g_start, axis=0, keepdims=True)
            cross_f = cross_f + fold(jnp.broadcast_to(cf_row, (8, LANES)), sp)
            cross_g = cross_g + fold(jnp.broadcast_to(cg_row, (8, LANES)), sp)
            lefts, rights = [], []
            for scaled, sh, sl_, lowhalf in (
                (xst * tl, lh, ll, True),
                (xst * ex, mh, ml, True),
                (el * dy, hh, hl, False),
                (eg * dy, gh, gl, False),
            ):
                ah, al = split(scaled)
                for a, s in ((ah, sh), (al, sh), (ah, sl_)):
                    lefts.append(a)
                    rights.append(
                        jnp.concatenate([s, zero_state] if lowhalf else [zero_state, s], axis=0)
                    )
            dbc = dbc + nt(jnp.concatenate(lefts, axis=1), jnp.concatenate(rights, axis=1))
        cb_lo, cb_hi = half_masks(cb)
        dbc = dbc + nn_split(q_t, cb_lo.astype(BF16)) + nn_split(q_t.T, cb_hi.astype(BF16))
        dpre[at, INNER:] = dbc * slope[at, INNER:]
        v_f = red_f + at_f[...].T - back_f
        v_g = red_g + at_g[...].T - back_g
        da = precise(tri_high(), v_f) + precise(tri_low(), v_g) + cross_f[0:1] + cross_g[0:1]
        dst = red_s + da * rates
        keep = jnp.logical_and(
            iota((SPAN, LANES), 0) + b * SPAN < left[0], iota((SPAN, LANES), 1) < HEADS
        )
        dr = jnp.where(keep, dst * sigmoid(raw[at, :] + heads[0:1, :]), 0.0)
        draw[at, :] = dr.astype(BF16)
        dheads[0:1, :] += jnp.sum(dr, axis=0, keepdims=True)
        dheads[1:2, :] += jnp.sum(da * st, axis=0, keepdims=True) * rates
        dheads[2:3, :] += jnp.sum(red_k, axis=0, keepdims=True)
        return 0

    lax.fori_loop(0, blocks, block_body, 0)
    cf[...] = conv_in[...].astype(F32)
    dtaps[...] = jnp.zeros_like(dtaps)

    def taps_body(j, _):
        cols = pl.ds(pl.multiple_of(j * LANES, LANES), LANES)
        dp = dpre[:, cols]
        for k in range(CONV):
            first = HALO - CONV + 1 + k
            dtaps[k : k + 1, cols] = jnp.sum(dp * cf[first : first + rows, cols], axis=0, keepdims=True)
        dtaps[CONV : CONV + 1, cols] = jnp.sum(dp, axis=0, keepdims=True)
        return 0

    lax.fori_loop(0, CONV_CH // LANES, taps_body, 0)


def back(conv_low, hgrad, steps, raw, slope, conv_in, hst, gst, lst, mst, into, adj, decb, heads, left, spread):
    rows = hgrad.shape[0]
    blocks = rows // SPAN
    vm = pl.BlockSpec(memory_space=pltpu.VMEM)
    sm = pl.BlockSpec(memory_space=pltpu.SMEM)
    sds = jax.ShapeDtypeStruct
    st = pltpu.VMEM((blocks, STATE, INNER), F32)
    return pl.pallas_call(
        back_kernel,
        out_shape=(
            sds((rows, CONV_CH), F32),
            sds((rows, LANES), BF16),
            sds((8, LANES), F32),
            sds((8, CONV_CH), F32),
        ),
        in_specs=[vm] * 14 + [sm, vm],
        out_specs=(vm,) * 4,
        scratch_shapes=[
            st, st, st, st,
            pltpu.VMEM((LANES, SPAN), F32),
            pltpu.VMEM((LANES, SPAN), F32),
            pltpu.VMEM((rows + HALO, CONV_CH), F32),
        ],
        compiler_params=pltpu.CompilerParams(vmem_limit_bytes=VMEM_BYTES),
        name="back",
    )(conv_low, hgrad, steps, raw, slope, conv_in, hst, gst, lst, mst, into, adj, decb, heads, left, spread)


def tail_kernel(
    dpre, halo, dgate, draw, nlow, w_in, x, cot, gain, taps,
    grad_x, gin, dgain,
    df, pg, ng,
):
    rows = x.shape[0]
    df[0:rows, :] = dpre[...]
    df[rows : rows + 8, :] = halo[...]

    def taps_body(j, _):
        cols = pl.ds(pl.multiple_of(j * LANES, LANES), LANES)
        total = jnp.zeros((rows, LANES), F32)
        for k in range(CONV):
            first = CONV - 1 - k
            total = total + taps[k : k + 1, cols] * df[first : first + rows, cols]
        pg[:, pl.ds(pl.multiple_of(INNER + j * LANES, LANES), LANES)] = total.astype(BF16)
        return 0

    lax.fori_loop(0, CONV_CH // LANES, taps_body, 0)
    pg[:, 0:INNER] = dgate[...]
    pg[:, INNER + CONV_CH :] = draw[...]
    nt_low = nlow[...].T
    ng[...] = jnp.zeros_like(ng)

    def proj_body(j, _):
        cols = pl.ds(pl.multiple_of(j * 256, 256), 256)
        part = pg[:, cols]
        gin[:, cols] = nn(nt_low, part)
        ng[...] += nt(part, w_in[:, cols])
        return 0

    lax.fori_loop(0, WIDE // 256, proj_body, 0)
    dgain[...] = jnp.zeros_like(dgain)

    def norm_body(i, _):
        at = pl.ds(pl.multiple_of(i * 16, 16), 16)
        v = x[at, :].astype(F32)
        r = lax.rsqrt(jnp.mean(v * v, axis=1, keepdims=True) + EPS)
        unit = v * r
        g = ng[at, :]
        prod = g * unit
        dgain[...] += prod[0:8] + prod[8:16]
        gg = g * gain[...]
        grad_x[at, :] = cot[at, :].astype(F32) + r * (gg - unit * jnp.mean(gg * unit, axis=1, keepdims=True))
        return 0

    lax.fori_loop(0, rows // 16, norm_body, 0)


def tail(dpre, halo, dgate, draw, nlow, w_in, x, cot, gain, taps):
    rows = x.shape[0]
    vm = pl.BlockSpec(memory_space=pltpu.VMEM)
    sds = jax.ShapeDtypeStruct
    return pl.pallas_call(
        tail_kernel,
        out_shape=(sds((rows, D), F32), sds((D, WIDE), F32), sds((8, D), F32)),
        in_specs=[vm] * 10,
        out_specs=(vm,) * 3,
        scratch_shapes=[
            pltpu.VMEM((rows + 8, CONV_CH), F32),
            pltpu.VMEM((rows, WIDE), BF16),
            pltpu.VMEM((rows, D), F32),
        ],
        compiler_params=pltpu.CompilerParams(vmem_limit_bytes=VMEM_BYTES),
        name="tail",
    )(dpre, halo, dgate, draw, nlow, w_in, x, cot, gain, taps)


def shifted(value, axis, steps):
    count = lax.axis_size(axis)
    first, last = (max(0, -steps), min(count, count - steps))
    return lax.ppermute(value, axis, [(source, source + steps) for source in range(first, last)])


def on_device(
    x_in, lengths, cotangent, w_in, w_out, small_params, row_in, col_in, row_out, col_out, small_second
):
    n_s = lax.axis_size("seq")
    n_h = lax.axis_size("head")
    seq_index = lax.axis_index("seq")
    head_index = lax.axis_index("head")
    rows = x_in.shape[0]
    rin, cph = w_in.shape
    oph, cout = w_out.shape
    rp = -(-rin // 16) * 16
    wi = tile_count(cph, n_h) * LANES
    wo = tile_count(oph, n_h) * LANES
    pay = jnp.zeros((rp, wi + wo), BF16)
    pay = lax.dynamic_update_slice(pay, w_in.astype(BF16), (0, lax.rem(cph * head_index, LANES)))
    pay = lax.dynamic_update_slice(pay, w_out.astype(BF16).T, (0, wi + lax.rem(oph * head_index, LANES)))
    full = gather(pay, n_s, n_h)[:, :, :rin].reshape(n_h, D, wi + wo)

    first = D + CONV * CONV_CH
    gain = small_params[:D].reshape(1, D)
    taps = jnp.zeros((8, CONV_CH), F32).at[: CONV + 1].set(
        small_params[D : first + CONV_CH].reshape(CONV + 1, CONV_CH)
    )
    first = first + CONV_CH
    heads = jnp.zeros((8, LANES), F32).at[:3, :HEADS].set(
        small_params[first : first + 3 * HEADS].reshape(3, HEADS)
    )
    out_gain = small_params[first + 3 * HEADS :].reshape(1, INNER)
    left = (lengths[0] - head_index * rows).reshape(1)
    spread = jnp.asarray(
        (np.arange(LANES)[:, None] == np.arange(INNER)[None, :] // HEAD_DIM).astype(np.float32)
    ).astype(BF16)
    x_halo = jnp.concatenate([shifted(x_in[rows - HALO :], "head", 1), x_in], axis=0)
    (nlow, w_full, o_full, gate, conv_in, conv_low, slope, raw, steps, hst, gst, dev, decb, dec) = front(
        x_halo, full, gain, taps, heads, left, spread, n_h, cph, oph, wi
    )
    into = chain(dev, dec, n_h, 1)
    result, dgate, hgrad, gout, og_part, lst, mst, dev2 = middle(
        x_in, cotangent, gate, conv_low, steps, hst, gst, into, decb, o_full, heads, out_gain, left, spread
    )
    adj = chain(dev2, dec, n_h, 2)
    dpre, draw, dheads, dtaps = back(
        conv_low, hgrad, steps, raw, slope, conv_in, hst, gst, lst, mst, into, adj, decb, heads, left, spread
    )
    halo = shifted(dpre[:8], "head", -1)
    grad_x, gin, ng_part = tail(dpre, halo, dgate, draw, nlow, w_full, x_in, cotangent, gain, taps)
    small_part = jnp.concatenate(
        [
            jnp.sum(ng_part, axis=0),
            dtaps[: CONV + 1].reshape(-1),
            dheads[:3, :HEADS].reshape(-1),
            jnp.sum(og_part, axis=0),
        ]
    )
    head_in = lax.psum_scatter(gin[:, :PROJ], "head", scatter_dimension=1, tiled=True)
    head_out = lax.psum_scatter(gout.T, "head", scatter_dimension=0, tiled=True)
    grad_in = lax.psum_scatter(head_in, "seq", scatter_dimension=0, tiled=True)
    grad_out = lax.psum_scatter(head_out, "seq", scatter_dimension=1, tiled=True)
    return (result, grad_x) + finish(
        grad_in, grad_out, small_part, w_in, w_out, small_params, row_in, col_in, row_out, col_out, small_second
    )


def finish(
    grad_in, grad_out, small_part, w_in, w_out, small_params, row_in, col_in, row_out, col_out, small_second
):
    seq_count = lax.axis_size("seq")
    head_count = lax.axis_size("head")
    seq_index = lax.axis_index("seq")
    head_index = lax.axis_index("head")
    square_in = grad_in * grad_in
    square_out = grad_out * grad_out
    rows_in, cols_in = grad_in.shape
    rows_out, cols_out = grad_out.shape
    row_in_part = lax.dynamic_update_slice_in_dim(
        jnp.zeros((D,), F32), jnp.sum(square_in, axis=1), seq_index * rows_in, 0
    )
    col_in_part = lax.dynamic_update_slice_in_dim(
        jnp.zeros((PROJ,), F32), jnp.sum(square_in, axis=0), head_index * cols_in, 0
    )
    row_out_part = lax.dynamic_update_slice_in_dim(
        jnp.zeros((INNER,), F32), jnp.sum(square_out, axis=1), head_index * rows_out, 0
    )
    col_out_part = lax.dynamic_update_slice_in_dim(
        jnp.zeros((D,), F32), jnp.sum(square_out, axis=0), seq_index * cols_out, 0
    )
    old_totals = jnp.stack([jnp.sum(row_in) / head_count, jnp.sum(row_out) / seq_count])
    small_grad, row_in_total, col_in_total, row_out_total, col_out_total, old_total = lax.psum(
        (small_part, row_in_part, col_in_part, row_out_part, col_out_part, old_totals), ("seq", "head")
    )
    decay = DECAY
    row_in_new = decay * row_in + (1.0 - decay) * (
        lax.dynamic_slice_in_dim(row_in_total, seq_index * rows_in, rows_in) / PROJ + EPS_SQUARE
    )
    col_in_new = decay * col_in + (1.0 - decay) * (
        lax.dynamic_slice_in_dim(col_in_total, head_index * cols_in, cols_in) / D + EPS_SQUARE
    )
    mean_in = decay * old_total[0] / D + (1.0 - decay) * (jnp.sum(row_in_total) / (D * PROJ) + EPS_SQUARE)
    row_out_new = decay * row_out + (1.0 - decay) * (
        lax.dynamic_slice_in_dim(row_out_total, head_index * rows_out, rows_out) / D + EPS_SQUARE
    )
    col_out_new = decay * col_out + (1.0 - decay) * (
        lax.dynamic_slice_in_dim(col_out_total, seq_index * cols_out, cols_out) / INNER + EPS_SQUARE
    )
    mean_out = decay * old_total[1] / INNER + (1.0 - decay) * (
        jnp.sum(row_out_total) / (INNER * D) + EPS_SQUARE
    )
    scaled_in = grad_in * lax.rsqrt(row_in_new[:, None] * col_in_new[None, :] / mean_in)
    scaled_out = grad_out * lax.rsqrt(row_out_new[:, None] * col_out_new[None, :] / mean_out)
    update_sums = lax.psum(
        jnp.stack([jnp.sum(scaled_in * scaled_in), jnp.sum(scaled_out * scaled_out)]), ("seq", "head")
    )
    spread_in = jnp.sqrt(update_sums[0] / (D * PROJ))
    spread_out = jnp.sqrt(update_sums[1] / (INNER * D))
    w_in_new = w_in - LEARN_RATE * scaled_in / jnp.maximum(1.0, spread_in / CLIP_RMS)
    w_out_new = w_out - LEARN_RATE * scaled_out / jnp.maximum(1.0, spread_out / CLIP_RMS)
    small_second_new = decay * small_second + (1.0 - decay) * (small_grad * small_grad + EPS_SQUARE)
    scaled_small = small_grad * lax.rsqrt(small_second_new)
    spread_small = jnp.sqrt(jnp.mean(scaled_small * scaled_small))
    small_new = small_params - LEARN_SMALL * scaled_small / jnp.maximum(1.0, spread_small / CLIP_RMS)
    return (
        grad_in, row_in_new, col_in_new, w_in_new, grad_out, row_out_new, col_out_new, w_out_new,
        small_grad, small_second_new, small_new,
    )


def solution(mesh):
    both = P(("seq", "head"), None)
    factors = (P("seq", "head"), P("seq"), P("head"), P("seq", "head"))
    return jax.shard_map(
        on_device,
        mesh=mesh,
        in_specs=(
            both, P("seq"), both, P("seq", "head"), P("head", "seq"), P(), P("seq"), P("head"), P("head"), P("seq"), P(),
        ),
        out_specs=(
            both, both, P("seq", "head"), P("seq"), P("head"), P("seq", "head"), P("head", "seq"), P("head"), P("seq"),
            P("head", "seq"), P(), P(), P(),
        ),
        check_vma=False,
    )
```

time: 1480 us -> 873 us (0.59); the launches traced: 1460 us -> 872 us
  local copies, waits for them, and re-layouts: 352 us -> 15.3 us
  Pallas kernels: 0 us -> 305 us
  other arithmetic: 284 us -> 14.6 us
  blocking collectives: 257 us -> 81.3 us
  matrix products: 148 us -> 0 us
  waiting for transfers between devices: 365 us -> 428 us
  starting transfers between devices: 33.8 us -> 6.62 us
    pallas_call x0 -> x7, Pallas kernels: none -> 305 us  [the longest x2 144 us: chain(): pl.pallas_call(functools.partial(chain_kernel, n_h), out_shape=jax.ShapeD...]
    unnamed x9 -> x5, waiting for transfers between devices: 60.1 us -> 344 us
    all_to_all x6 -> x0, waiting for transfers between devices: 175 us -> none  [the longest x1 100 us: on_device(): lax.all_to_all(x_grad.reshape(seq_rows, 1, head_width), 'head', split_axi...]
    unnamed x1 -> x0, blocking collectives: 164 us -> none
    dot_general x30 -> x0, matrix products: 148 us -> none  [the longest x6 48.4 us: direction_scan(): within = jnp.einsum('khts,kshp->kthp', mixing, x_blocks, precision=PRECISE)]
    all_gather x3 -> x0, waiting for transfers between devices: 122 us -> none  [the longest x1 93.4 us: on_device(): lax.all_gather(in_part, 'head', axis=1, tiled=True)]
    reduce_sum x44 -> x11, other arithmetic: 88.7 us -> 8.74 us  [the longest x1 1.75 us: finish(): jnp.sum(scaled_in * scaled_in)]
    reduce_scatter x1 -> x3, waiting for transfers between devices: 0.01 us -> 78.8 us  [the longest x1 46.9 us: on_device(): grad_in = lax.psum_scatter(head_in, 'seq', scatter_dimension=0, tiled=True)]
  transfers between devices with their start and end apart: 15 -> 6, of which waited for: 11 -> 4; matrix products, arithmetic and copies ran while one was open for 38% -> 2% of each run, Pallas kernels for 0% -> 23%
where the time goes in v1:
time: 873 us; the launch traced here: 872 us
  waiting for transfers between devices  428 us (49%)
  Pallas kernels  305 us (35%)
  blocking collectives  81.3 us (9%)
  between operations  21.5 us (2%)
  local copies, waits for them, and re-layouts  15.3 us (2%)
  other arithmetic  14.6 us (2%)
    unnamed x5, waiting for transfers between devices  344 us
    pallas_call x2, Pallas kernels, chain(): pl.pallas_call(functools.partial(chain_kernel, n_h), out_shape=jax.ShapeD...  144 us
    pallas_call x1, Pallas kernels, gather(): pl.pallas_call(functools.partial(gather_kernel, n_s, n_h), out_shape=jax....  55.5 us
    reduce_scatter x1, waiting for transfers between devices, on_device(): grad_in = lax.psum_scatter(head_in, 'seq', scatter_dimension=0, tiled=True)  46.9 us
    psum x1, blocking collectives, finish(): lax.psum(jnp.stack([jnp.sum(scaled_in * scaled_in), jnp.sum(scaled_out *...  41.4 us
    psum x1, blocking collectives, finish(): lax.psum((small_part, row_in_part, col_in_part, row_out_part, col_out_par...  39.9 us
    pallas_call x1, Pallas kernels, back(): pl.pallas_call(back_kernel, out_shape=(sds((rows, CONV_CH), F32), sds((ro...  35.7 us
    reduce_scatter x1, waiting for transfers between devices, on_device(): lax.psum_scatter(head_out, 'seq', scatter_dimension=1, tiled=True)  31.9 us
  transfers between devices with their start and end apart: 6, of which 4 were waited for; matrix products, arithmetic and copies ran while one was open for 2% of the time, Pallas kernels for 23%

profile of v1, /device:TPU:0, one launch (start us, length us, event | category | flops | bytes accessed | tf_op | source)
XLA Modules:
  0.0 872.0 jit_solution(8299666761500263882)
XLA Ops:
  8.0 4.9 collective-permute-start
  13.0 1.0 convert_element_type.9
  14.0 2.1 dynamic_update_slice.18
  16.9 55.5 %gather_weights.1 = bf16[4,8,96,1408]{3,2,1,0:T(8,128)(2,1)} custom-call(bf16[96,1408]{1,0:T(8,128)(2,1)} %copy-done.4), custom_call_target="tpu_custom_call" | custom-call | tf_op jit(solution)/shard_map/gather_weights/pallas_call | solution.py:158
  76.5 22.4 %front.1 = (bf16[384,768]{1,0:T(8,128)(2,1)}, bf16[768,3328]{1,0:T(8,128)(2,1)}, bf16[768,1536]{1,0:T(8,128)(2,1)}, bf16[384,1536]{1,0:T(8,128)(2,1)}, bf16[400,...) custom-call(bf16[400,768]{1,0:T(8,128)(2,1)} %pad_maximum_fusion.x, ...), custom_call_target="tpu_custom_call" | custom-call | tf_op jit(solution)/shard_map/front/pallas_call | solution.py:370
  98.8 54.5 %state_chain.2.into = f32[2,64,1536]{2,1,0:T(8,128)} custom-call(f32[2,64,1536]{2,1,0:T(8,128)} %get-tuple-element.71.dev, f32[8,1536]{1,0:T(8,128)} %get-tuple-element.72.dec), custom_call_target="tpu_custom_call" | custom-call | tf_op jit(solution)/shard_map/state_chain/pallas_call | solution.py:252
  153.4 24.5 %middle.1 = (bf16[384,768]{1,0:T(8,128)(2,1)}, bf16[384,1536]{1,0:T(8,128)(2,1)}, bf16[384,1536]{1,0:T(8,128)(2,1)}, f32[768,1536]{1,0:T(8,128)}, f32[8,1536]{1,...) custom-call(bf16[384,768]{1,0:T(8,128)(2,1)} %x.7, bf16[384,768]{1,0:T(8,128)(2,1)} %cot.3, ...), custom_call_target="tpu_custom_call" | custom-call | tf_op jit(solution)/shard_map/middle/pallas_call | solution.py:530
  177.9 89.6 %state_chain.3.adj = f32[2,64,1536]{2,1,0:T(8,128)} custom-call(f32[2,64,1536]{2,1,0:T(8,128)} %get-tuple-element.82.dev, f32[8,1536]{1,0:T(8,128)} %get-tuple-element.72.dec), custom_call_target="tpu_custom_call" | custom-call | tf_op jit(solution)/shard_map/state_chain/pallas_call | solution.py:252
  267.5 35.7 %back.1 = (f32[384,1664]{1,0:T(8,128)}, bf16[384,128]{1,0:T(8,128)(2,1)}, f32[8,128]{1,0:T(8,128)}, f32[8,1664]{1,0:T(8,128)}) custom-call(bf16[384,1664]{1,0:T(8,128)(2,1)} %get-tuple-element.67.conv_low, bf16[384,1536]{1,0:T(8,128)(2,1)} %get-tuple-element.76.hgrad, f32[384,128]{1,0:T(8,128)} %get-tuple-element.68.steps, ...), custom_call_target="tpu_custom_call" | custom-call | tf_op jit(solution)/shard_map/back/pallas_call | solution.py:703
  304.0 1.3 collective-permute-start.1
  305.3 4.7 collective-permute-done.1.halo
  310.6 22.5 %tail.1 = (f32[384,768]{1,0:T(8,128)}, f32[768,3328]{1,0:T(8,128)}, f32[8,768]{1,0:T(8,128)}) custom-call(f32[384,1664]{1,0:T(8,128)} %get-tuple-element.83.dpre, f32[8,1664]{1,0:T(8,128)} %copy-done.10, bf16[384,1536]{1,0:T(8,128)(2,1)} %get-tuple-element.84.dgate, bf16[384,128]{1,0:T(8,128)(2,1)} %get-tuple-element.85.draw, ...), custom_call_target="tpu_custom_call" | custom-call | tf_op jit(solution)/shard_map/tail/pallas_call | solution.py:777
  335.5 343.7 %all-reduce.7.cloned.1.call-done = f32[768,3224]{1,0:T(8,128)} async-done(((f32[768,3224]{1,0:T(8,128)}), f32[768,3224]{1,0:T(8,128)}) %all-reduce.7.cloned.1.call-update) | async-done | bytes 9904144
  679.2 4.2 constant_dynamic-slice_fusion
  686.9 31.9 %reduce-scatter.9.cloned.1.call-done = f32[384,96]{0,1:T(8,128)} async-done(((f32[384,768]{0,1:T(8,128)}), f32[384,96]{0,1:T(8,128)}) %reduce-scatter.9.cloned.1.call-update) | async-done | bytes 147472 | tf_op jit(solution)/shard_map/reduce_scatter | solution.py:855
  718.8 1.1 multiply_reduce_fusion.4
  720.5 46.9 %reduce-scatter.5.cloned.1.call-done = f32[96,806]{1,0:T(8,128)} async-done(((f32[768,806]{1,0:T(8,128)}), f32[96,806]{1,0:T(8,128)}) %reduce-scatter.5.cloned.1.call-update) | async-done | bytes 309520 | tf_op jit(solution)/shard_map/reduce_scatter | solution.py:854
  767.3 1.2 multiply_reduce_fusion.1
  769.1 39.9 %all-reduce.4 = (f32[768]{0:T(1024)S(1)}, f32[3224]{0:T(1024)S(1)}, f32[2]{0:T(128)S(1)}, f32[1536]{0:T(1024)S(1)}, f32[768]{0:T(1024)S(1)}) all-reduce(f32[768]{0:T(1024)S(1)} %dynamic_update_slice.20, f32[3224]{0:T(1024)S(1)} %dynamic_update_slice.21, f32[2]{0:T(128)S(1)} %pad_maximum_fusion.1, ...), channel_id=1, replica_groups=mesh['seq'=8,'head'=4] {'seq','head'}, use_global_device_ids=true, to_apply=%region_3.0 | all-reduce | flops 6298 | bytes 50384 | tf_op jit(solution)/shard_map/psum | solution.py:885
  813.6 1.8 multiply_reduce_fusion
  815.3 1.6 multiply_reduce_fusion.3
  817.0 1.4 pad_maximum_fusion.2
  818.3 41.4 %all-reduce.3 = (f32[2]{0:T(128)S(1)}, f32[10696]{0:T(1024)S(1)}) all-reduce(f32[2]{0:T(128)S(1)} %pad_maximum_fusion.2, f32[10696]{0:T(1024)S(1)} %concatenate.11), channel_id=1, replica_groups=mesh['seq'=8,'head'=4] {'seq','head'}, use_global_device_ids=true, to_apply=%region_19.0 | all-reduce | flops 10698 | bytes 85584 | tf_op jit(solution)/shard_map/psum | solution.py:907
  864.5 0.9 divide_subtract_fusion
  (104 shorter events, 15.8 us)
Async XLA Ops:
  7.2 9.0 %copy-start.5 = (f32[384,96]{0,1:T(8,128)S(1)}, f32[384,96]{0,1:T(8,128)}, u32[]{:S(2)}) copy-start(f32[384,96]{0,1:T(8,128)} %param.20) | copy-start | bytes 442372
  7.2 9.0 %copy-start.6 = (f32[10696]{0:T(1024)S(1)}, f32[10696]{0:T(1024)}, u32[]{:S(2)}) copy-start(f32[10696]{0:T(1024)} %param.21) | copy-start | bytes 128356
  7.2 326.0 %reduce-scatter.7.cloned.1.call-start = ((), (), s32[]{:S(2)}) async-start(), calls=%async_computation.4 | async-start | bytes 5898240 | tf_op jit(solution)/shard_map/reduce_scatter | solution.py:853
  8.0 67.6 %collective-permute-start = (bf16[16,768]{1,0:T(8,128)(2,1)S(1)}, bf16[16,768]{1,0:T(8,128)(2,1)S(1)}, u32[]{:S(2)}, u32[]{:S(2)}) collective-permute-start(bf16[16,768]{1,0:T(8,128)(2,1)S(1)} %slice.75), channel_id=1, source_target_pairs={{0,1},{1,2},{2,3},{4,5},{5,6},{6,7},{8,9},{9,10},{10,11},{12,13},{... | collective-permute-start | bytes 73736 | tf_op jit(solution)/shard_map/ppermute | solution.py:795
  16.9 56.3 %slice-start = ((f32[10696]{0:T(1024)}), f32[768]{0:T(1024)S(1)}, s32[]{:S(2)}) async-start(f32[10696]{0:T(1024)} %param.21), calls=%async_computation.7 | async-start | bytes 8192 | tf_op jit(solution)/shard_map/slice | solution.py:817
  16.9 58.7 %copy-start = (bf16[384,768]{1,0:T(8,128)(2,1)S(1)}, bf16[384,768]{1,0:T(8,128)(2,1)}, u32[]{:S(2)}) copy-start(bf16[384,768]{1,0:T(8,128)(2,1)} %x.7) | copy-start | bytes 1769476
  177.9 501.4 %all-reduce.7.cloned.1.call-start = ((), (), s32[]{:S(2)}) async-start(), calls=%async_computation.6 | async-start | bytes 20447232
  304.0 6.0 collective-permute-start.1
  333.2 385.7 %reduce-scatter.9.cloned.1.call-start = ((), (), s32[]{:S(2)}) async-start(), calls=%async_computation.5 | async-start | bytes 1327104 | tf_op jit(solution)/shard_map/reduce_scatter | solution.py:855
  333.9 433.4 %reduce-scatter.5.cloned.1.call-start = ((), (), s32[]{:S(2)}) async-start(), calls=%async_computation.3 | async-start | bytes 3096576 | tf_op jit(solution)/shard_map/reduce_scatter | solution.py:854
  683.5 3.4 copy-start.15
  683.5 129.3 %copy-start.20 = (f32[806]{0:T(1024)S(1)}, f32[806]{0:T(1024)}, u32[]{:S(2)}) copy-start(f32[806]{0:T(1024)} %param.23) | copy-start | bytes 9676
  683.5 129.4 %copy-start.23 = (f32[96]{0:T(128)S(1)}, f32[96]{0:T(128)}, u32[]{:S(2)}) copy-start(f32[96]{0:T(128)} %param.25) | copy-start | bytes 1156
  683.5 176.3 %copy-start.13 = (f32[10696]{0:T(1024)S(1)}, f32[10696]{0:T(1024)}, u32[]{:S(2)}) copy-start(f32[10696]{0:T(1024)} %param.26) | copy-start | bytes 128356
  683.5 179.6 %copy-start.7 = (f32[10696]{0:T(1024)S(1)}, f32[10696]{0:T(1024)}, u32[]{:S(2)}) copy-start(f32[10696]{0:T(1024)} %param.21) | copy-start | bytes 128356
  683.5 181.0 %copy-start.2 = (f32[96,806]{1,0:T(8,128)S(1)}, f32[96,806]{1,0:T(8,128)}, u32[]{:S(2)}) copy-start(f32[96,806]{1,0:T(8,128)} %param.19) | copy-start | bytes 928516
  718.8 144.9 %copy-start.3 = (f32[384,96]{0,1:T(8,128)S(1)}, f32[384,96]{0,1:T(8,128)}, u32[]{:S(2)}) copy-start(f32[384,96]{0,1:T(8,128)} %reduce-scatter.9.cloned.1.call-done) | copy-start | bytes 442372
  767.3 97.2 %copy-start.1 = (f32[96,806]{1,0:T(8,128)S(1)}, f32[96,806]{1,0:T(8,128)}, u32[]{:S(2)}) copy-start(f32[96,806]{1,0:T(8,128)} %reduce-scatter.5.cloned.1.call-done) | copy-start | bytes 928516
  809.6 55.8 %copy-start.16 = (f32[384]{0:T(512)}, f32[384]{0:T(512)S(1)}, u32[]{:S(2)}) copy-start(f32[384]{0:T(512)S(1)} %multiply_add_fusion.2) | copy-start | bytes 4612
  812.8 52.6 %copy-start.14 = (f32[806]{0:T(1024)}, f32[806]{0:T(1024)S(1)}, u32[]{:S(2)}) copy-start(f32[806]{0:T(1024)S(1)} %multiply_add_fusion.1) | copy-start | bytes 9676
  812.9 52.5 %copy-start.18 = (f32[96]{0:T(128)}, f32[96]{0:T(128)S(1)}, u32[]{:S(2)}) copy-start(f32[96]{0:T(128)S(1)} %get-tuple-element.113) | copy-start | bytes 1156
  812.9 52.5 %copy-start.19 = (f32[96]{0:T(128)}, f32[96]{0:T(128)S(1)}, u32[]{:S(2)}) copy-start(f32[96]{0:T(128)S(1)} %get-tuple-element.112) | copy-start | bytes 1156
  859.8 5.7 copy-start.8
  860.4 5.0 copy-start.9
  (8 other events, 14.8 us)
Sparse Core Ops, SparseCore 0:
  178.0 89.4 reduce-scatter.6
  333.3 345.8 all-reduce.6
  683.0 35.7 reduce-scatter.8
  723.0 44.2 reduce-scatter.4

commit v2 on v1

--- a/solution.py
+++ b/solution.py
@@ -183,57 +183,81 @@
     for z in (up, down):
         pl.semaphore_signal(bar, inc=1, device_id=(s, z), device_id_type=MESH)
     pl.semaphore_wait(bar, 2)
-    parts = 4
-    width = INNER // parts
+    chain_run(n_h, s, h, up, down, dev, dec, out, snd, us, ur, ds, dr)
+
+
+CHAIN_PARTS = 4
+
+
+def chain_run(n_h, s, h, up, down, dev, dec, out, snd, us, ur, ds, dr):
+    parts = CHAIN_PARTS
+    width = STATE // parts
+    inner = jnp.logical_and(h > 0, h < n_h - 1)
 
     def rc(d, c, sem_s, sem_r, dev_h):
-        cols = pl.ds(c * width, width)
+        at = pl.ds(c * width, width)
         return pltpu.make_async_remote_copy(
-            src_ref=snd.at[d, :, cols],
-            dst_ref=out.at[d, :, cols],
+            src_ref=snd.at[d, at],
+            dst_ref=out.at[d, at],
             send_sem=sem_s.at[c],
             recv_sem=sem_r.at[c],
             device_id=(s, dev_h),
             device_id_type=MESH,
         )
 
-    first = h == 0
-    last = h == n_h - 1
-
-    @pl.when(first)
+    @pl.when(h == 0)
     def _():
         out[0] = jnp.zeros((STATE, INNER), F32)
         snd[0] = dev[0]
         for c in range(parts):
             rc(0, c, us, ur, up).start()
 
-    @pl.when(last)
+    @pl.when(h == n_h - 1)
     def _():
         out[1] = jnp.zeros((STATE, INNER), F32)
         snd[1] = dev[1]
         for c in range(parts):
             rc(1, c, ds, dr, down).start()
 
-    for c in range(parts):
-        cols = slice(c * width, (c + 1) * width)
+    def up_step(c):
+        at = slice(c * width, (c + 1) * width)
 
         @pl.when(h > 0)
         def _():
             rc(0, c, us, ur, down).wait_recv()
 
-        @pl.when(jnp.logical_and(h > 0, h < n_h - 1))
+        @pl.when(inner)
         def _():
-            snd[0, :, cols] = out[0, :, cols] * dec[0:1, cols] + dev[0, :, cols]
+            snd[0, at] = out[0, at] * dec[0:1] + dev[0, at]
             rc(0, c, us, ur, up).start()
+
+    def down_step(c):
+        at = slice(c * width, (c + 1) * width)
 
         @pl.when(h < n_h - 1)
         def _():
             rc(1, c, ds, dr, up).wait_recv()
 
-        @pl.when(jnp.logical_and(h > 0, h < n_h - 1))
+        @pl.when(inner)
         def _():
-            snd[1, :, cols] = out[1, :, cols] * dec[0:1, cols] + dev[1, :, cols]
+            snd[1, at] = out[1, at] * dec[0:1] + dev[1, at]
             rc(1, c, ds, dr, down).start()
+
+    @pl.when(h < n_h // 2)
+    def _():
+        up_step(0)
+        for c in range(parts):
+            if c + 1 < parts:
+                up_step(c + 1)
+            down_step(c)
+
+    @pl.when(h >= n_h // 2)
+    def _():
+        down_step(0)
+        for c in range(parts):
+            if c + 1 < parts:
+                down_step(c + 1)
+            up_step(c)
 
     @pl.when(h < n_h - 1)
     def _():
@@ -254,7 +278,7 @@
         out_shape=jax.ShapeDtypeStruct((2, STATE, INNER), F32),
         in_specs=[vm, vm],
         out_specs=vm,
-        scratch_shapes=[pltpu.VMEM((2, STATE, INNER), F32), dma((4,)), dma((4,)), dma((4,)), dma((4,))],
+        scratch_shapes=[pltpu.VMEM((2, STATE, INNER), F32)] + [dma((CHAIN_PARTS,))] * 4,
         compiler_params=pltpu.CompilerParams(
             collective_id=cid, has_side_effects=True, vmem_limit_bytes=VMEM_BYTES
         ),
@@ -789,6 +813,405 @@
     )(dpre, halo, dgate, draw, nlow, w_in, x, cot, gain, taps)
 
 
+SMALL_ROWS = 88
+NORM_ROWS = D // LANES
+TAPS_ROWS = CONV_CH // LANES
+HEAD_ROW = NORM_ROWS + (CONV + 1) * TAPS_ROWS
+GAIN_ROW = HEAD_ROW + 3
+
+
+def chunk_bounds(per, parts, width):
+    return [(per * q) // LANES * LANES for q in range(parts)] + [width]
+
+
+def peers_of(s, h, n_s, n_h):
+    n_c = n_s // 2
+    chip = s // 2
+    core = lax.rem(s, 2)
+    zpeer = [lax.rem(h + j, n_h) for j in range(1, n_h)]
+    cpeer = [lax.rem(chip + j, n_c) for j in range(1, n_c)]
+    return chip, core, chip * 2 + (1 - core), zpeer, cpeer
+
+
+def remote(src, dst, send, recv, dev):
+    return pltpu.make_async_remote_copy(
+        src_ref=src, dst_ref=dst, send_sem=send, recv_sem=recv, device_id=dev, device_id_type=MESH
+    )
+
+
+def scatter_kernel(
+    n_s, n_h, cph, oph, rin, wi, wo,
+    gin, gout, ngp, dtaps, dheads, ogp,
+    outw, small,
+    r0, pb, r1, acc, zb, r2, sz, sp,
+    s0s, s0r, s1s, s1r, s2s, s2r, szs, szr, sps, spr,
+):
+    s = lax.axis_index("seq")
+    h = lax.axis_index("head")
+    n_c = n_s // 2
+    chip, core, sib, zpeer, cpeer = peers_of(s, h, n_s, n_h)
+    speer = [lax.rem(s + j, n_s) for j in range(1, n_s)]
+    ib = chunk_bounds(cph, n_h, WIDE)
+    ob = chunk_bounds(oph, n_h, INNER)
+    base = [ib[q] + ob[q] for q in range(n_h + 1)]
+    bar = pltpu.get_barrier_semaphore()
+    for z in zpeer:
+        pl.semaphore_signal(bar, inc=1, device_id=(s, z), device_id_type=MESH)
+    for p in speer:
+        pl.semaphore_signal(bar, inc=1, device_id=(p, h), device_id_type=MESH)
+    pl.semaphore_wait(bar, n_h + n_s - 2)
+    sends = []
+
+    def go(c):
+        c.start()
+        sends.append(c)
+
+    def slab(target):
+        return pl.ds(pl.multiple_of(rin * target, 8), rin)
+
+    ks = cpeer + [chip]
+
+    def pieces(q):
+        wq = ib[q + 1] - ib[q]
+        yield 0, gin, slice(ib[q], ib[q + 1]), slice(base[q], base[q] + wq)
+        yield 1, gout, slice(ob[q], ob[q + 1]), slice(base[q] + wq, base[q + 1])
+
+    for i in range(NORM_ROWS):
+        sz[h, i : i + 1, :] = jnp.sum(ngp[:, i * LANES : (i + 1) * LANES], axis=0, keepdims=True)
+    for k in range(CONV + 1):
+        for i in range(TAPS_ROWS):
+            r = NORM_ROWS + k * TAPS_ROWS + i
+            sz[h, r : r + 1, :] = dtaps[k : k + 1, i * LANES : (i + 1) * LANES]
+    sz[h, HEAD_ROW : HEAD_ROW + 3, :] = dheads[0:3, :]
+    for i in range(INNER // LANES):
+        r = GAIN_ROW + i
+        sz[h, r : r + 1, :] = jnp.sum(ogp[:, i * LANES : (i + 1) * LANES], axis=0, keepdims=True)
+    sz[h, GAIN_ROW + INNER // LANES :, :] = jnp.zeros((SMALL_ROWS - GAIN_ROW - INNER // LANES, LANES), F32)
+    for j, z in enumerate(zpeer):
+        go(remote(sz.at[h], sz.at[h], szs.at[j], szr.at[h], (s, z)))
+
+    for q in range(n_h):
+        for j, k in enumerate(ks):
+            for n, src, cols, dst in pieces(q):
+                go(
+                    remote(
+                        src.at[slab(2 * k + 1 - core), cols],
+                        r0.at[k, :, dst],
+                        s0s.at[q, j, n],
+                        s0r.at[q, k, n],
+                        (sib, h),
+                    )
+                )
+
+    def plane_send(q):
+        for j, k in enumerate(ks):
+            for n, src, cols, dst in pieces(q):
+                remote(
+                    src.at[slab(2 * k + core), cols], r0.at[k, :, dst], s0s.at[q, j, n], s0r.at[q, k, n], (sib, h)
+                ).wait_recv()
+                v = src[slab(2 * k + core), cols] + r0[k, :, dst]
+                if j < n_c - 1:
+                    pb[j, 0:rin, dst] = v.astype(BF16)
+                else:
+                    acc[:, dst] = v
+            if j < n_c - 1:
+                at = slice(base[q], base[q + 1])
+                go(remote(pb.at[j, :, at], r1.at[chip, :, at], s1s.at[q, j], s1r.at[q, chip], (2 * k + core, h)))
+
+    def plane_recv(q):
+        at = slice(base[q], base[q + 1])
+        for j, k in enumerate(cpeer):
+            remote(pb.at[j, :, at], r1.at[k, :, at], s1s.at[q, j], s1r.at[q, k], (2 * k + core, h)).wait_recv()
+            acc[:, at] += r1[k, 0:rin, at].astype(F32)
+
+    def window(q):
+        t0, t1 = tiles_of(cph, q)
+        span = (t1 - t0) * LANES
+        wq = ib[q + 1] - ib[q]
+        zb[q, :, 0:wq] = acc[:, base[q] : base[q] + wq]
+        if span > wq:
+            zb[q, :, wq:span] = acc[:, base[q + 1] : base[q + 1] + span - wq]
+        if span < wi:
+            zb[q, :, span:wi] = jnp.zeros((rin, wi - span), F32)
+        t0, t1 = tiles_of(oph, q)
+        span = (t1 - t0) * LANES
+        oq = ob[q + 1] - ob[q]
+        zb[q, :, wi : wi + oq] = acc[:, base[q] + wq : base[q + 1]]
+        if span > oq:
+            start = base[q + 1] + ib[q + 2] - ib[q + 1]
+            zb[q, :, wi + oq : wi + span] = acc[:, start : start + span - oq]
+        if span < wo:
+            zb[q, :, wi + span :] = jnp.zeros((rin, wo - span), F32)
+
+        @pl.when(h != q)
+        def _():
+            remote(zb.at[q], r2.at[h], s2s.at[q], s2r.at[h], (s, q)).start()
+
+    for q in range(n_h):
+        plane_send(q)
+        if q == 0:
+            total = jnp.zeros((SMALL_ROWS, LANES), F32)
+            for j, z in enumerate(zpeer):
+                remote(sz.at[z], sz.at[z], szs.at[j], szr.at[z], (s, z)).wait_recv()
+            for z in range(n_h):
+                total = total + sz[z]
+            sp[s] = total
+            for j, p in enumerate(speer):
+                go(remote(sp.at[s], sp.at[s], sps.at[j], spr.at[s], (p, h)))
+        if q >= 1:
+            plane_recv(q - 1)
+        if q >= 2:
+            window(q - 2)
+    plane_recv(n_h - 1)
+    window(n_h - 2)
+    window(n_h - 1)
+    for j, p in enumerate(speer):
+        remote(sp.at[p], sp.at[p], sps.at[j], spr.at[p], (p, h)).wait_recv()
+    total = jnp.zeros((SMALL_ROWS, LANES), F32)
+    for p in range(n_s):
+        total = total + sp[p]
+    small[...] = total
+    outw[...] = zb[h]
+    for z in zpeer:
+        remote(zb.at[0], r2.at[z], s2s.at[0], s2r.at[z], (s, z)).wait_recv()
+        outw[...] += r2[z]
+    for q in range(n_h):
+
+        @pl.when(h != q)
+        def _():
+            remote(zb.at[q], r2.at[h], s2s.at[q], s2r.at[h], (s, q)).wait_send()
+
+    for c in sends:
+        c.wait_send()
+
+
+def scatter(gin, gout, ngp, dtaps, dheads, ogp, n_s, n_h, cph, oph, rin, wi, wo):
+    n_c = n_s // 2
+    rp = -(-rin // 16) * 16
+    wide = WIDE + INNER
+    dma = pltpu.SemaphoreType.DMA
+    vm = pl.BlockSpec(memory_space=pltpu.VMEM)
+    sds = jax.ShapeDtypeStruct
+    return pl.pallas_call(
+        functools.partial(scatter_kernel, n_s, n_h, cph, oph, rin, wi, wo),
+        out_shape=(sds((rin, wi + wo), F32), sds((SMALL_ROWS, LANES), F32)),
+        in_specs=[vm] * 6,
+        out_specs=(vm, vm),
+        scratch_shapes=[
+            pltpu.VMEM((n_c, rin, wide), F32),
+            pltpu.VMEM((n_c - 1, rp, wide), BF16),
+            pltpu.VMEM((n_c, rp, wide), BF16),
+            pltpu.VMEM((rin, wide), F32),
+            pltpu.VMEM((n_h, rin, wi + wo), F32),
+            pltpu.VMEM((n_h, rin, wi + wo), F32),
+            pltpu.VMEM((n_h, SMALL_ROWS, LANES), F32),
+            pltpu.VMEM((n_s, SMALL_ROWS, LANES), F32),
+            dma((n_h, n_c, 2)),
+            dma((n_h, n_c, 2)),
+            dma((n_h, n_c)),
+            dma((n_h, n_c)),
+            dma((n_h,)),
+            dma((n_h,)),
+            dma((n_h,)),
+            dma((n_h,)),
+            dma((n_s,)),
+            dma((n_s,)),
+        ],
+        compiler_params=pltpu.CompilerParams(
+            collective_id=3, has_side_effects=True, vmem_limit_bytes=VMEM_BYTES
+        ),
+        name="sum_gradients",
+    )(gin, gout, ngp, dtaps, dheads, ogp)
+
+
+def finish_kernel(
+    n_s, n_h, cph, oph, rin, wi, wo,
+    gw, small, w_in, w_out, row_in, col_in, row_out, col_out, params, second,
+    grad_in, row_in_new, col_in_new, w_in_new, grad_out, row_out_new, col_out_new, w_out_new, second_new, params_new,
+    z1, p1, z2, p2, mask,
+    z1s, z1r, p1s, p1r, z2s, z2r, p2s, p2r,
+):
+    s = lax.axis_index("seq")
+    h = lax.axis_index("head")
+    _, _, _, zpeer, _ = peers_of(s, h, n_s, n_h)
+    speer = [lax.rem(s + j, n_s) for j in range(1, n_s)]
+    bar = pltpu.get_barrier_semaphore()
+    for z in zpeer:
+        pl.semaphore_signal(bar, inc=1, device_id=(s, z), device_id_type=MESH)
+    for p in speer:
+        pl.semaphore_signal(bar, inc=1, device_id=(p, h), device_id_type=MESH)
+    sends = []
+
+    def start(buf, me, peers, along_z, snd, rcv):
+        for j, p in enumerate(peers):
+            c = remote(buf.at[me], buf.at[me], snd.at[j], rcv.at[me], (s, p) if along_z else (p, h))
+            c.start()
+            sends.append(c)
+
+    def arrive(buf, peers, along_z, snd, rcv):
+        for j, p in enumerate(peers):
+            remote(buf.at[p], buf.at[p], snd.at[j], rcv.at[p], (s, p) if along_z else (p, h)).wait_recv()
+        total = buf[0]
+        for i in range(1, buf.shape[0]):
+            total = total + buf[i]
+        return total
+
+    keep = 1.0 - DECAY
+    off_in = lax.rem(cph * h, LANES)
+    off_out = lax.rem(oph * h, LANES)
+    rows8 = -(-rin // 8) * 8
+    g_in = pltpu.roll(gw[:, :wi], lax.rem(wi - off_in, wi), 1)[:, :cph]
+    grad_in[...] = g_in
+    g_out = pltpu.roll(gw[:, wi:], lax.rem(wo - off_out, wo), 1)[:, :oph]
+    padded = jnp.concatenate([g_out, jnp.zeros((LANES - rin, oph), F32)], axis=0)
+    grad_out[...] = padded.T[:, :rin]
+    sq_in = g_in * g_in
+    sq_out = g_out * g_out
+    wide_in = jnp.broadcast_to(jnp.sum(sq_in, axis=1, keepdims=True), (rin, LANES))
+    wide_out = jnp.broadcast_to(jnp.sum(sq_out, axis=1, keepdims=True), (rin, LANES))
+    fill = jnp.zeros((LANES - rin, LANES), F32)
+    pick = iota((8, LANES), 0) == 0
+    line_in = jnp.concatenate([wide_in, fill], axis=0).T[0:8]
+    line_out = jnp.concatenate([wide_out, fill], axis=0).T[0:8]
+    z1[h] = jnp.where(pick, line_in, line_out)
+    cs_in = jnp.sum(sq_in, axis=0, keepdims=True)
+    rs_out = jnp.sum(sq_out, axis=0, keepdims=True)
+    pl.semaphore_wait(bar, n_h + n_s - 2)
+    start(z1, h, zpeer, True, z1s, z1r)
+
+    g = small[...]
+    sec = DECAY * second[...] + keep * (g * g + EPS_SQUARE)
+    second_new[...] = sec
+    u = g * lax.rsqrt(sec)
+    total_small = jnp.sum(u * u, keepdims=True)
+    spread_small = jnp.sqrt(total_small / (D + (CONV + 1) * CONV_CH + 3 * HEADS + INNER))
+    params_new[...] = params[...] - LEARN_SMALL * u / jnp.maximum(1.0, spread_small / CLIP_RMS)
+
+    ti = iota((8, LANES), 1) < rin
+    sums = arrive(z1, zpeer, True, z1s, z1r)
+    line_r = DECAY * row_in[...] + keep * (sums[0:1] / PROJ + EPS_SQUARE)
+    line_c = DECAY * col_out[...] + keep * (sums[1:2] / INNER + EPS_SQUARE)
+    row_in_new[...] = line_r
+    col_out_new[...] = line_c
+    row_total = jnp.sum(jnp.where(ti[0:1], line_r, 0.0), axis=1, keepdims=True)
+
+    n_ci = -(-cph // LANES)
+    n_ro = -(-oph // LANES)
+    mask[...] = jnp.zeros_like(mask)
+    mask[0:1, 0:cph] = cs_in
+    mask[0:1, wi : wi + oph] = rs_out
+    p1[s] = jnp.zeros_like(p1[0])
+    for i in range(n_ci):
+        p1[s, i : i + 1, :] = mask[0:1, i * LANES : (i + 1) * LANES]
+    for i in range(n_ro):
+        p1[s, n_ci + i : n_ci + i + 1, :] = mask[0:1, wi + i * LANES : wi + (i + 1) * LANES]
+    p1[s, n_ci + n_ro : n_ci + n_ro + 1, :] = jnp.broadcast_to(row_total, (1, LANES))
+    start(p1, s, speer, False, p1s, p1r)
+    up_r = jnp.broadcast_to(line_r, (LANES, LANES)).T[0:rin, 0:1]
+    up_c = jnp.broadcast_to(line_c, (LANES, LANES)).T[0:rin, 0:1]
+    sums = arrive(p1, speer, False, p1s, p1r)
+    for i in range(n_ci):
+        mask[0:1, i * LANES : (i + 1) * LANES] = sums[i : i + 1]
+    for i in range(n_ro):
+        mask[0:1, wi + i * LANES : wi + (i + 1) * LANES] = sums[n_ci + i : n_ci + i + 1]
+    line_ci = DECAY * col_in[...] + keep * (mask[0:1, 0:cph] / D + EPS_SQUARE)
+    line_ro = DECAY * row_out[...] + keep * (mask[0:1, wi : wi + oph] / D + EPS_SQUARE)
+    col_in_new[...] = line_ci
+    row_out_new[...] = line_ro
+    mean_in = sums[n_ci + n_ro : n_ci + n_ro + 1, 0:1] / D
+    u_in = g_in * lax.rsqrt(up_r * line_ci / mean_in)
+    u_out = g_out * lax.rsqrt(up_c * line_ro)
+    lane = iota((8, LANES), 1)
+    z2[h] = jnp.where(
+        lane == 0,
+        jnp.sum(u_in * u_in, keepdims=True),
+        jnp.where(
+            lane == 1,
+            jnp.sum(u_out * u_out, keepdims=True),
+            jnp.where(lane == 2, jnp.sum(line_ro, axis=1, keepdims=True), 0.0),
+        ),
+    )
+    start(z2, h, zpeer, True, z2s, z2r)
+    p2[s] = arrive(z2, zpeer, True, z2s, z2r)
+    start(p2, s, speer, False, p2s, p2r)
+    mean_out = p2[s, 0:1, 2:3] / INNER
+    sums = arrive(p2, speer, False, p2s, p2r)
+    clip_in = jnp.maximum(1.0, jnp.sqrt(sums[0:1, 0:1] / (D * PROJ)) / CLIP_RMS)
+    clip_out = jnp.maximum(1.0, jnp.sqrt(sums[0:1, 1:2] * mean_out / (INNER * D)) / CLIP_RMS)
+    w_in_new[...] = w_in[...] - LEARN_RATE * u_in / clip_in
+    step_out = LEARN_RATE * (u_out * jnp.sqrt(mean_out)) / clip_out
+    padded = jnp.concatenate([step_out, jnp.zeros((LANES - rin, oph), F32)], axis=0)
+    w_out_new[...] = w_out[...] - padded.T[:, :rin]
+    for c in sends:
+        c.wait_send()
+
+
+def finish(gw, small, w_in, w_out, row_in, col_in, row_out, col_out, params, second, n_s, n_h, wi, wo):
+    rin, cph = w_in.shape
+    oph, _ = w_out.shape
+    dma = pltpu.SemaphoreType.DMA
+    vm = pl.BlockSpec(memory_space=pltpu.VMEM)
+    sds = jax.ShapeDtypeStruct
+    n_rows = -(-(-(-cph // LANES) + -(-oph // LANES) + 1) // 8) * 8
+    line = sds((1, LANES), F32)
+    return pl.pallas_call(
+        functools.partial(finish_kernel, n_s, n_h, cph, oph, rin, wi, wo),
+        out_shape=(
+            sds((rin, cph), F32),
+            line,
+            sds((1, cph), F32),
+            sds((rin, cph), F32),
+            sds((oph, rin), F32),
+            sds((1, oph), F32),
+            line,
+            sds((oph, rin), F32),
+            sds((SMALL_ROWS, LANES), F32),
+            sds((SMALL_ROWS, LANES), F32),
+        ),
+        in_specs=[vm] * 10,
+        out_specs=(vm,) * 10,
+        scratch_shapes=[
+            pltpu.VMEM((n_h, 8, LANES), F32),
+            pltpu.VMEM((n_s, n_rows, LANES), F32),
+            pltpu.VMEM((n_h, 8, LANES), F32),
+            pltpu.VMEM((n_s, 8, LANES), F32),
+            pltpu.VMEM((8, wi + wo), F32),
+            dma((n_h,)),
+            dma((n_h,)),
+            dma((n_s,)),
+            dma((n_s,)),
+            dma((n_h,)),
+            dma((n_h,)),
+            dma((n_s,)),
+            dma((n_s,)),
+        ],
+        compiler_params=pltpu.CompilerParams(
+            collective_id=4, has_side_effects=True, vmem_limit_bytes=VMEM_BYTES
+        ),
+        name="optimizer",
+    )(gw, small, w_in, w_out, row_in, col_in, row_out, col_out, params, second)
+
+
+def to_rows(flat, fill):
+    first = D + (CONV + 1) * CONV_CH
+    rows = [flat[:first].reshape(-1, LANES)]
+    middle = flat[first : first + 3 * HEADS].reshape(3, HEADS)
+    rows.append(jnp.pad(middle, ((0, 0), (0, LANES - HEADS)), constant_values=fill))
+    rows.append(flat[first + 3 * HEADS :].reshape(-1, LANES))
+    rows.append(jnp.full((SMALL_ROWS - GAIN_ROW - INNER // LANES, LANES), fill, F32))
+    return jnp.concatenate(rows, axis=0)
+
+
+def from_rows(rows):
+    return jnp.concatenate(
+        [
+            rows[:HEAD_ROW].reshape(-1),
+            rows[HEAD_ROW:GAIN_ROW, :HEADS].reshape(-1),
+            rows[GAIN_ROW : GAIN_ROW + INNER // LANES].reshape(-1),
+        ]
+    )
+
+
 def shifted(value, axis, steps):
     count = lax.axis_size(axis)
     first, last = (max(0, -steps), min(count, count - steps))
@@ -841,83 +1264,15 @@
     )
     halo = shifted(dpre[:8], "head", -1)
     grad_x, gin, ng_part = tail(dpre, halo, dgate, draw, nlow, w_full, x_in, cotangent, gain, taps)
-    small_part = jnp.concatenate(
-        [
-            jnp.sum(ng_part, axis=0),
-            dtaps[: CONV + 1].reshape(-1),
-            dheads[:3, :HEADS].reshape(-1),
-            jnp.sum(og_part, axis=0),
-        ]
+    gw, small = scatter(gin, gout, ng_part, dtaps, dheads, og_part, n_s, n_h, cph, oph, rin, wi, wo)
+    line = lambda v: jnp.pad(v.reshape(1, -1), ((0, 0), (0, LANES - v.shape[0])))
+    (grad_in, row_in_new, col_in_new, w_in_new, grad_out, row_out_new, col_out_new, w_out_new, second_new, params_new) = finish(
+        gw, small, w_in, w_out, line(row_in), col_in.reshape(1, -1), row_out.reshape(1, -1), line(col_out),
+        to_rows(small_params, 0.0), to_rows(small_second, 1.0), n_s, n_h, wi, wo,
     )
-    head_in = lax.psum_scatter(gin[:, :PROJ], "head", scatter_dimension=1, tiled=True)
-    head_out = lax.psum_scatter(gout.T, "head", scatter_dimension=0, tiled=True)
-    grad_in = lax.psum_scatter(head_in, "seq", scatter_dimension=0, tiled=True)
-    grad_out = lax.psum_scatter(head_out, "seq", scatter_dimension=1, tiled=True)
-    return (result, grad_x) + finish(
-        grad_in, grad_out, small_part, w_in, w_out, small_params, row_in, col_in, row_out, col_out, small_second
-    )
-
-
-def finish(
-    grad_in, grad_out, small_part, w_in, w_out, small_params, row_in, col_in, row_out, col_out, small_second
-):
-    seq_count = lax.axis_size("seq")
-    head_count = lax.axis_size("head")
-    seq_index = lax.axis_index("seq")
-    head_index = lax.axis_index("head")
-    square_in = grad_in * grad_in
-    square_out = grad_out * grad_out
-    rows_in, cols_in = grad_in.shape
-    rows_out, cols_out = grad_out.shape
-    row_in_part = lax.dynamic_update_slice_in_dim(
-        jnp.zeros((D,), F32), jnp.sum(square_in, axis=1), seq_index * rows_in, 0
-    )
-    col_in_part = lax.dynamic_update_slice_in_dim(
-        jnp.zeros((PROJ,), F32), jnp.sum(square_in, axis=0), head_index * cols_in, 0
-    )
-    row_out_part = lax.dynamic_update_slice_in_dim(
-        jnp.zeros((INNER,), F32), jnp.sum(square_out, axis=1), head_index * rows_out, 0
-    )
-    col_out_part = lax.dynamic_update_slice_in_dim(
-        jnp.zeros((D,), F32), jnp.sum(square_out, axis=0), seq_index * cols_out, 0
-    )
-    old_totals = jnp.stack([jnp.sum(row_in) / head_count, jnp.sum(row_out) / seq_count])
-    small_grad, row_in_total, col_in_total, row_out_total, col_out_total, old_total = lax.psum(
-        (small_part, row_in_part, col_in_part, row_out_part, col_out_part, old_totals), ("seq", "head")
-    )
-    decay = DECAY
-    row_in_new = decay * row_in + (1.0 - decay) * (
-        lax.dynamic_slice_in_dim(row_in_total, seq_index * rows_in, rows_in) / PROJ + EPS_SQUARE
-    )
-    col_in_new = decay * col_in + (1.0 - decay) * (
-        lax.dynamic_slice_in_dim(col_in_total, head_index * cols_in, cols_in) / D + EPS_SQUARE
-    )
-    mean_in = decay * old_total[0] / D + (1.0 - decay) * (jnp.sum(row_in_total) / (D * PROJ) + EPS_SQUARE)
-    row_out_new = decay * row_out + (1.0 - decay) * (
-        lax.dynamic_slice_in_dim(row_out_total, head_index * rows_out, rows_out) / D + EPS_SQUARE
-    )
-    col_out_new = decay * col_out + (1.0 - decay) * (
-        lax.dynamic_slice_in_dim(col_out_total, seq_index * cols_out, cols_out) / INNER + EPS_SQUARE
-    )
-    mean_out = decay * old_total[1] / INNER + (1.0 - decay) * (
-        jnp.sum(row_out_total) / (INNER * D) + EPS_SQUARE
-    )
-    scaled_in = grad_in * lax.rsqrt(row_in_new[:, None] * col_in_new[None, :] / mean_in)
-    scaled_out = grad_out * lax.rsqrt(row_out_new[:, None] * col_out_new[None, :] / mean_out)
-    update_sums = lax.psum(
-        jnp.stack([jnp.sum(scaled_in * scaled_in), jnp.sum(scaled_out * scaled_out)]), ("seq", "head")
-    )
-    spread_in = jnp.sqrt(update_sums[0] / (D * PROJ))
-    spread_out = jnp.sqrt(update_sums[1] / (INNER * D))
-    w_in_new = w_in - LEARN_RATE * scaled_in / jnp.maximum(1.0, spread_in / CLIP_RMS)
-    w_out_new = w_out - LEARN_RATE * scaled_out / jnp.maximum(1.0, spread_out / CLIP_RMS)
-    small_second_new = decay * small_second + (1.0 - decay) * (small_grad * small_grad + EPS_SQUARE)
-    scaled_small = small_grad * lax.rsqrt(small_second_new)
-    spread_small = jnp.sqrt(jnp.mean(scaled_small * scaled_small))
-    small_new = small_params - LEARN_SMALL * scaled_small / jnp.maximum(1.0, spread_small / CLIP_RMS)
     return (
-        grad_in, row_in_new, col_in_new, w_in_new, grad_out, row_out_new, col_out_new, w_out_new,
-        small_grad, small_second_new, small_new,
+        result, grad_x, grad_in, row_in_new[0, :rin], col_in_new.reshape(-1), w_in_new, grad_out, row_out_new.reshape(-1),
+        col_out_new[0, :rin], w_out_new, from_rows(small), from_rows(second_new), from_rows(params_new),
     )
 
 

time: 873 us -> 385 us (0.44)
  waiting for transfers between devices: 428 us -> 0.77 us
  blocking collectives: 81.3 us -> 0 us
  Pallas kernels: 305 us -> 344 us
  between operations: 21.5 us -> 1.53 us
  local copies, waits for them, and re-layouts: 15.3 us -> 26 us
  other arithmetic: 14.6 us -> 5.82 us
    unnamed x5 -> x0, waiting for transfers between devices: 344 us -> none
    pallas_call x0 -> x2, Pallas kernels: none -> 126 us  [the longest x1 81.3 us: scatter(): pl.pallas_call(functools.partial(scatter_kernel, n_s, n_h, cph, oph, rin,...]
    pallas_call x2, Pallas kernels: 144 us -> 57.3 us  [chain(): pl.pallas_call(functools.partial(chain_kernel, n_h), out_shape=jax.ShapeD...]
    psum x2 -> x0, blocking collectives: 81.3 us -> none  [the longest x1 41.4 us: finish(): lax.psum(jnp.stack([jnp.sum(scaled_in * scaled_in), jnp.sum(scaled_out *...]
    reduce_scatter x3 -> x0, waiting for transfers between devices: 78.8 us -> none  [the longest x1 46.9 us: on_device(): grad_in = lax.psum_scatter(head_in, 'seq', scatter_dimension=0, tiled=True)]
    reduce_sum x11 -> x0, other arithmetic: 8.74 us -> none  [the longest x1 1.75 us: finish(): jnp.sum(scaled_in * scaled_in)]
  transfers between devices with their start and end apart: 6 -> 2, of which waited for: 4 -> 1; matrix products, arithmetic and copies ran while one was open for 2% -> 4% of each run, Pallas kernels for 23% -> 14%
where the time goes in v2:
time: 385 us; the launch traced here: 384 us
  Pallas kernels  344 us (89%)
  local copies, waits for them, and re-layouts  26 us (7%)
  starting transfers between devices  6.46 us (2%)
  other arithmetic  5.82 us (2%)
    pallas_call x1, Pallas kernels, scatter(): pl.pallas_call(functools.partial(scatter_kernel, n_s, n_h, cph, oph, rin,...  81.3 us
    pallas_call x2, Pallas kernels, chain(): pl.pallas_call(functools.partial(chain_kernel, n_h), out_shape=jax.ShapeD...  57.3 us
    pallas_call x1, Pallas kernels, gather(): pl.pallas_call(functools.partial(gather_kernel, n_s, n_h), out_shape=jax....  55.6 us
    pallas_call x1, Pallas kernels, finish(): pl.pallas_call(functools.partial(finish_kernel, n_s, n_h, cph, oph, rin,...  44.4 us
    pallas_call x1, Pallas kernels, back(): pl.pallas_call(back_kernel, out_shape=(sds((rows, CONV_CH), F32), sds((ro...  35.8 us
    pallas_call x1, Pallas kernels, middle(): pl.pallas_call(middle_kernel, out_shape=(sds((rows, D), BF16), sds((rows,...  24.5 us
    pallas_call x1, Pallas kernels, tail(): pl.pallas_call(tail_kernel, out_shape=(sds((rows, D), F32), sds((D, WIDE)...  22.6 us
    pallas_call x1, Pallas kernels, front(): pl.pallas_call(functools.partial(front_kernel, n_h, cph, oph, wi), out_sh...  22.3 us
  transfers between devices with their start and end apart: 2, of which 1 were waited for; matrix products, arithmetic and copies ran while one was open for 4% of the time, Pallas kernels for 14%

profile of v2, /device:TPU:0, one launch (start us, length us, event | category | flops | bytes accessed | tf_op | source)
XLA Modules:
  0.0 384.5 jit_solution(14380504673417879585)
XLA Ops:
  0.7 0.8 slice.101
  1.4 4.9 %collective-permute-start = (bf16[16,768]{1,0:T(8,128)(2,1)S(1)}, bf16[16,768]{1,0:T(8,128)(2,1)S(1)}, u32[]{:S(2)}, u32[]{:S(2)}) collective-permute-start(bf16[16,768]{1,0:T(8,128)(2,1)S(1)} %slice.101), channel_id=1, source_target_pairs={{0,1},{1,2},{2,3},{4,5},{5,6},{6,7},{8,9},{9,10},{10,11},{12,13},{... | collective-permute-start | bytes 73736 | tf_op jit(solution)/shard_map/ppermute | solution.py:1218
  8.6 1.0 convert_element_type.12
  10.6 2.1 dynamic_update_slice.6
  15.6 55.6 %gather_weights.1 = bf16[4,8,96,1408]{3,2,1,0:T(8,128)(2,1)} custom-call(bf16[96,1408]{1,0:T(8,128)(2,1)} %copy-done.1), custom_call_target="tpu_custom_call" | custom-call | tf_op jit(solution)/shard_map/gather_weights/pallas_call | solution.py:158
  73.9 0.9 pad_maximum_fusion.x
  74.8 22.3 %front.1 = (bf16[384,768]{1,0:T(8,128)(2,1)}, bf16[768,3328]{1,0:T(8,128)(2,1)}, bf16[768,1536]{1,0:T(8,128)(2,1)}, bf16[384,1536]{1,0:T(8,128)(2,1)}, bf16[400,...) custom-call(bf16[400,768]{1,0:T(8,128)(2,1)} %pad_maximum_fusion.x, ...), custom_call_target="tpu_custom_call" | custom-call | tf_op jit(solution)/shard_map/front/pallas_call | solution.py:394
  97.1 34.1 %state_chain.2.into = f32[2,64,1536]{2,1,0:T(8,128)} custom-call(f32[2,64,1536]{2,1,0:T(8,128)} %get-tuple-element.83.dev, f32[8,1536]{1,0:T(8,128)} %get-tuple-element.84.dec), custom_call_target="tpu_custom_call" | custom-call | tf_op jit(solution)/shard_map/state_chain/pallas_call | solution.py:276
  131.2 24.5 %middle.1 = (bf16[384,768]{1,0:T(8,128)(2,1)}, bf16[384,1536]{1,0:T(8,128)(2,1)}, bf16[384,1536]{1,0:T(8,128)(2,1)}, f32[768,1536]{1,0:T(8,128)}, f32[8,1536]{1,...) custom-call(bf16[384,768]{1,0:T(8,128)(2,1)} %x.15, bf16[384,768]{1,0:T(8,128)(2,1)} %cot.3, ...), custom_call_target="tpu_custom_call" | custom-call | tf_op jit(solution)/shard_map/middle/pallas_call | solution.py:554
  155.8 23.2 %state_chain.3.adj = f32[2,64,1536]{2,1,0:T(8,128)} custom-call(f32[2,64,1536]{2,1,0:T(8,128)} %get-tuple-element.94.dev, f32[8,1536]{1,0:T(8,128)} %get-tuple-element.84.dec), custom_call_target="tpu_custom_call" | custom-call | tf_op jit(solution)/shard_map/state_chain/pallas_call | solution.py:276
  179.0 35.8 %back.1 = (f32[384,1664]{1,0:T(8,128)}, bf16[384,128]{1,0:T(8,128)(2,1)}, f32[8,128]{1,0:T(8,128)}, f32[8,1664]{1,0:T(8,128)}) custom-call(bf16[384,1664]{1,0:T(8,128)(2,1)} %get-tuple-element.79.conv_low, bf16[384,1536]{1,0:T(8,128)(2,1)} %get-tuple-element.88.hgrad, f32[384,128]{1,0:T(8,128)} %get-tuple-element.80.steps, ...), custom_call_target="tpu_custom_call" | custom-call | tf_op jit(solution)/shard_map/back/pallas_call | solution.py:727
  214.8 0.8 slice.106
  215.6 1.5 collective-permute-start.1
  217.9 0.8 copy.25.w_out
  222.3 22.6 %tail.1 = (f32[384,768]{1,0:T(8,128)}, f32[768,3328]{1,0:T(8,128)}, f32[8,768]{1,0:T(8,128)}) custom-call(f32[384,1664]{1,0:T(8,128)} %get-tuple-element.95.dpre, f32[8,1664]{1,0:T(8,128)} %copy-done.7, bf16[384,1536]{1,0:T(8,128)(2,1)} %get-tuple-element.96.dgate, bf16[384,128]{1,0:T(8,128)(2,1)} %get-tuple-element.97.draw, ...), custom_call_target="tpu_custom_call" | custom-call | tf_op jit(solution)/shard_map/tail/pallas_call | solution.py:801
  244.9 81.3 %sum_gradients.1 = (f32[96,1408]{1,0:T(8,128)}, f32[88,128]{1,0:T(8,128)}) custom-call(f32[768,3328]{1,0:T(8,128)} %get-tuple-element.101.gin, f32[768,1536]{1,0:T(8,128)} %get-tuple-element.102.gout, f32[8,768]{1,0:T(8,128)} %get-tuple-element.103.ngp, f32[8,1664]{1,0:T(8,128)} %get-tuple-element.104.dtaps, f32[8,128]{1,0:T(8,128)} %get-tuple-element.105.dheads, ...), custom_call_target="tpu_custom_call" | custom-call | tf_op jit(solution)/shard_map/sum_gradients/pallas_call | solution.py:995
  326.2 44.4 %optimizer.1 = (f32[96,806]{1,0:T(8,128)}, f32[1,128]{1,0:T(1,128)}, f32[1,806]{1,0:T(1,128)}, f32[96,806]{1,0:T(8,128)}, f32[384,96]{1,0:T(8,128)}, /*index=5*/...) custom-call(f32[96,1408]{1,0:T(8,128)} %get-tuple-element.107.gw, ...), custom_call_target="tpu_custom_call" | custom-call | tf_op jit(solution)/shard_map/optimizer/pallas_call | solution.py:1157
  370.6 0.8 slice_bitcast_fusion.5
  371.4 0.8 slice_bitcast_fusion
  373.9 1.7 copy.26
  375.6 1.7 copy.27
  377.3 1.3 reduce.4
  378.6 1.2 reduce.5
  379.8 1.1 slice_bitcast_fusion.9
  (67 shorter events, 17.5 us)
Async XLA Ops:
  0.6 14.3 %copy-start.6 = (f32[10696]{0:T(1024)S(1)}, f32[10696]{0:T(1024)}, u32[]{:S(2)}) copy-start(f32[10696]{0:T(1024)} %param.21) | copy-start | bytes 128356
  0.7 12.1 %copy-start.2 = (f32[384,96]{0,1:T(8,128)S(1)}, f32[384,96]{0,1:T(8,128)}, u32[]{:S(2)}) copy-start(f32[384,96]{0,1:T(8,128)} %param.20) | copy-start | bytes 442372
  1.4 72.4 %collective-permute-start = (bf16[16,768]{1,0:T(8,128)(2,1)S(1)}, bf16[16,768]{1,0:T(8,128)(2,1)S(1)}, u32[]{:S(2)}, u32[]{:S(2)}) collective-permute-start(bf16[16,768]{1,0:T(8,128)(2,1)S(1)} %slice.101), channel_id=1, source_target_pairs={{0,1},{1,2},{2,3},{4,5},{5,6},{6,7},{8,9},{9,10},{10,11},{12,13},{... | collective-permute-start | bytes 73736 | tf_op jit(solution)/shard_map/ppermute | solution.py:1218
  12.8 2.8 copy-start.1
  15.6 56.9 %slice-start = ((f32[10696]{0:T(1024)}), f32[768]{0:T(1024)S(1)}, s32[]{:S(2)}) async-start(f32[10696]{0:T(1024)} %param.21), calls=%async_computation | async-start | bytes 8192 | tf_op jit(solution)/shard_map/slice | solution.py:1240
  15.6 58.3 %copy-start = (bf16[384,768]{1,0:T(8,128)(2,1)S(1)}, bf16[384,768]{1,0:T(8,128)(2,1)}, u32[]{:S(2)}) copy-start(bf16[384,768]{1,0:T(8,128)(2,1)} %x.15) | copy-start | bytes 1769476
  179.0 39.7 %copy-start.8 = (f32[806]{0:T(1024)S(1)}, f32[806]{0:T(1024)}, u32[]{:S(2)}) copy-start(f32[806]{0:T(1024)} %param.23) | copy-start | bytes 9676
  179.0 40.3 %copy-start.9 = (f32[384]{0:T(512)S(1)}, f32[384]{0:T(512)}, u32[]{:S(2)}) copy-start(f32[384]{0:T(512)} %param.24) | copy-start | bytes 4612
  179.0 40.9 %copy-start.10 = (f32[96]{0:T(128)S(1)}, f32[96]{0:T(128)}, u32[]{:S(2)}) copy-start(f32[96]{0:T(128)} %param.22) | copy-start | bytes 1156
  179.0 41.4 %copy-start.11 = (f32[96]{0:T(128)S(1)}, f32[96]{0:T(128)}, u32[]{:S(2)}) copy-start(f32[96]{0:T(128)} %param.25) | copy-start | bytes 1156
  215.6 6.0 %collective-permute-start.1 = (f32[8,1664]{1,0:T(8,128)S(1)}, f32[8,1664]{1,0:T(8,128)S(1)}, u32[]{:S(2)}, u32[]{:S(2)}) collective-permute-start(f32[8,1664]{1,0:T(8,128)S(1)} %slice.106), channel_id=1, source_target_pairs={{1,0},{2,1},{3,2},{5,4},{6,5},{7,6},{9,8},{10,9},{11,10},{13,12},{... | collective-permute-start | bytes 159752 | tf_op jit(solution)/shard_map/ppermute | solution.py:1218
  221.7 0.6 copy-start.7
  326.2 47.4 %copy-start.5 = (f32[88,128]{1,0:T(8,128)S(1)}, f32[88,128]{1,0:T(8,128)}, u32[]{:S(2)}) copy-start(f32[88,128]{1,0:T(8,128)} %get-tuple-element.108.small) | copy-start | bytes 135172
  370.6 12.4 %copy-start.4 = (f32[96,806]{1,0:T(8,128)S(1)}, f32[96,806]{1,0:T(8,128)}, u32[]{:S(2)}) copy-start(f32[96,806]{1,0:T(8,128)} %get-tuple-element.155) | copy-start | bytes 928516
  370.6 13.1 %copy-start.3 = (f32[96,806]{1,0:T(8,128)S(1)}, f32[96,806]{1,0:T(8,128)}, u32[]{:S(2)}) copy-start(f32[96,806]{1,0:T(8,128)} %get-tuple-element.158) | copy-start | bytes 928516

commit v3 on v0

v3 whole, which is shorter than its diff:
```python
import functools

import jax
import jax.numpy as jnp
import numpy as np
from jax import lax
from jax.experimental import pallas as pl
from jax.experimental.pallas import tpu as pltpu
from jax.sharding import PartitionSpec as P

D = 768
HEADS = 24
HEAD_DIM = 64
STATE = 64
CONV = 4
SPAN = 128
STEP = 8
INNER = 1536
CONV_CH = 1664
PROJ = 3224
WIDE = 3328
LANES = 128
HALO = 16

EPS = 1e-05
EPS_SQUARE = 1e-30
LEARN_RATE = 0.3
LEARN_SMALL = 3.0
CLIP_RMS = 0.1
DECAY = 1.0 - STEP ** (-0.8)
F32 = jnp.float32
BF16 = jnp.bfloat16
HIGHEST = lax.Precision.HIGHEST
MESH = pl.DeviceIdType.MESH
VMEM_BYTES = 60 << 20


def nn(left, right):
    return lax.dot_general(left, right, (((1,), (0,)), ((), ())), preferred_element_type=F32)


def nt(left, right):
    return lax.dot_general(left, right, (((1,), (1,)), ((), ())), preferred_element_type=F32)


def split(value):
    high = value.astype(BF16)
    return high, (value - high.astype(F32)).astype(BF16)


def nn_split(value, exact):
    high, low = split(value)
    return nn(high, exact) + nn(low, exact)


def expand(value, spread):
    return nn_split(value, spread)


def fold(value, spread):
    high, low = split(value)
    return nt(high, spread) + nt(low, spread)


def iota(shape, dim):
    return lax.broadcasted_iota(jnp.int32, shape, dim)


def tri_low():
    return (iota((SPAN, SPAN), 0) >= iota((SPAN, SPAN), 1)).astype(F32)


def tri_high():
    return (iota((SPAN, SPAN), 0) <= iota((SPAN, SPAN), 1)).astype(F32)


def precise(left, right):
    return lax.dot_general(
        left, right, (((1,), (0,)), ((), ())), precision=HIGHEST, preferred_element_type=F32
    )


def sigmoid(value):
    return 1.0 / (1.0 + jnp.exp(-value))


def tiles_of(per_part, index):
    return (per_part * index) // LANES, -(-(per_part * (index + 1)) // LANES)


def tile_count(per_part, parts):
    return max(e - s for s, e in (tiles_of(per_part, i) for i in range(parts)))


def half_masks(value):
    low = iota(value.shape, 1) < HEAD_DIM
    zero = jnp.zeros_like(value)
    return jnp.where(low, value, zero), jnp.where(low, zero, value)


def head_terms(steps, rates):
    logs = steps * rates
    incl = precise(tri_low(), logs)
    return incl, incl - logs, incl[SPAN - 1 : SPAN]


CHAIN_PARTS = 4


class Chain:
    def __init__(self, n_h, s, h, dev, dec, out, snd, us, ur, ds, dr):
        self.n_h, self.s, self.h = n_h, s, h
        self.dev, self.dec, self.out, self.snd = dev, dec, out, snd
        self.sems = ((us, ur), (ds, dr))
        self.next = (lax.rem(h + 1, n_h), lax.rem(h + n_h - 1, n_h))
        self.inner = jnp.logical_and(h > 0, h < n_h - 1)
        self.first = (h == 0, h == n_h - 1)
        self.last = (h == n_h - 1, h == 0)

    def link(self, d, c):
        width = STATE // CHAIN_PARTS
        at = pl.ds(c * width, width)
        snd, rcv = self.sems[d]
        return remote(self.snd.at[d, at], self.out.at[d, at], snd.at[c], rcv.at[c], (self.s, self.next[d]))

    def begin(self):
        for d in range(2):

            @pl.when(self.first[d])
            def _():
                self.out[d] = jnp.zeros((STATE, INNER), F32)
                self.snd[d] = self.dev[d]
                for c in range(CHAIN_PARTS):
                    self.link(d, c).start()

    def step(self, d, c):
        width = STATE // CHAIN_PARTS
        at = slice(c * width, (c + 1) * width)

        @pl.when(jnp.logical_not(self.first[d]))
        def _():
            self.link(d, c).wait_recv()

        @pl.when(self.inner)
        def _():
            self.snd[d, at] = self.out[d, at] * self.dec[0:1] + self.dev[d, at]
            self.link(d, c).start()

    def at(self, k):
        for c in range(CHAIN_PARTS):

            @pl.when(k == 2 * self.h + c)
            def _():
                self.step(0, c)

            @pl.when(k == 2 * (self.n_h - 1 - self.h) + c)
            def _():
                self.step(1, c)

    def steps(self):
        return 2 * (self.n_h - 1) + CHAIN_PARTS

    def finish(self):
        for d in range(2):

            @pl.when(jnp.logical_not(self.last[d]))
            def _():
                for c in range(CHAIN_PARTS):
                    self.link(d, c).wait_send()


def remote(src, dst, send, recv, dev):
    return pltpu.make_async_remote_copy(
        src_ref=src, dst_ref=dst, send_sem=send, recv_sem=recv, device_id=dev, device_id_type=MESH
    )


def split3(value):
    high = value.astype(BF16)
    rest = value - high.astype(F32)
    mid, low = split(rest)
    return high, mid, low


def flat_rows(flat, rows, fill):
    count = SMALL // LANES
    for i in range(count):
        rows[i : i + 1, :] = flat[pl.ds(i * LANES, LANES)].reshape(1, LANES)
    rows[count:, :] = jnp.full((rows.shape[0] - count, LANES), fill, F32)
    rest = SMALL - count * LANES
    rows[count : count + 1, 0:rest] = flat[pl.ds(count * LANES, rest)].reshape(1, rest)


def piece_map(dp, rin, rp):
    place = iota((dp, D), 0)
    return jnp.logical_and(place // rp * rin + place % rp == iota((dp, D), 1), place % rp < rin).astype(BF16)


def unpack_rows(rows, rin, rp, gain, taps, heads, out_gain):
    dp = gain.shape[1]
    first = D // LANES
    flat_gain = jnp.concatenate([rows[i : i + 1, :] for i in range(first)], axis=1)
    if dp == D:
        gain[...] = flat_gain
    else:
        parts = split3(jnp.broadcast_to(flat_gain, (8, D)))
        gain[...] = sum(nt(p, piece_map(dp, rin, rp)) for p in parts)[0:1]
    taps[...] = jnp.zeros_like(taps)
    for k in range(CONV + 1):
        for i in range(TAPS_ROWS):
            r = first + k * TAPS_ROWS + i
            taps[k : k + 1, i * LANES : (i + 1) * LANES] = rows[r : r + 1, :]
    r = HEAD_ROW
    lane = iota((1, LANES), 1)
    line = rows[r : r + 1, :]
    heads[...] = jnp.zeros_like(heads)
    for n in range(3):
        v = line if n == 0 else pltpu.roll(line, LANES - n * HEADS, 1)
        heads[n : n + 1, :] = jnp.where(lane < HEADS, v, 0.0)
    if out_gain is not None:
        turn = LANES - 3 * HEADS
        for i in range(INNER // LANES):
            here = pltpu.roll(rows[r + i : r + i + 1, :], turn, 1)
            after = pltpu.roll(rows[r + i + 1 : r + i + 2, :], turn, 1)
            out_gain[0:1, i * LANES : (i + 1) * LANES] = jnp.where(lane < turn, here, after)


def fill_spread(spread):
    spread[...] = (iota((LANES, INNER), 0) == iota((LANES, INNER), 1) // HEAD_DIM).astype(BF16)


class Gather:
    def __init__(self, n_s, n_h, s, h, full, lanes, sems):
        self.n_s, self.n_h, self.s, self.h, self.full, self.lanes = n_s, n_h, s, h, full, lanes
        self.zs, self.zr, self.ps, self.pr, self.ds, self.dr, self.cs, self.cr = sems
        self.n_c = n_s // 2
        self.chip = s // 2
        self.core = lax.rem(s, 2)
        self.sib = self.chip * 2 + (1 - self.core)
        self.cpeer = [lax.rem(self.chip + j, self.n_c) for j in range(1, self.n_c)]
        self.square = self.n_c == 4
        self.xn = self.chip + 1 - 2 * lax.rem(self.chip, 2)
        self.yn = lax.rem(self.chip + self.n_c // 2, self.n_c)
        self.diag = 3 - self.chip
        self.inner = jnp.logical_and(h > 0, h < n_h - 1)
        self.order = [h] + [self.nth(j) for j in range(1, n_h)]

    def nth(self, j):
        n_h, h = self.n_h, self.h
        below = jnp.where(j - 1 >= h, j, j - 1)
        mirror = n_h - 1 - h
        above = n_h - 1 - jnp.where(j - 1 >= mirror, j, j - 1)
        return jnp.where(2 * h < n_h, below, above)

    def blk(self, q, c, part=None):
        ref = self.full.at[q, c * 2 + self.core]
        rp = self.full.shape[2]
        if part is None:
            return ref.at[:, self.lanes]
        mid = rp // 2 // 16 * 16
        return ref.at[pl.ds(0, mid) if part == 0 else pl.ds(mid, rp - mid), self.lanes]

    def along(self, q, way):
        ref = self.blk(q, self.chip)
        to = lax.rem(self.h + (1 if way == 0 else self.n_h - 1), self.n_h)
        return remote(ref, ref, self.zs.at[q, way], self.zr.at[q], (self.s, to))

    def begin(self):
        @pl.when(self.h < self.n_h - 1)
        def _():
            self.along(self.h, 0).start()

        @pl.when(self.h > 0)
        def _():
            self.along(self.h, 1).start()

        self.spread_out(0)

    def z_in(self, i):
        q = self.order[i]
        self.along(q, 0).wait_recv()

        @pl.when(jnp.logical_and(q < self.h, self.h < self.n_h - 1))
        def _():
            self.along(q, 0).start()

        @pl.when(jnp.logical_and(q > self.h, self.h > 0))
        def _():
            self.along(q, 1).start()

    def z_done(self):
        for i in range(self.n_h):
            q = self.order[i]

            @pl.when(jnp.logical_and(q <= self.h, self.h < self.n_h - 1))
            def _():
                self.along(q, 0).wait_send()

            @pl.when(jnp.logical_and(q >= self.h, self.h > 0))
            def _():
                self.along(q, 1).wait_send()

    def to_chip(self, i, m, part, q, c):
        ref = self.blk(q, self.chip, part)
        n = 0 if part is None else part
        return remote(ref, ref, self.ps.at[i, m, n], self.pr.at[q, self.chip, n], (c * 2 + self.core, self.h))

    def over(self, i, j, q, c):
        ref = self.blk(q, c)
        return remote(ref, ref, self.cs.at[i, j], self.cr.at[q, c], (self.sib, self.h))

    def spread_out(self, i):
        for c in self.to_chips(i):
            c.start()
        self.over(i, 0, self.order[i], self.chip).start()

    def to_chips(self, i):
        q = self.order[i]
        if self.square:
            near = ((0, self.xn), (1, self.yn))
            return [self.to_chip(i, m, (n + m) % 2, q, c) for n in range(2) for m, c in near]
        return [self.to_chip(i, j, None, q, c) for j, c in enumerate(self.cpeer)]

    def onward(self, i, n):
        q = self.order[i]
        c, to = (self.xn, self.yn) if n == 0 else (self.yn, self.xn)
        ref = self.blk(q, c, n)
        return remote(ref, ref, self.ds.at[i, n], self.dr.at[q, n], (to * 2 + self.core, self.h))

    def got(self, q, c, part):
        ref = self.blk(q, c, part)
        n = 0 if part is None else part
        remote(ref, ref, self.ps.at[0, 0, 0], self.pr.at[q, c, n], (self.sib, self.h)).wait_recv()

    def pass_on(self, i):
        q = self.order[i]
        if self.square:
            for n, c in ((0, self.xn), (1, self.yn)):
                self.got(q, c, n)
                self.onward(i, n).start()
            for n, c in ((1, self.xn), (0, self.yn)):
                self.got(q, c, n)
                self.over(i, 2 - n, q, c).start()
        else:
            for j, c in enumerate(self.cpeer):
                self.got(q, c, None)
                self.over(i, j + 1, q, c).start()

    def last_in(self, i):
        if self.square:
            q = self.order[i]
            for n in range(2):
                ref = self.blk(q, self.diag, n)
                remote(ref, ref, self.ds.at[0, 0], self.dr.at[q, n], (self.sib, self.h)).wait_recv()
            self.over(i, 3, q, self.diag).start()

    def complete(self, i):
        q = self.order[i]
        for c in [self.chip] + self.cpeer:
            ref = self.full.at[q, c * 2 + 1 - self.core].at[:, self.lanes]
            remote(ref, ref, self.cs.at[0, 0], self.cr.at[q, c], (self.sib, self.h)).wait_recv()

    def plan(self, columns):
        n_h = self.n_h

        def run(*steps):
            def all_steps():
                for step in steps:
                    step()

            return all_steps

        plan = [lambda: self.z_in(1), lambda: self.spread_out(1)]
        if n_h > 2:
            plan.append(lambda: pl.when(self.inner)(lambda: self.z_in(2)))
        plan.append(lambda: self.pass_on(0))
        for i in range(2, n_h):
            if i == 2:
                plan.append(lambda: pl.when(jnp.logical_not(self.inner))(lambda: self.z_in(2)))
            else:
                plan.append(lambda i=i: self.z_in(i))
            plan.append(lambda i=i: self.spread_out(i))
            plan.append(run(lambda i=i: self.last_in(i - 2), lambda i=i: self.pass_on(i - 1)))
            plan.append(run(lambda i=i: self.complete(i - 2), lambda i=i: columns(i - 2)))
        plan.append(run(lambda: self.last_in(n_h - 2), lambda: self.pass_on(n_h - 1)))
        plan.append(run(lambda: self.complete(n_h - 2), lambda: columns(n_h - 2)))
        plan.append(run(lambda: self.last_in(n_h - 1), lambda: self.complete(n_h - 1), lambda: columns(n_h - 1)))
        return plan

    def finish(self):
        self.z_done()
        for i in range(self.n_h):
            q = self.order[i]
            chips = [self.chip] + ([self.xn, self.yn, self.diag] if self.square else self.cpeer)
            for c in self.to_chips(i):
                c.wait_send()
            for j, c in enumerate(chips):
                self.over(i, j, q, c).wait_send()
            if self.square:
                for n in range(2):
                    self.onward(i, n).wait_send()


def gather_sems(n_s, n_h):
    dma = pltpu.SemaphoreType.DMA
    n_c = n_s // 2
    return [
        dma((n_h, 2)), dma((n_h,)), dma((n_h, n_c, 2)), dma((n_h, n_c, 2)), dma((n_h, 2)), dma((n_h, 2)), dma((n_h, n_c)),
        dma((n_h, n_c)),
    ]


def fore_kernel(
    n_s, n_h, cph, oph, rin, rp, wi, wo,
    x, cot, w_in, w_out_t, flat, lengths,
    result, w_full_o, nlow_o, conv_in_o, conv_low_o, slope_o, raw, steps, decb, dec, dgate, hgrad, glow, dgain, lst, mst,
    dev2, hin_o, gin_o,
    full, w_full, o_full, xh, shift_in, shift_out, nscr, conv_in, conv_low, slope, cf, gate, hst, gst, dev, into, csnd, incl_r,
    excl_r, incl_t, excl_t, steps_t, inter_s, yb, el, eg, gg_scr, hin, gin, prm, gain, taps, heads, out_gain, spread,
    xs_, xr_, us, ur, dws, dwr, outs, *gsems,
):
    s = lax.axis_index("seq")
    h = lax.axis_index("head")
    n_c = n_s // 2
    rows = x.shape[0]
    dp = x.shape[1]
    blocks = rows // SPAN
    chip = s // 2
    core = lax.rem(s, 2)
    sib = chip * 2 + (1 - core)
    cpeer = [lax.rem(chip + j, n_c) for j in range(1, n_c)]
    left = lengths[0] - h * rows
    g_in = Gather(n_s, n_h, s, h, full, slice(0, wi), gsems[:8])
    g_out = Gather(n_s, n_h, s, h, full, slice(wi, wi + wo), gsems[8:])
    zpeer = [lax.rem(h + j, n_h) for j in range(1, n_h)]
    bar = pltpu.get_barrier_semaphore()
    for z in zpeer:
        pl.semaphore_signal(bar, inc=1, device_id=(s, z), device_id_type=MESH)
    for c in cpeer:
        pl.semaphore_signal(bar, inc=1, device_id=(c * 2 + core, h), device_id_type=MESH)
    pl.semaphore_signal(bar, inc=1, device_id=(sib, h), device_id_type=MESH)

    shift_in[...] = jnp.zeros_like(shift_in)
    shift_in[0:rin, 0:cph] = w_in[...]
    full[h, s, :, 0:wi] = pltpu.roll(shift_in[...], lax.rem(cph * h, LANES), 1).astype(BF16)
    shift_out[...] = jnp.zeros_like(shift_out)
    shift_out[0:rin, 0:oph] = w_out_t[...]
    turned = shift_out[...]
    if oph % LANES:
        turned = pltpu.roll(turned, lax.rem(oph * h, LANES), 1)
    full[h, s, :, wi:] = turned.astype(BF16)
    pl.semaphore_wait(bar, n_h + n_c - 1)

    g_in.begin()
    up = lax.rem(h + 1, n_h)
    halo = remote(x.at[rows - HALO : rows], xh, xs_.at[0], xr_.at[0], (s, up))

    @pl.when(h < n_h - 1)
    def _():
        halo.start()

    flat_rows(flat, prm, 0.0)
    unpack_rows(prm, rin, rp, gain, taps, heads, out_gain)
    fill_spread(spread)

    def norm_rows(src, at, dst):
        v = src[at, :].astype(F32)
        n = v * lax.rsqrt(jnp.sum(v * v, axis=1, keepdims=True) * (1.0 / D) + EPS) * gain[...]
        nscr[dst, :] = n.astype(BF16)

    def norm_body(i, _):
        at = pl.multiple_of(i * 16, 16)
        norm_rows(x, pl.ds(at, 16), pl.ds(at + HALO, 16))
        return 0

    lax.fori_loop(0, rows // 16, norm_body, 0)

    @pl.when(h > 0)
    def _():
        halo.wait_recv()

    @pl.when(h == 0)
    def _():
        xh[...] = jnp.zeros_like(xh)

    norm_rows(xh, slice(0, HALO), slice(0, HALO))

    def leave(src, dst, n):
        return pltpu.make_async_copy(src, dst, outs.at[n])

    leaving = [leave(nscr.at[HALO:], nlow_o, 0)]
    leaving[0].start()

    def project(tile, weights):
        w_full[:, pl.ds(pl.multiple_of(tile * LANES, LANES), LANES)] = weights
        v = nn(nscr[...], weights).astype(BF16)
        first, last = INNER // LANES, WIDE // LANES - 1

        @pl.when(tile < first)
        def _():
            gate[:, pl.ds(pl.multiple_of(tile * LANES, LANES), LANES)] = v[HALO:]

        @pl.when(tile == last)
        def _():
            raw[...] = v[HALO:].astype(F32)

        @pl.when(jnp.logical_and(tile >= first, tile < last))
        def _():
            at = pl.ds(pl.multiple_of((tile - first) * LANES, LANES), LANES)
            conv_in[:, at] = v
            cf[...] = v.astype(F32)
            total = jnp.zeros((rows, LANES), F32) + taps[CONV : CONV + 1, at]
            for k in range(CONV):
                start = HALO - CONV + 1 + k
                total = total + taps[k : k + 1, at] * cf[start : start + rows, :]
            sg = sigmoid(total)
            conv_low[:, at] = (total * sg).astype(BF16)
            slope[:, at] = sg * (1.0 + total * (1.0 - sg))

    def columns(i):
        q = g_in.order[i]
        t0 = (cph * q) // LANES
        lo = (cph * q + LANES - 1) // LANES
        hi = jnp.where(q == n_h - 1, WIDE // LANES, (cph * (q + 1)) // LANES)

        def tile_body(t, _):
            at = pl.ds(pl.multiple_of((t - t0) * LANES, LANES), LANES)
            project(t, full[q, :, :, at].reshape(dp, LANES))
            return 0

        lax.fori_loop(lo, hi, tile_body, 0)

    for step in g_in.plan(columns):
        step()
    g_out.begin()
    for q in range(1, n_h):
        if (cph * q) % LANES:
            tile, t0 = (cph * q) // LANES, (cph * (q - 1)) // LANES
            at = (tile - t0) * LANES
            project(tile, (full[q - 1, :, :, at : at + LANES] + full[q, :, :, 0:LANES]).reshape(dp, LANES))
    for n, (src, dst) in enumerate(((w_full, w_full_o), (conv_in, conv_in_o), (conv_low, conv_low_o), (slope, slope_o))):
        leaving.append(leave(src, dst, n + 1))
        leaving[-1].start()

    biased = raw[...] + heads[0:1, :]
    soft = jnp.maximum(biased, 0.0) + jnp.log1p(jnp.exp(-jnp.abs(biased)))
    keep = jnp.logical_and(iota((rows, LANES), 0) < left, iota((rows, LANES), 1) < HEADS)
    steps[...] = jnp.where(keep, soft, 0.0)
    rates = -jnp.exp(heads[1:2, :])
    for b in range(blocks):
        at = slice(b * SPAN, (b + 1) * SPAN)
        st = steps[at, :]
        incl, excl, total = head_terms(st, rates)
        incl_r[b] = incl
        excl_r[b] = excl
        incl_t[b] = incl.T
        excl_t[b] = excl.T
        steps_t[b] = st.T
        wide = split(jnp.concatenate([jnp.exp(total - incl) * st, jnp.exp(excl) * st], axis=0))
        bc = conv_low[at, INNER:].astype(F32)
        bt = bc.T[:STATE].astype(BF16)
        bt2 = jnp.concatenate([bt, bt], axis=1)
        c_low = half_masks(pltpu.roll(bc, STATE, 1))[0].astype(BF16)
        inter_s[b] = nt(c_low, bc.astype(BF16))
        tot = jnp.broadcast_to(jnp.exp(total), (8, LANES))
        for g in range(INNER // 256):
            cols = slice(g * 256, (g + 1) * 256)
            sp = spread[:, cols]
            xs = conv_low[at, cols].astype(F32)
            w = nn(wide[0], sp) + nn(wide[1], sp)
            for n, dst in ((0, hst), (1, gst)):
                hi, lo = split(w[n * SPAN : (n + 1) * SPAN] * xs)
                dst[b, :, cols] = nn(bt2, jnp.concatenate([hi, lo], axis=0))
            decb[b, :, cols] = expand(tot, sp)
    hv, gv, dv = hst[0], gst[blocks - 1], decb[0]
    for b in range(1, blocks):
        hv = hv * decb[b, 0:1, :] + hst[b]
        dv = dv * decb[b]
    for b in range(blocks - 2, -1, -1):
        gv = gv * decb[b, 0:1, :] + gst[b]
    dev[0] = hv
    dev[1] = gv
    dec[...] = dv
    chain = Chain(n_h, s, h, dev, dec, into, csnd, us, ur, dws, dwr)
    chain.begin()

    row = iota((SPAN, SPAN), 0)
    col = iota((SPAN, SPAN), 1)
    twice = 1.0 + (row == col).astype(F32)
    skip8 = jnp.broadcast_to(heads[2:3, :], (8, LANES))

    def pair_body(pair, _):
        cols = pl.ds(pl.multiple_of(pair * LANES, LANES), LANES)
        after = row >= col
        hot = (iota((LANES, 2 * LANES), 0) == 2 * pair + iota((LANES, 2 * LANES), 1) // LANES).astype(BF16)
        hot3 = jnp.concatenate([hot, hot, hot], axis=0)
        skip = expand(skip8, spread[:, cols])[0:1]
        for b in range(blocks):
            at = slice(b * SPAN, (b + 1) * SPAN)
            both = jnp.concatenate([incl_r[b], excl_r[b]], axis=0)
            wide = nn(jnp.concatenate(split3(both), axis=1), hot3)
            inter = inter_s[b] * twice
            xs = conv_low[at, cols]
            mix = []
            for n in range(2):
                hd = 2 * pair + n
                lanes = slice(n * LANES, (n + 1) * LANES)
                gap = jnp.where(
                    after,
                    wide[0:SPAN, lanes] - incl_t[b, pl.ds(hd, 1), :],
                    excl_t[b, pl.ds(hd, 1), :] - wide[SPAN:, lanes],
                )
                mix.append(inter * jnp.exp(gap) * steps_t[b, pl.ds(hd, 1), :])
            x0, x1 = half_masks(xs)
            y = nn_split(jnp.concatenate(mix, axis=1), jnp.concatenate([x0, x1], axis=0))
            yb[at, cols] = y + skip * xs.astype(F32)
        chain.at(pair)
        for n, step in enumerate(out_plan):
            pl.when(pair == n * 12 // len(out_plan))(step)
        return 0

    out_plan = g_out.plan(lambda i: None)
    lax.fori_loop(0, HEADS // 2, pair_body, 0)
    for k in range(HEADS // 2, chain.steps()):
        chain.at(k)

    for tile in range(INNER // LANES):
        parts = []
        for q in range(n_h):
            t0, t1 = tiles_of(oph, q)
            if t0 <= tile < t1:
                at = wi + (tile - t0) * LANES
                parts.append(full[q, :, :, at : at + LANES])
        v = parts[0] if len(parts) == 1 else parts[0] + parts[1]
        o_full[:, tile * LANES : (tile + 1) * LANES] = v.reshape(dp, LANES)

    hin[0] = into[0]
    gin[blocks] = into[1]
    for b in range(blocks):
        hin[b + 1] = hin[b] * decb[b, 0:1, :] + hst[b]
    for b in range(blocks - 1, -1, -1):
        gin[b] = gin[b + 1] * decb[b, 0:1, :] + gst[b]
    for src, dst, n in ((hin, hin_o, 5), (gin, gin_o, 6)):
        leaving.append(leave(src, dst, n))
        leaving[-1].start()
    keep_row = (iota((rows, 1), 0) < left).astype(F32)
    bgrad = (cot[...].astype(F32) * keep_row).astype(BF16)
    for g in range(INNER // 256):
        cols = slice(g * 256, (g + 1) * 256)
        sp = spread[:, cols]
        gg_scr[:, cols] = nn(bgrad, o_full[:, cols])
        for b in range(blocks):
            at = slice(b * SPAN, (b + 1) * SPAN)
            incl = incl_r[b]
            hi, lo = split(jnp.concatenate([jnp.exp(incl), jnp.exp(incl[SPAN - 1 : SPAN] - excl_r[b])], axis=0))
            wide = nn(hi, sp) + nn(lo, sp)
            el[at, cols] = wide[0:SPAN]
            eg[at, cols] = wide[SPAN:]
            cc = pltpu.roll(conv_low[at, INNER:].astype(F32), STATE, 1)[:, :STATE].astype(BF16)
            cc2 = jnp.concatenate([cc, cc], axis=1)
            yf = nn(cc2, jnp.concatenate(split(hin[b, :, cols]), axis=0))
            yg = nn(cc2, jnp.concatenate(split(gin[b + 1, :, cols]), axis=0))
            yb[at, cols] += wide[0:SPAN] * yf + wide[SPAN:] * yg
    dgain[...] = jnp.zeros_like(dgain)

    def gate_body(i, _):
        at = pl.ds(pl.multiple_of(i * 16, 16), 16)
        z = gate[at, :].astype(F32)
        hv = yb[at, :].astype(BF16).astype(F32)
        sg = sigmoid(z)
        sl = z * sg
        gated = hv * sl
        r = lax.rsqrt(jnp.mean(gated * gated, axis=1, keepdims=True) + EPS)
        unit = gated * r
        glow[at, :] = (unit * out_gain[...]).astype(BF16)
        gr = gg_scr[at, :]
        prod = gr * unit
        dgain[...] += prod[0:8] + prod[8:16]
        gg = gr * out_gain[...]
        dg = r * (gg - unit * jnp.mean(gg * unit, axis=1, keepdims=True))
        hgrad[at, :] = (dg * sl).astype(BF16)
        dgate[at, :] = (dg * hv * (sg * (1.0 + z * (1.0 - sg)))).astype(BF16)
        return 0

    lax.fori_loop(0, rows // 16, gate_body, 0)
    for g in range(dp // 256):
        cols = slice(g * 256, (g + 1) * 256)
        branch = nt(glow[...], o_full[cols, :])
        result[:, cols] = (x[:, cols].astype(F32) + keep_row * branch).astype(BF16)

    def state_body(b, _):
        at = pl.ds(pl.multiple_of(b * SPAN, SPAN), SPAN)
        ct = conv_low[at, INNER:].astype(F32).T[STATE:].astype(BF16)
        ct2 = jnp.concatenate([ct, ct], axis=1)
        for g in range(INNER // 256):
            cols = slice(g * 256, (g + 1) * 256)
            dy = hgrad[at, cols].astype(F32)
            for scale, dst in ((el, lst), (eg, mst)):
                hi, lo = split(scale[at, cols] * dy)
                dst[b, :, cols] = nn(ct2, jnp.concatenate([hi, lo], axis=0))
        return 0

    lax.fori_loop(0, blocks, state_body, 0)
    mv, lv = mst[0], lst[blocks - 1]
    for b in range(1, blocks):
        mv = mv * decb[b, 0:1, :] + mst[b]
    for b in range(blocks - 2, -1, -1):
        lv = lv * decb[b, 0:1, :] + lst[b]
    dev2[0] = mv
    dev2[1] = lv
    chain.finish()

    @pl.when(h < n_h - 1)
    def _():
        halo.wait_send()

    g_in.finish()
    g_out.finish()
    for c in leaving:
        c.wait()


def fore(n_s, n_h, rp, *args):
    x, _, w_in, w_out_t = args[:4]
    rin, cph = w_in.shape
    oph = w_out_t.shape[1]
    rows, dp = x.shape
    blocks = rows // SPAN
    wi = tile_count(cph, n_h) * LANES
    wo = tile_count(oph, n_h) * LANES
    dma = pltpu.SemaphoreType.DMA
    vm = pl.BlockSpec(memory_space=pltpu.VMEM)
    sm = pl.BlockSpec(memory_space=pltpu.SMEM)
    hbm = pl.BlockSpec(memory_space=pl.ANY)
    sds = jax.ShapeDtypeStruct
    vf = lambda *shape: pltpu.VMEM(shape, F32)
    vb = lambda *shape: pltpu.VMEM(shape, BF16)
    tables = vf(blocks, SPAN, LANES)
    act = sds((rows, INNER), BF16)
    states = sds((blocks, STATE, INNER), F32)
    entries = sds((blocks + 1, STATE, INNER), F32)
    outs = [
        (sds((rows, dp), BF16), vm),
        (sds((dp, WIDE), BF16), hbm),
        (sds((rows, dp), BF16), hbm),
        (sds((rows + HALO, CONV_CH), BF16), hbm),
        (sds((rows, CONV_CH), BF16), hbm),
        (sds((rows, CONV_CH), F32), hbm),
        (sds((rows, LANES), F32), vm),
        (sds((rows, LANES), F32), vm),
        (sds((blocks, 8, INNER), F32), vm),
        (sds((8, INNER), F32), vm),
        (act, vm),
        (act, vm),
        (act, vm),
        (sds((8, INNER), F32), vm),
        (states, vm),
        (states, vm),
        (sds((2, STATE, INNER), F32), vm),
        (entries, hbm),
        (entries, hbm),
    ]
    return pl.pallas_call(
        functools.partial(fore_kernel, n_s, n_h, cph, oph, rin, rp, wi, wo),
        out_shape=tuple(o for o, _ in outs),
        in_specs=[vm, vm, vm, vm, vm, sm],
        out_specs=tuple(p for _, p in outs),
        scratch_shapes=[
            vb(n_h, n_s, rp, wi + wo),
            vb(dp, WIDE),
            vb(dp, INNER),
            vb(HALO, dp),
            vf(rp, wi),
            vf(rp, wo),
            vb(rows + HALO, dp),
            vb(rows + HALO, CONV_CH),
            vb(rows, CONV_CH),
            vf(rows, CONV_CH),
            vf(rows + HALO, LANES),
            vb(rows, INNER),
            vf(blocks, STATE, INNER),
            vf(blocks, STATE, INNER),
            vf(2, STATE, INNER),
            vf(2, STATE, INNER),
            vf(2, STATE, INNER),
            tables, tables, tables, tables, tables, tables,
            vf(rows, INNER),
            vf(rows, INNER),
            vf(rows, INNER),
            vf(rows, INNER),
            vf(blocks + 1, STATE, INNER),
            vf(blocks + 1, STATE, INNER),
            vf(FLAT_ROWS, LANES),
            vf(1, dp),
            vf(8, CONV_CH),
            vf(8, LANES),
            vf(1, INNER),
            vb(LANES, INNER),
            dma((1,)),
            dma((1,)),
        ]
        + [dma((CHAIN_PARTS,))] * 4
        + [dma((7,))]
        + gather_sems(n_s, n_h) * 2,
        compiler_params=pltpu.CompilerParams(
            collective_id=1, has_side_effects=True, vmem_limit_bytes=FORE_VMEM
        ),
        name="fore",
    )(*args)


FORE_VMEM = 63 << 20
SMALL = 10696
FLAT_ROWS = 88
TAPS_ROWS = CONV_CH // LANES
HEAD_ROW = D // LANES + (CONV + 1) * TAPS_ROWS


CHUNK = 256
OUT_CHUNK = 384
N_IN = WIDE // CHUNK
N_OUT = INNER // OUT_CHUNK
X_CHUNK = INNER // CHUNK
SLOTS = 4
THIRD = 6
HOP = 2


def rear_kernel(
    n_s, n_h, cph, oph, rin, rp, in_slots,
    x, cot, flat, lengths, w_full_i, nlow, dgate_i, glow, conv_low, hgrad, steps, raw, slope_i, conv_in_i,
    hin_i, gin_i, lst_i, mst_i, dev, decb, dec, ogp, w_in, w_out_t, row_in, col_in, row_out, col_out, second_i,
    grad_x, grad_in, row_in_new, col_in_new, w_in_new, grad_out, row_out_new, col_out_new, w_out_new, small, second_new,
    params_new,
    w_full, slope, conv_in, hin, gin, lst, mst, prm, sec_rows, gain, taps, heads, spread,
    adj, csnd, nt_p, bt_p, pg, ng, dpre, halo, dfs, cfs, incl_r, excl_r, incl_t, excl_t, q_t, at_f, at_g, back_f, back_g,
    red, cross, dbc, dheads, dtaps, ngain, inter_s,
    sb, r0, vs, pbi, r1i, acci, r2i, pbo, r1o, acco, r2o, win,
    sz, spl, z1, p1, z2, p2, line,
    us, ur, ds, dr, hs, hr, s0s, s0r, s1s, s1r, s2s, s2r, o0s, o0r, o1s, o1r, o2s, o2r,
    load, szs, szr, sps, spr, z1s, z1r, p1s, p1r, z2s, z2r, p2s, p2r,
):
    s = lax.axis_index("seq")
    h = lax.axis_index("head")
    n_c = n_s // 2
    rows = x.shape[0]
    dp = x.shape[1]
    half = n_c * rp
    blocks = rows // SPAN
    chip = s // 2
    core = lax.rem(s, 2)
    sib = chip * 2 + (1 - core)
    up = lax.rem(h + 1, n_h)
    down = lax.rem(h + n_h - 1, n_h)
    zpeer = [lax.rem(h + j, n_h) for j in range(1, n_h)]
    cpeer = [lax.rem(chip + j, n_c) for j in range(1, n_c)]
    speer = [lax.rem(s + j, n_s) for j in range(1, n_s)]
    bar = pltpu.get_barrier_semaphore()
    for z in zpeer:
        pl.semaphore_signal(bar, inc=1, device_id=(s, z), device_id_type=MESH)
    for p in speer:
        pl.semaphore_signal(bar, inc=1, device_id=(p, h), device_id_type=MESH)
    pl.semaphore_wait(bar, n_h + n_s - 2)

    chain = Chain(n_h, s, h, dev, dec, adj, csnd, us, ur, ds, dr)
    chain.begin()
    pairs_of = (
        (dgate_i, pg.at[:, 0:INNER]), (w_full_i, w_full), (slope_i, slope), (hin_i, hin), (gin_i, gin), (lst_i, lst), (mst_i, mst),
        (conv_in_i, conv_in),
    )
    loads = [pltpu.make_async_copy(src, dst, load.at[n]) for n, (src, dst) in enumerate(pairs_of)]
    for c in loads:
        c.start()
    left = lengths[0] - h * rows

    def over_in(i):
        own = pl.ds(0, CHUNK)
        return remote(
            sb.at[lax.rem(i, 2), :, own], r0.at[lax.rem(i, SLOTS), :, own], s0s.at[i], s0r.at[i], (sib, h)
        )

    def over_out(i):
        return remote(sb.at[lax.rem(i, 2)], r0.at[lax.rem(i, SLOTS)], o0s.at[i], o0r.at[i], (sib, h))

    def first_in(i):
        @pl.when(i >= 2)
        def _():
            over_in(i - 2).wait_send()

        @pl.when(i < 2)
        def _():
            over_out(i + N_OUT - 2).wait_send()

        cols = pl.ds(pl.multiple_of(i * CHUNK, CHUNK), CHUNK)
        part = pg[:, cols]
        sb[lax.rem(i, 2), :, 0:CHUNK] = nn(nt_p[1 - core], part)
        over_in(i).start()
        ng[...] += nt(part, w_full[:, cols])

    def second_in(i):
        cols = pl.ds(pl.multiple_of(i * CHUNK, CHUNK), CHUNK)
        mine = nn(nt_p[core], pg[:, cols])
        over_in(i).wait_recv()
        vs[:, :, 0:CHUNK] = (mine + r0[lax.rem(i, SLOTS), :, 0:CHUNK]).reshape(n_c, rp, CHUNK)
        for j, k in enumerate(cpeer):
            pbi[i, j] = vs[k, :, 0:CHUNK].astype(BF16)
            remote(pbi.at[i, j], r1i.at[i, chip], s1s.at[i, j], s1r.at[i, chip], (2 * k + core, h)).start()
        acci[i] = vs[chip, :, 0:CHUNK]

    def owners(i, wide, per):
        one = (wide * i) // per
        two = (wide * i + wide - 1) // per
        return one, jnp.minimum(two, n_h - 1)

    def third_in(i):
        total = acci[i]
        for j, k in enumerate(cpeer):
            remote(pbi.at[i, j], r1i.at[i, k], s1s.at[i, j], s1r.at[i, k], (2 * k + core, h)).wait_recv()
            total = total + r1i[i, k].astype(F32)
        acci[i] = total

    def links(i, wide, per, acc, rec, snd, rcv):
        one, two = owners(i, wide, per)
        for n, q, real in ((0, one, None), (1, two, two != one))[: rec.shape[1]]:
            for way, to in ((0, up), (1, down)):
                sends_it = h < q if way == 0 else h > q
                if real is not None:
                    sends_it = jnp.logical_and(real, sends_it)
                begins = h == 0 if way == 0 else h == n_h - 1
                dst = rec.at[i, n, way]
                make = lambda src, n=n, way=way, to=to, dst=dst: remote(
                    src, dst, snd.at[i, n, way], rcv.at[i, n, way], (s, to)
                )
                yield way, sends_it, begins, make, n

    def along(i, way, *stream):
        acc, rec = stream[2], stream[3]
        for w, sends_it, begins, make, n in links(i, *stream):
            if w != way:
                continue

            @pl.when(jnp.logical_and(sends_it, begins))
            def _():
                make(acc.at[i]).start()

            @pl.when(jnp.logical_and(sends_it, jnp.logical_not(begins)))
            def _():
                make(acc.at[i]).wait_recv()
                rec[i, n, way] += acc[i]
                make(rec.at[i, n, way]).start()

    def drain_z(i, *stream):
        for _, sends_it, _, make, n in links(i, *stream):

            @pl.when(sends_it)
            def _():
                make(stream[2].at[i]).wait_send()

    in_stream = (CHUNK, cph, acci, r2i, s2s, s2r)
    out_stream = (OUT_CHUNK, oph, acco, r2o, o2s, o2r)

    def drain_in(i):
        for j, k in enumerate(cpeer):
            remote(pbi.at[i, j], r1i.at[i, chip], s1s.at[i, j], s1r.at[i, chip], (2 * k + core, h)).wait_send()
        drain_z(i, *in_stream)

    def first_out(i):
        @pl.when(i >= 2)
        def _():
            over_out(i - 2).wait_send()

        cols = pl.ds(pl.multiple_of(i * OUT_CHUNK, LANES), OUT_CHUNK)
        sb[lax.rem(i, 2)] = nn(bt_p[1 - core], glow[:, cols])
        over_out(i).start()

    def second_out(i):
        cols = pl.ds(pl.multiple_of(i * OUT_CHUNK, LANES), OUT_CHUNK)
        mine = nn(bt_p[core], glow[:, cols])
        over_out(i).wait_recv()
        vs[...] = (mine + r0[lax.rem(i, SLOTS)]).reshape(n_c, rp, OUT_CHUNK)
        for j, k in enumerate(cpeer):
            pbo[i, j] = vs[k].astype(BF16)
            remote(pbo.at[i, j], r1o.at[i, chip], o1s.at[i, j], o1r.at[i, chip], (2 * k + core, h)).start()
        acco[i] = vs[chip]

    def third_out(i):
        total = acco[i]
        for j, k in enumerate(cpeer):
            remote(pbo.at[i, j], r1o.at[i, k], o1s.at[i, j], o1r.at[i, k], (2 * k + core, h)).wait_recv()
            total = total + r1o[i, k].astype(F32)
        acco[i] = total

    def drain_out(i):
        for j, k in enumerate(cpeer):
            remote(pbo.at[i, j], r1o.at[i, chip], o1s.at[i, j], o1r.at[i, chip], (2 * k + core, h)).wait_send()
        drain_z(i, *out_stream)

    def among(k, first, count):
        return jnp.logical_and(k >= first, k < first + count)

    def stage_at(k):
        @pl.when(k < N_OUT)
        def _():
            first_out(k)

        @pl.when(jnp.logical_and(k >= N_OUT, k < N_OUT + N_IN))
        def _():
            first_in(k - N_OUT)

        @pl.when(jnp.logical_and(k >= 1, k < N_OUT + 1))
        def _():
            second_out(k - 1)

        @pl.when(jnp.logical_and(k >= N_OUT + 1, k < N_OUT + N_IN + 1))
        def _():
            second_in(k - 1 - N_OUT)

        @pl.when(among(k, THIRD, N_OUT))
        def _():
            third_out(k - THIRD)

        @pl.when(among(k, N_OUT + THIRD, N_IN))
        def _():
            third_in(k - THIRD - N_OUT)

        for way, lag in ((0, THIRD + HOP * h), (1, THIRD + HOP * (n_h - 1 - h))):

            @pl.when(among(k, lag, N_OUT))
            def _():
                along(k - lag, way, *out_stream)

            @pl.when(among(k, N_OUT + lag, N_IN))
            def _():
                along(k - lag - N_OUT, way, *in_stream)

    last_stage = N_OUT + N_IN - 1 + THIRD + HOP * (n_h - 2)

    keep_row = (iota((rows, 1), 0) < left).astype(F32)
    for src, dst in ((nlow[...], nt_p), ((cot[...].astype(F32) * keep_row).astype(BF16), bt_p)):
        turned = src.T
        for q in range(n_s):
            dst[q % 2, (q // 2) * rp : (q // 2 + 1) * rp, :] = turned[q * rp : (q + 1) * rp]
    flat_rows(flat, prm, 0.0)
    flat_rows(second_i, sec_rows, 1.0)
    unpack_rows(prm, rin, rp, gain, taps, heads, None)
    fill_spread(spread)
    ng[...] = jnp.zeros_like(ng)
    dheads[...] = jnp.zeros_like(dheads)
    dtaps[...] = jnp.zeros_like(dtaps)
    rates = -jnp.exp(heads[1:2, :])
    row = iota((SPAN, SPAN), 0)
    col = iota((SPAN, SPAN), 1)
    twice = 1.0 + (row == col).astype(F32)
    for ref in (q_t, at_f, at_g, back_f, back_g, red, cross, dbc):
        ref[...] = jnp.zeros_like(ref)
    for b in range(blocks):
        at = slice(b * SPAN, (b + 1) * SPAN)
        incl, excl, total = head_terms(steps[at, :], rates)
        incl_r[b] = incl
        excl_r[b] = excl
        incl_t[b] = incl.T
        excl_t[b] = excl.T
        bc = conv_low[at, INNER:].astype(F32)
        cb = pltpu.roll(bc, STATE, 1)
        inter_s[b] = nt(half_masks(bc)[0].astype(BF16), cb.astype(BF16))

    def pair_body(pair, _):
        cols = pl.ds(pl.multiple_of(pair * LANES, LANES), LANES)
        sp = spread[:, cols]
        later = col >= row
        hot = (iota((LANES, 2 * LANES), 0) == 2 * pair + iota((LANES, 2 * LANES), 1) // LANES).astype(BF16)
        hot3 = jnp.concatenate([hot, hot, hot], axis=0)
        for b in range(blocks):
            at = slice(b * SPAN, (b + 1) * SPAN)
            both = jnp.concatenate([incl_r[b], excl_r[b]], axis=0)
            wide = nn(jnp.concatenate(split3(both), axis=1), hot3)
            inter = inter_s[b]
            inter2 = inter * twice
            hi, lo = split(steps[at, :])
            xs = conv_low[at, cols].astype(F32)
            dyl = hgrad[at, cols]
            xh, xl = split((nn(hi, sp) + nn(lo, sp)) * xs)
            xhs = half_masks(xh)
            xls = half_masks(xl)
            dy2 = jnp.concatenate([dyl, dyl], axis=1)
            kern = []
            qt = q_t[b]
            for n in range(2):
                hd = 2 * pair + n
                lanes = slice(n * LANES, (n + 1) * LANES)
                gap = jnp.where(
                    later,
                    incl_t[b, pl.ds(hd, 1), :] - wide[0:SPAN, lanes],
                    wide[SPAN:, lanes] - excl_t[b, pl.ds(hd, 1), :],
                )
                decay = jnp.exp(gap)
                kern.append(inter2 * decay)
                weigh = nt(jnp.concatenate([xhs[n], xls[n]], axis=1), dy2) * decay
                qt = qt + weigh * twice
                pairs = weigh * inter
                above = jnp.where(col > row, pairs, 0.0)
                below = jnp.where(col < row, pairs, 0.0)
                at_f[b, pl.ds(hd, 1), :] = jnp.sum(above, axis=0, keepdims=True)
                at_g[b, pl.ds(hd, 1), :] = jnp.sum(below, axis=0, keepdims=True)
                here = iota((SPAN, LANES), 1) == hd
                back_f[b] = jnp.where(here, jnp.sum(above, axis=1, keepdims=True), back_f[b])
                back_g[b] = jnp.where(here, jnp.sum(below, axis=1, keepdims=True), back_g[b])
            q_t[b] = qt
            dys = half_masks(dyl)
            dpre[at, cols] = nn_split(jnp.concatenate(kern, axis=1), jnp.concatenate(dys, axis=0))
        chain.at(pair)

        @pl.when(pair < N_OUT + X_CHUNK)
        def _():
            stage_at(pair)

        return 0

    pairs_n = HEADS // 2
    for c in loads[:2]:
        c.wait()
    lax.fori_loop(0, pairs_n, pair_body, 0)
    for k in range(pairs_n, chain.steps()):
        chain.at(k)
    for c in loads[2:]:
        c.wait()

    @pl.when(h == n_h - 1)
    def _():
        halo[...] = jnp.zeros_like(halo)

    def halo_copy(g, size):
        cols = pl.ds(pl.multiple_of(g * CHUNK, CHUNK), size)
        return remote(dpre.at[0:8, cols], halo.at[:, cols], hs.at[g], hr.at[g], (s, down))

    def halo_send(g, size):
        @pl.when(h > 0)
        def _():
            halo_copy(g, size).start()

    def conv_back(g, size):
        cols = pl.ds(pl.multiple_of(g * CHUNK, CHUNK), size)
        own = slice(0, size)
        dp_ = dpre[:, cols]
        dfs[0:rows, own] = dp_
        cfs[:, own] = conv_in[:, cols].astype(F32)
        for k in range(CONV):
            first = HALO - CONV + 1 + k
            dtaps[k : k + 1, cols] = jnp.sum(dp_ * cfs[first : first + rows, own], axis=0, keepdims=True)
        dtaps[CONV : CONV + 1, cols] = jnp.sum(dp_, axis=0, keepdims=True)

        @pl.when(h < n_h - 1)
        def _():
            halo_copy(g, size).wait_recv()

        dfs[rows : rows + 8, own] = halo[:, cols]
        total = jnp.zeros((rows, size), F32)
        for k in range(CONV):
            first = CONV - 1 - k
            total = total + taps[k : k + 1, cols] * dfs[first : first + rows, own]
        pg[:, pl.ds(pl.multiple_of(INNER + g * CHUNK, CHUNK), size)] = total.astype(BF16)

    skip8 = jnp.broadcast_to(heads[2:3, :], (8, LANES))

    def group_compute(g):
        cols = pl.ds(pl.multiple_of(g * CHUNK, CHUNK), CHUNK)
        sp = spread[:, cols]
        skip = expand(skip8, sp)[0:1]
        ms, ls = [adj[0, :, cols]], [adj[1, :, cols]]
        for b in range(blocks - 1):
            ms.append(ms[-1] * decb[b, 0:1, cols] + mst[b, :, cols])
        for b in range(blocks - 1, 0, -1):
            ls.insert(0, ls[0] * decb[b, 0:1, cols] + lst[b, :, cols])
        zero_state = jnp.zeros((STATE, CHUNK), BF16)
        for b in range(blocks):
            at = slice(b * SPAN, (b + 1) * SPAN)
            incl, excl = incl_r[b], excl_r[b]
            total = incl[SPAN - 1 : SPAN]
            st = steps[at, :]
            terms = jnp.concatenate(
                [st, jnp.exp(incl), jnp.exp(total - excl), jnp.exp(total - incl), jnp.exp(excl)], axis=0
            )
            hi, lo = split(terms)
            wide = nn(hi, sp) + nn(lo, sp)
            st_e, el, eg, tl, ex = [wide[n * SPAN : (n + 1) * SPAN] for n in range(5)]
            bc = conv_low[at, INNER:].astype(F32)
            cb = pltpu.roll(bc, STATE, 1)
            bb = bc[:, :STATE].astype(BF16)
            cc = cb[:, :STATE].astype(BF16)
            bb2 = jnp.concatenate([bb, bb], axis=1)
            cc2 = jnp.concatenate([cc, cc], axis=1)
            xs = conv_low[at, cols].astype(F32)
            dy = hgrad[at, cols].astype(F32)
            xst = st_e * xs
            parts = [split(v) for v in (hin[b, :, cols], gin[b + 1, :, cols], ls[b], ms[b])]
            into_f = el * nn(cc2, jnp.concatenate(parts[0], axis=0))
            into_g = eg * nn(cc2, jnp.concatenate(parts[1], axis=0))
            out_f = tl * nn(bb2, jnp.concatenate(parts[2], axis=0))
            out_g = ex * nn(bb2, jnp.concatenate(parts[3], axis=0))
            dxu = dpre[at, cols] + out_f + out_g
            dpre[at, cols] = (st_e * dxu + skip * dy) * slope[at, cols]
            stack = jnp.concatenate([dy * into_f - xst * out_f, dy * into_g - xst * out_g, xs * dxu, xs * dy], axis=0)
            red[b] += fold(stack, sp)
            pair_f = jnp.sum(ls[b] * hin[b + 1, :, cols], axis=0, keepdims=True)
            pair_g = jnp.sum(ms[b] * gin[b, :, cols], axis=0, keepdims=True)
            cross[b] += fold(jnp.broadcast_to(pair_f + pair_g, (8, CHUNK)), sp)
            lefts, rights = [], []
            for scaled, (sh, sl), low in (
                (xst * tl, parts[2], True),
                (xst * ex, parts[3], True),
                (el * dy, parts[0], False),
                (eg * dy, parts[1], False),
            ):
                ah, al = split(scaled)
                for a, v in ((ah, sh), (al, sh), (ah, sl)):
                    lefts.append(a)
                    rights.append(jnp.concatenate([v, zero_state] if low else [zero_state, v], axis=0))
            dbc[b] += nt(jnp.concatenate(lefts, axis=1), jnp.concatenate(rights, axis=1))

    def group_body(g, _):
        group_compute(g)
        halo_send(g, CHUNK)

        @pl.when(g >= 1)
        def _():
            conv_back(g - 1, CHUNK)
            stage_at(N_OUT + X_CHUNK + g - 1)

        return 0

    lax.fori_loop(0, X_CHUNK, group_body, 0)

    for b in range(blocks):
        at = slice(b * SPAN, (b + 1) * SPAN)
        bc = conv_low[at, INNER:].astype(F32)
        cb_lo, cb_hi = half_masks(pltpu.roll(bc, STATE, 1))
        qt = q_t[b]
        d = dbc[b] + nn_split(qt, cb_lo.astype(BF16)) + nn_split(qt.T, cb_hi.astype(BF16))
        dpre[at, INNER:] = d * slope[at, INNER:]
    halo_send(X_CHUNK, LANES)
    conv_back(X_CHUNK - 1, CHUNK)
    stage_at(N_OUT + 2 * X_CHUNK - 1)
    for b in range(blocks):
        at = slice(b * SPAN, (b + 1) * SPAN)
        st = steps[at, :]
        rd = red[b]
        v_f = rd[0:SPAN] + at_f[b].T - back_f[b]
        v_g = rd[SPAN : 2 * SPAN] + at_g[b].T - back_g[b]
        da = precise(tri_high(), v_f) + precise(tri_low(), v_g) + cross[b, 0:1]
        dstep = rd[2 * SPAN : 3 * SPAN] + da * rates
        keep = jnp.logical_and(iota((SPAN, LANES), 0) + b * SPAN < left, iota((SPAN, LANES), 1) < HEADS)
        draw = jnp.where(keep, dstep * sigmoid(raw[at, :] + heads[0:1, :]), 0.0)
        pg[at, INNER + CONV_CH :] = draw.astype(BF16)
        dheads[0:1, :] += jnp.sum(draw, axis=0, keepdims=True)
        dheads[1:2, :] += jnp.sum(da * st, axis=0, keepdims=True) * rates
        dheads[2:3, :] += jnp.sum(rd[3 * SPAN :], axis=0, keepdims=True)
    conv_back(X_CHUNK, LANES)
    stage_at(N_OUT + N_IN - 1)
    stage_at(N_OUT + N_IN)

    ngain[...] = jnp.zeros_like(ngain)

    def norm_body(i, _):
        at = pl.ds(pl.multiple_of(i * 16, 16), 16)
        v = x[at, :].astype(F32)
        r = lax.rsqrt(jnp.sum(v * v, axis=1, keepdims=True) * (1.0 / D) + EPS)
        unit = v * r
        g = ng[at, :]
        prod = g * unit
        ngain[...] += prod[0:8] + prod[8:16]
        gg = g * gain[...]
        mean = jnp.sum(gg * unit, axis=1, keepdims=True) * (1.0 / D)
        grad_x[at, :] = cot[at, :].astype(F32) + r * (gg - unit * mean)
        return 0

    lax.fori_loop(0, rows // 16, norm_body, 0)

    sends = []

    def start(buf, me, peers, along_z, snd, rcv):
        for j, p in enumerate(peers):
            c = remote(buf.at[me], buf.at[me], snd.at[j], rcv.at[me], (s, p) if along_z else (p, h))
            c.start()
            sends.append(c)

    def arrive(buf, peers, along_z, snd, rcv):
        for j, p in enumerate(peers):
            remote(buf.at[p], buf.at[p], snd.at[j], rcv.at[p], (s, p) if along_z else (p, h)).wait_recv()
        total = buf[0]
        for i in range(1, buf.shape[0]):
            total = total + buf[i]
        return total

    first = D // LANES
    gsum = ngain[...]
    if dp != D:
        gsum = sum(nn(p, piece_map(dp, rin, rp)) for p in split3(gsum))
    for i in range(first):
        sz[h, i : i + 1, :] = jnp.sum(gsum[:, i * LANES : (i + 1) * LANES], axis=0, keepdims=True)
    for k in range(CONV + 1):
        for i in range(TAPS_ROWS):
            t = first + k * TAPS_ROWS + i
            sz[h, t : t + 1, :] = dtaps[k : k + 1, i * LANES : (i + 1) * LANES]
    lane1 = iota((1, LANES), 1)
    turn = 3 * HEADS
    before = dheads[0:1, :]
    for n in range(1, 3):
        before = jnp.where(lane1 < n * HEADS, before, pltpu.roll(dheads[n : n + 1, :], n * HEADS, 1))
    for i in range(INNER // LANES):
        tile = jnp.sum(ogp[:, i * LANES : (i + 1) * LANES], axis=0, keepdims=True)
        tile = pltpu.roll(tile, turn, 1)
        sz[h, HEAD_ROW + i : HEAD_ROW + i + 1, :] = jnp.where(lane1 < turn, before, tile)
        before = tile
    t = HEAD_ROW + INNER // LANES
    sz[h, t : t + 1, :] = jnp.where(lane1 < turn, before, 0.0)
    sz[h, t + 1 :, :] = jnp.zeros((FLAT_ROWS - t - 1, LANES), F32)
    start(sz, h, zpeer, True, szs, szr)

    def stage_body(k, _):
        stage_at(k)
        return 0

    lax.fori_loop(N_OUT + N_IN + 1, last_stage + 1, stage_body, 0)

    def window(slots, dst, wide, per, acc, rec, snd, rcv):
        c0 = (per * h) // wide
        c1 = (per * (h + 1) + wide - 1) // wide
        for c in range(slots):
            index = jnp.minimum(c0 + c, acc.shape[0] - 1)
            at = slice(c * wide, (c + 1) * wide)
            dst[:, at] = acc[index]
            n = jnp.where(owners(index, wide, per)[0] == h, 0, 1) if rec.shape[1] > 1 else 0
            for way, there in ((0, h > 0), (1, h < n_h - 1)):

                @pl.when(jnp.logical_and(c0 + c < c1, there))
                def _():
                    remote(acc.at[index], rec.at[index, n, way], snd.at[0, 0, 0], rcv.at[index, n, way], (s, up)).wait_recv()
                    dst[:, at] += rec[index, n, way]

    wi = in_slots * CHUNK
    window(in_slots, win, *in_stream)
    g_in = pltpu.roll(win[...], lax.rem(wi - lax.rem(cph * h, CHUNK), wi), 1)[0:rin, :cph]
    window(1, win, *out_stream)
    g_out = win[0:rin, 0:OUT_CHUNK]
    if oph != OUT_CHUNK:
        g_out = pltpu.roll(g_out, lax.rem(OUT_CHUNK - lax.rem(oph * h, OUT_CHUNK), OUT_CHUNK), 1)[:, :oph]
    grad_in[...] = g_in
    grad_out[...] = g_out

    decay_keep = 1.0 - DECAY
    sq_in = g_in * g_in
    sq_out = g_out * g_out
    fill = jnp.zeros((LANES - rin, LANES), F32)
    line_in = jnp.concatenate(
        [jnp.broadcast_to(jnp.sum(sq_in, axis=1, keepdims=True), (rin, LANES)), fill], axis=0
    ).T[0:8]
    line_out = jnp.concatenate(
        [jnp.broadcast_to(jnp.sum(sq_out, axis=1, keepdims=True), (rin, LANES)), fill], axis=0
    ).T[0:8]
    z1[h] = jnp.where(iota((8, LANES), 0) == 0, line_in, line_out)
    start(z1, h, zpeer, True, z1s, z1r)
    cs_in = jnp.sum(sq_in, axis=0, keepdims=True)
    rs_out = jnp.sum(sq_out, axis=0, keepdims=True)
    n_ci = -(-cph // LANES)
    n_ro = -(-oph // LANES)
    line[...] = jnp.zeros_like(line)
    line[0:1, 0:cph] = cs_in
    line[0:1, n_ci * LANES : n_ci * LANES + oph] = rs_out
    p1[s] = jnp.zeros_like(p1[0])
    for i in range(n_ci + n_ro):
        p1[s, i : i + 1, :] = line[0:1, i * LANES : (i + 1) * LANES]
    start(p1, s, speer, False, p1s, p1r)
    spl[s] = arrive(sz, zpeer, True, szs, szr)
    start(spl, s, speer, False, sps, spr)
    sums = arrive(z1, zpeer, True, z1s, z1r)
    line_r = DECAY * row_in[...].reshape(1, rin) + decay_keep * (sums[0:1, 0:rin] / PROJ + EPS_SQUARE)
    line_c = DECAY * col_out[...].reshape(1, rin) + decay_keep * (sums[1:2, 0:rin] / INNER + EPS_SQUARE)
    row_in_new[...] = line_r.reshape(rin)
    col_out_new[...] = line_c.reshape(rin)
    fill_line = jnp.zeros((1, LANES - rin), F32)
    up_r = jnp.broadcast_to(jnp.concatenate([line_r, fill_line], axis=1), (LANES, LANES)).T[0:rin, 0:1]
    up_c = jnp.broadcast_to(jnp.concatenate([line_c, fill_line], axis=1), (LANES, LANES)).T[0:rin, 0:1]
    sums = arrive(p1, speer, False, p1s, p1r)
    for i in range(n_ci + n_ro):
        line[0:1, i * LANES : (i + 1) * LANES] = sums[i : i + 1]
    line_ci = DECAY * col_in[...].reshape(1, cph) + decay_keep * (line[0:1, 0:cph] / D + EPS_SQUARE)
    line_ro = DECAY * row_out[...].reshape(1, oph) + decay_keep * (
        line[0:1, n_ci * LANES : n_ci * LANES + oph] / D + EPS_SQUARE
    )
    col_in_new[...] = line_ci.reshape(cph)
    row_out_new[...] = line_ro.reshape(oph)
    u_in = g_in * lax.rsqrt(up_r * line_ci)
    u_out = g_out * lax.rsqrt(up_c * line_ro)
    lane = iota((8, LANES), 1)
    values = (
        jnp.sum(u_in * u_in, keepdims=True),
        jnp.sum(u_out * u_out, keepdims=True),
        jnp.sum(line_ro, axis=1, keepdims=True),
        jnp.sum(line_r, axis=1, keepdims=True) / n_h,
    )
    note = jnp.zeros((8, LANES), F32)
    for n, v in enumerate(values):
        note = jnp.where(lane == n, v, note)
    z2[h] = note
    start(z2, h, zpeer, True, z2s, z2r)

    g = arrive(spl, speer, False, sps, spr)
    sec = DECAY * sec_rows[...] + decay_keep * (g * g + EPS_SQUARE)
    u = g * lax.rsqrt(sec)
    spread_small = jnp.sqrt(jnp.sum(u * u, keepdims=True) / SMALL)
    par = prm[...] - LEARN_SMALL * u / jnp.maximum(1.0, spread_small / CLIP_RMS)

    p2[s] = arrive(z2, zpeer, True, z2s, z2r)
    start(p2, s, speer, False, p2s, p2r)
    mean_out = p2[s, 0:1, 2:3] / INNER
    whole, rest = SMALL // LANES, SMALL % LANES
    for v, dst in ((g, small), (sec, second_new), (par, params_new)):
        for i in range(whole):
            dst[pl.ds(i * LANES, LANES)] = v[i : i + 1].reshape(LANES)
        dst[pl.ds(whole * LANES, rest)] = v[whole : whole + 1, 0:rest].reshape(rest)

    chain.finish()

    @pl.when(h > 0)
    def _():
        for g in range(X_CHUNK):
            halo_copy(g, CHUNK).wait_send()
        halo_copy(X_CHUNK, LANES).wait_send()

    for i in (N_IN - 2, N_IN - 1):
        over_in(i).wait_send()

    def drain_body(i, _):
        drain_in(i)

        @pl.when(i < N_OUT)
        def _():
            drain_out(i)

        return 0

    lax.fori_loop(0, N_IN, drain_body, 0)
    sums = arrive(p2, speer, False, p2s, p2r)
    mean_in = sums[0:1, 3:4] / D
    clip_in = jnp.maximum(1.0, jnp.sqrt(sums[0:1, 0:1] * mean_in / (D * PROJ)) / CLIP_RMS)
    clip_out = jnp.maximum(1.0, jnp.sqrt(sums[0:1, 1:2] * mean_out / (INNER * D)) / CLIP_RMS)
    w_in_new[...] = w_in[...] - u_in * (LEARN_RATE * jnp.sqrt(mean_in) / clip_in)
    w_out_new[...] = w_out_t[...] - u_out * (LEARN_RATE * jnp.sqrt(mean_out) / clip_out)
    for c in sends:
        c.wait_send()


def rear(n_s, n_h, rp, *args):
    x = args[0]
    w_in, w_out_t = args[22], args[23]
    rin, cph = w_in.shape
    oph = w_out_t.shape[1]
    rows, dp = x.shape
    n_c = n_s // 2
    half = n_c * rp
    blocks = rows // SPAN
    in_slots = max(-(-cph * (q + 1) // CHUNK) - cph * q // CHUNK for q in range(n_h))
    out_dup = 1 if oph % OUT_CHUNK == 0 else 2
    n_line = -(-cph // LANES) + -(-oph // LANES)
    n_rows = -(-(n_line + 1) // 8) * 8
    dma = pltpu.SemaphoreType.DMA
    vm = pl.BlockSpec(memory_space=pltpu.VMEM)
    sm = pl.BlockSpec(memory_space=pltpu.SMEM)
    hbm = pl.BlockSpec(memory_space=pl.ANY)
    sds = jax.ShapeDtypeStruct
    vf = lambda *shape: pltpu.VMEM(shape, F32)
    vb = lambda *shape: pltpu.VMEM(shape, BF16)
    tables = vf(blocks, SPAN, LANES)
    specs = [vm] * len(args)
    specs[3] = sm
    for i in (4, 6, 12, 13, 14, 15, 16, 17):
        specs[i] = hbm
    return pl.pallas_call(
        functools.partial(rear_kernel, n_s, n_h, cph, oph, rin, rp, in_slots),
        out_shape=(
            sds((rows, dp), F32),
            sds((rin, cph), F32),
            sds((rin,), F32),
            sds((cph,), F32),
            sds((rin, cph), F32),
            sds((rin, oph), F32),
            sds((oph,), F32),
            sds((rin,), F32),
            sds((rin, oph), F32),
            sds((SMALL,), F32),
            sds((SMALL,), F32),
            sds((SMALL,), F32),
        ),
        in_specs=specs,
        out_specs=(vm,) * 12,
        scratch_shapes=[
            vb(dp, WIDE),
            vf(rows, CONV_CH),
            vb(rows + HALO, CONV_CH),
            vf(blocks + 1, STATE, INNER),
            vf(blocks + 1, STATE, INNER),
            vf(blocks, STATE, INNER),
            vf(blocks, STATE, INNER),
            vf(FLAT_ROWS, LANES),
            vf(FLAT_ROWS, LANES),
            vf(1, dp),
            vf(8, CONV_CH),
            vf(8, LANES),
            vb(LANES, INNER),
            vf(2, STATE, INNER),
            vf(2, STATE, INNER),
            vb(2, half, rows),
            vb(2, half, rows),
            vb(rows, WIDE),
            vf(rows, dp),
            vf(rows, CONV_CH),
            vf(8, CONV_CH),
            vf(rows + 8, CHUNK),
            vf(rows + HALO, CHUNK),
            tables, tables, tables, tables, tables, tables, tables, tables, tables,
            vf(blocks, 4 * SPAN, LANES),
            vf(blocks, 8, LANES),
            tables,
            vf(8, LANES),
            vf(8, CONV_CH),
            vf(8, dp),
            tables,
            vf(2, half, OUT_CHUNK),
            vf(SLOTS, half, OUT_CHUNK),
            vf(n_c, rp, OUT_CHUNK),
            vb(N_IN, n_c - 1, rp, CHUNK),
            vb(N_IN, n_c, rp, CHUNK),
            vf(N_IN, rp, CHUNK),
            vf(N_IN, 2, 2, rp, CHUNK),
            vb(N_OUT, n_c - 1, rp, OUT_CHUNK),
            vb(N_OUT, n_c, rp, OUT_CHUNK),
            vf(N_OUT, rp, OUT_CHUNK),
            vf(N_OUT, out_dup, 2, rp, OUT_CHUNK),
            vf(rp, in_slots * CHUNK),
            vf(n_h, FLAT_ROWS, LANES),
            vf(n_s, FLAT_ROWS, LANES),
            vf(n_h, 8, LANES),
            vf(n_s, n_rows, LANES),
            vf(n_h, 8, LANES),
            vf(n_s, 8, LANES),
            vf(8, n_line * LANES),
        ]
        + [dma((CHAIN_PARTS,))] * 4
        + [dma((X_CHUNK + 1,))] * 2
        + [dma((N_IN,)), dma((N_IN,)), dma((N_IN, n_c)), dma((N_IN, n_c)), dma((N_IN, 2, 2)), dma((N_IN, 2, 2))]
        + [dma((N_OUT,)), dma((N_OUT,)), dma((N_OUT, n_c)), dma((N_OUT, n_c)), dma((N_OUT, out_dup, 2)), dma((N_OUT, out_dup, 2))]
        + [dma((8,))]
        + [dma((n_h,)), dma((n_h,)), dma((n_s,)), dma((n_s,))] * 3,
        compiler_params=pltpu.CompilerParams(
            collective_id=2, has_side_effects=True, vmem_limit_bytes=REAR_VMEM
        ),
        name="rear",
    )(*args)


REAR_VMEM = 63 << 20


def on_device(
    x_in, lengths, cotangent, w_in, w_out, small_params, row_in, col_in, row_out, col_out, small_second
):
    n_s = lax.axis_size("seq")
    n_h = lax.axis_size("head")
    rin = w_in.shape[0]
    rp = -(-rin // 16) * 16
    dp = n_s * rp
    def pad(v, axis, fill=0):
        if rp == rin:
            return v
        shape = v.shape[:axis] + (n_s, rin) + v.shape[axis + 1 :]
        widths = [(0, 0)] * len(shape)
        widths[axis + 1] = (0, rp - rin)
        v = jnp.pad(v.reshape(shape), widths, constant_values=fill)
        return v.reshape(v.shape[:axis] + (dp,) + v.shape[axis + 2 :])

    def cut(v, axis):
        if rp == rin:
            return v
        shape = v.shape[:axis] + (n_s, rp) + v.shape[axis + 1 :]
        v = lax.slice_in_dim(v.reshape(shape), 0, rin, axis=axis + 1)
        return v.reshape(v.shape[:axis] + (D,) + v.shape[axis + 2 :])

    x = pad(x_in, 1)
    cot = pad(cotangent, 1)
    w_out_t = w_out.T
    (
        result, w_full, nlow, conv_in, conv_low, slope, raw, steps, decb, dec, dgate, hgrad, glow, og_part, lst, mst, dev2, hin,
        gin,
    ) = fore(n_s, n_h, rp, x, cot, w_in, w_out_t, small_params, lengths)
    (
        grad_x, grad_in, row_in_new, col_in_new, w_in_new, grad_out, row_out_new, col_out_new, w_out_new, small,
        second_new, params_new,
    ) = rear(
        n_s, n_h, rp,
        x, cot, small_params, lengths, w_full, nlow, dgate, glow, conv_low, hgrad, steps, raw, slope, conv_in, hin, gin, lst, mst,
        dev2, decb, dec, og_part, w_in, w_out_t, row_in, col_in, row_out, col_out, small_second,
    )
    return (
        cut(result, 1), cut(grad_x, 1), grad_in, row_in_new, col_in_new, w_in_new, grad_out.T, row_out_new, col_out_new,
        w_out_new.T, small, second_new, params_new,
    )


def solution(mesh):
    both = P(("seq", "head"), None)
    factors = (P("seq", "head"), P("seq"), P("head"), P("seq", "head"))
    return jax.shard_map(
        on_device,
        mesh=mesh,
        in_specs=(
            both, P("seq"), both, P("seq", "head"), P("head", "seq"), P(), P("seq"), P("head"), P("head"), P("seq"), P(),
        ),
        out_specs=(
            both, both, P("seq", "head"), P("seq"), P("head"), P("seq", "head"), P("head", "seq"), P("head"), P("seq"),
            P("head", "seq"), P(), P(), P(),
        ),
        check_vma=False,
    )
```

time: 1480 us -> 228 us (0.15); the launches traced: 1460 us -> 228 us
  waiting for transfers between devices: 365 us -> 0 us
  local copies, waits for them, and re-layouts: 352 us -> 9.51 us
  other arithmetic: 284 us -> 0 us
  blocking collectives: 257 us -> 0 us
  Pallas kernels: 0 us -> 217 us
  matrix products: 148 us -> 0 us
  starting transfers between devices: 33.8 us -> 0 us
  between operations: 23.3 us -> 1.38 us
    pallas_call x0 -> x2, Pallas kernels: none -> 217 us  [the longest x1 116 us: rear(): pl.pallas_call(functools.partial(rear_kernel, n_s, n_h, cph, oph, rin, rp...]
    all_to_all x6 -> x0, waiting for transfers between devices: 175 us -> none  [the longest x1 100 us: on_device(): lax.all_to_all(x_grad.reshape(seq_rows, 1, head_width), 'head', split_axi...]
    unnamed x1 -> x0, blocking collectives: 164 us -> none
    dot_general x30 -> x0, matrix products: 148 us -> none  [the longest x6 48.4 us: direction_scan(): within = jnp.einsum('khts,kshp->kthp', mixing, x_blocks, precision=PRECISE)]
    all_gather x3 -> x0, waiting for transfers between devices: 122 us -> none  [the longest x1 93.4 us: on_device(): lax.all_gather(in_part, 'head', axis=1, tiled=True)]
    reduce_sum x44 -> x0, other arithmetic: 88.7 us -> none  [the longest x24 58.5 us: advance(): return (carried_state * decay_part[:, None, None] + fresh, carried_state)]
    psum x2 -> x0, blocking collectives: 81.2 us -> none  [the longest x1 41.4 us: on_device(): lax.psum(jnp.stack([jnp.sum(scaled_in * scaled_in), jnp.sum(scaled_out *...]
    dynamic_update_slice x49 -> x0, other arithmetic: 74.4 us -> none  [the longest x48 74 us: direction_scan(): _, entering = lax.scan(advance, state_init, (block_decay, block_states))]
  transfers between devices with their start and end apart: 15 -> 0, of which waited for: 11 -> 0; matrix products, arithmetic and copies ran while one was open for 38% -> 0% of each run, Pallas kernels for 0% -> 0%
where the time goes in v3:
time: 228 us
  Pallas kernels  217 us (95%)
  local copies, waits for them, and re-layouts  9.51 us (4%)
    pallas_call x1, Pallas kernels, rear(): pl.pallas_call(functools.partial(rear_kernel, n_s, n_h, cph, oph, rin, rp...  116 us
    pallas_call x1, Pallas kernels, fore(): pl.pallas_call(functools.partial(fore_kernel, n_s, n_h, cph, oph, rin, rp...  101 us
    unnamed x39, local copies, waits for them, and re-layouts  9.51 us

profile of v3, /device:TPU:0, one launch (start us, length us, event | category | flops | bytes accessed | tf_op | source)
XLA Modules:
  0.0 227.8 jit_solution(13823066354548948811)
XLA Ops:
  1.3 100.6 %fore.1 = (bf16[384,768]{1,0:T(8,128)(2,1)}, bf16[768,3328]{1,0:T(8,128)(2,1)}, bf16[384,768]{1,0:T(8,128)(2,1)}, bf16[400,1664]{1,0:T(8,128)(2,1)}, bf16[384,16...) custom-call(bf16[384,768]{1,0:T(8,128)(2,1)} %x.3, ...), custom_call_target="tpu_custom_call" | custom-call | tf_op jit(solution)/shard_map/fore/pallas_call | solution.py:763
  101.9 0.0 copy-start.1
  101.9 116.4 %rear.1 = (f32[384,768]{1,0:T(8,128)}, f32[96,806]{1,0:T(8,128)}, f32[96]{0:T(128)}, f32[806]{0:T(1024)}, f32[96,806]{1,0:T(8,128)}, /*index=5*/f32[96,384]{1,0:...) custom-call(bf16[384,768]{1,0:T(8,128)(2,1)} %x.3, ...), custom_call_target="tpu_custom_call" | custom-call | tf_op jit(solution)/shard_map/rear/pallas_call | solution.py:1478
  218.3 0.0 copy-start
  218.3 0.0 copy-done.1
  218.3 0.8 copy.38
  219.1 0.6 copy-done
  219.8 1.0 copy.39
  220.8 0.1 copy-done.3
  220.9 0.0 copy-start.8
  220.9 0.0 copy-start.7
  220.9 0.0 copy-start.6
  221.0 0.7 copy.40
  221.7 0.5 copy.41
  222.2 0.6 copy.42
  222.8 0.7 copy.43
  223.5 0.7 copy.44
  224.2 0.0 copy-done.10
  224.2 0.6 copy.45
  224.8 0.5 copy.46
  225.3 0.7 copy.47
  226.0 0.6 copy.48
  226.6 0.6 copy.49
  227.2 0.6 copy.50
  (17 shorter events, 0.0 us)
Async XLA Ops:
  101.9 116.4 %copy-start.1 = (bf16[384,768]{1,0:T(8,128)(2,1)S(1)}, bf16[384,768]{1,0:T(8,128)(2,1)}, u32[]{:S(2)}) copy-start(bf16[384,768]{1,0:T(8,128)(2,1)} %get-tuple-element.88) | copy-start | bytes 1769476
  218.3 1.5 copy-start
  219.7 1.2 copy-start.3
  219.8 1.9 copy-start.12
  219.8 2.5 %copy-start.9 = (f32[806]{0:T(1024)S(1)}, f32[806]{0:T(1024)}, u32[]{:S(2)}) copy-start(f32[806]{0:T(1024)} %get-tuple-element.92) | copy-start | bytes 9676
  219.8 3.0 %copy-start.2 = (f32[96,806]{1,0:T(8,128)S(1)}, f32[96,806]{1,0:T(8,128)}, u32[]{:S(2)}) copy-start(f32[96,806]{1,0:T(8,128)} %get-tuple-element.93) | copy-start | bytes 928516
  220.9 2.6 %copy-start.5 = (f32[96,384]{1,0:T(8,128)S(1)}, f32[96,384]{1,0:T(8,128)}, u32[]{:S(2)}) copy-start(f32[96,384]{1,0:T(8,128)} %get-tuple-element.68) | copy-start | bytes 442372
  220.9 3.3 %copy-start.10 = (f32[384]{0:T(512)S(1)}, f32[384]{0:T(512)}, u32[]{:S(2)}) copy-start(f32[384]{0:T(512)} %get-tuple-element.95) | copy-start | bytes 4612
  220.9 3.9 %copy-start.11 = (f32[96]{0:T(128)S(1)}, f32[96]{0:T(128)}, u32[]{:S(2)}) copy-start(f32[96]{0:T(128)} %get-tuple-element.96) | copy-start | bytes 1156
  220.9 4.4 %copy-start.4 = (f32[96,384]{1,0:T(8,128)S(1)}, f32[96,384]{1,0:T(8,128)}, u32[]{:S(2)}) copy-start(f32[96,384]{1,0:T(8,128)} %get-tuple-element.71) | copy-start | bytes 442372
  220.9 5.0 %copy-start.8 = (f32[10696]{0:T(1024)S(1)}, f32[10696]{0:T(1024)}, u32[]{:S(2)}) copy-start(f32[10696]{0:T(1024)} %get-tuple-element.98) | copy-start | bytes 128356
  220.9 5.7 %copy-start.7 = (f32[10696]{0:T(1024)S(1)}, f32[10696]{0:T(1024)}, u32[]{:S(2)}) copy-start(f32[10696]{0:T(1024)} %get-tuple-element.99) | copy-start | bytes 128356
  220.9 6.3 %copy-start.6 = (f32[10696]{0:T(1024)S(1)}, f32[10696]{0:T(1024)}, u32[]{:S(2)}) copy-start(f32[10696]{0:T(1024)} %get-tuple-element.100) | copy-start | bytes 128356

commit v4 on v3

--- a/solution.py
+++ b/solution.py
@@ -48,9 +48,17 @@
     return high, (value - high.astype(F32)).astype(BF16)
 
 
+def stacked(value):
+    return jnp.concatenate(split(value), axis=0)
+
+
+def halves_sum(value):
+    rows = value.shape[0] // 2
+    return value[:rows] + value[rows:]
+
+
 def nn_split(value, exact):
-    high, low = split(value)
-    return nn(high, exact) + nn(low, exact)
+    return halves_sum(nn(stacked(value), exact))
 
 
 def expand(value, spread):
@@ -58,8 +66,7 @@
 
 
 def fold(value, spread):
-    high, low = split(value)
-    return nt(high, spread) + nt(low, spread)
+    return halves_sum(nt(stacked(value), spread))
 
 
 def iota(shape, dim):
@@ -146,19 +153,19 @@
             self.snd[d, at] = self.out[d, at] * self.dec[0:1] + self.dev[d, at]
             self.link(d, c).start()
 
-    def at(self, k):
+    def at(self, k, stride=2):
         for c in range(CHAIN_PARTS):
 
-            @pl.when(k == 2 * self.h + c)
+            @pl.when(k == stride * self.h + c)
             def _():
                 self.step(0, c)
 
-            @pl.when(k == 2 * (self.n_h - 1 - self.h) + c)
+            @pl.when(k == stride * (self.n_h - 1 - self.h) + c)
             def _():
                 self.step(1, c)
 
-    def steps(self):
-        return 2 * (self.n_h - 1) + CHAIN_PARTS
+    def steps(self, stride=2):
+        return stride * (self.n_h - 1) + CHAIN_PARTS
 
     def finish(self):
         for d in range(2):
@@ -229,9 +236,18 @@
     spread[...] = (iota((LANES, INNER), 0) == iota((LANES, INNER), 1) // HEAD_DIM).astype(BF16)
 
 
+def run_all(*steps):
+    def run():
+        for step in steps:
+            step()
+
+    return run
+
+
 class Gather:
-    def __init__(self, n_s, n_h, s, h, full, lanes, sems):
-        self.n_s, self.n_h, self.s, self.h, self.full, self.lanes = n_s, n_h, s, h, full, lanes
+    def __init__(self, n_s, n_h, s, h, full, base, count, parts, sems):
+        self.n_s, self.n_h, self.s, self.h, self.full = n_s, n_h, s, h, full
+        self.base, self.count, self.parts = base, count, parts
         self.zs, self.zr, self.ps, self.pr, self.ds, self.dr, self.cs, self.cr = sems
         self.n_c = n_s // 2
         self.chip = s // 2
@@ -242,182 +258,219 @@
         self.xn = self.chip + 1 - 2 * lax.rem(self.chip, 2)
         self.yn = lax.rem(self.chip + self.n_c // 2, self.n_c)
         self.diag = 3 - self.chip
-        self.inner = jnp.logical_and(h > 0, h < n_h - 1)
-        self.order = [h] + [self.nth(j) for j in range(1, n_h)]
-
-    def nth(self, j):
-        n_h, h = self.n_h, self.h
-        below = jnp.where(j - 1 >= h, j, j - 1)
-        mirror = n_h - 1 - h
-        above = n_h - 1 - jnp.where(j - 1 >= mirror, j, j - 1)
-        return jnp.where(2 * h < n_h, below, above)
-
-    def blk(self, q, c, part=None):
-        ref = self.full.at[q, c * 2 + self.core]
+        place = jnp.clip(h - base, 0, count - 1)
+        self.order = [base + place] + [base + self.nth(j, place, count) for j in range(1, count)]
+        self.items = [(q, p) for q in self.order for p in range(len(parts))]
+
+    def nth(self, j, place, count):
+        below = jnp.where(j - 1 >= place, j, j - 1)
+        mirror = count - 1 - place
+        above = count - 1 - jnp.where(j - 1 >= mirror, j, j - 1)
+        return jnp.where(2 * place < count, below, above)
+
+    def when(self, item, work):
+        q, p = item
+        only = self.parts[p][1]
+        if only is None:
+            work()
+        else:
+            pl.when(q == only)(work)
+
+    def blk(self, item, c, part=None, other=False):
+        q, p = item
+        core = 1 - self.core if other else self.core
+        ref = self.full.at[q, c * 2 + core]
         rp = self.full.shape[2]
+        lanes = self.parts[p][0]
         if part is None:
-            return ref.at[:, self.lanes]
+            return ref.at[:, lanes]
         mid = rp // 2 // 16 * 16
-        return ref.at[pl.ds(0, mid) if part == 0 else pl.ds(mid, rp - mid), self.lanes]
-
-    def along(self, q, way):
-        ref = self.blk(q, self.chip)
+        return ref.at[pl.ds(0, mid) if part == 0 else pl.ds(mid, rp - mid), lanes]
+
+    def along(self, item, way):
+        ref = self.blk(item, self.chip)
         to = lax.rem(self.h + (1 if way == 0 else self.n_h - 1), self.n_h)
-        return remote(ref, ref, self.zs.at[q, way], self.zr.at[q], (self.s, to))
+        q, p = item
+        return remote(ref, ref, self.zs.at[q - self.base, p, way], self.zr.at[q - self.base, p], (self.s, to))
 
     def begin(self):
-        @pl.when(self.h < self.n_h - 1)
-        def _():
-            self.along(self.h, 0).start()
-
-        @pl.when(self.h > 0)
-        def _():
-            self.along(self.h, 1).start()
-
-        self.spread_out(0)
+        for p in range(len(self.parts)):
+            item = (self.h, p)
+            mine = jnp.logical_and(self.h >= self.base, self.h < self.base + self.count)
+            if self.parts[p][1] is not None:
+                mine = jnp.logical_and(mine, self.h == self.parts[p][1])
+            for way, there in ((0, self.h < self.n_h - 1), (1, self.h > 0)):
+                pl.when(jnp.logical_and(mine, there))(lambda item=item, way=way: self.along(item, way).start())
 
     def z_in(self, i):
-        q = self.order[i]
-        self.along(q, 0).wait_recv()
-
-        @pl.when(jnp.logical_and(q < self.h, self.h < self.n_h - 1))
-        def _():
-            self.along(q, 0).start()
-
-        @pl.when(jnp.logical_and(q > self.h, self.h > 0))
-        def _():
-            self.along(q, 1).start()
-
-    def z_done(self):
-        for i in range(self.n_h):
-            q = self.order[i]
-
-            @pl.when(jnp.logical_and(q <= self.h, self.h < self.n_h - 1))
-            def _():
-                self.along(q, 0).wait_send()
-
-            @pl.when(jnp.logical_and(q >= self.h, self.h > 0))
-            def _():
-                self.along(q, 1).wait_send()
-
-    def to_chip(self, i, m, part, q, c):
-        ref = self.blk(q, self.chip, part)
+        item = self.items[i]
+        q = item[0]
+
+        def take():
+            self.along(item, 0).wait_recv()
+            up = jnp.logical_and(q < self.h, self.h < self.n_h - 1)
+            down = jnp.logical_and(q > self.h, self.h > 0)
+            pl.when(up)(lambda: self.along(item, 0).start())
+            pl.when(down)(lambda: self.along(item, 1).start())
+
+        self.when(item, lambda: pl.when(q != self.h)(take))
+
+    def z_done(self, i):
+        item = self.items[i]
+        q = item[0]
+        up = jnp.logical_and(q <= self.h, self.h < self.n_h - 1)
+        down = jnp.logical_and(q >= self.h, self.h > 0)
+        self.when(item, lambda: pl.when(up)(lambda: self.along(item, 0).wait_send()))
+        self.when(item, lambda: pl.when(down)(lambda: self.along(item, 1).wait_send()))
+
+    def to_chip(self, i, m, part, c):
+        item = self.items[i]
+        q, p = item
+        ref = self.blk(item, self.chip, part)
         n = 0 if part is None else part
-        return remote(ref, ref, self.ps.at[i, m, n], self.pr.at[q, self.chip, n], (c * 2 + self.core, self.h))
-
-    def over(self, i, j, q, c):
-        ref = self.blk(q, c)
-        return remote(ref, ref, self.cs.at[i, j], self.cr.at[q, c], (self.sib, self.h))
-
-    def spread_out(self, i):
-        for c in self.to_chips(i):
-            c.start()
-        self.over(i, 0, self.order[i], self.chip).start()
+        return remote(ref, ref, self.ps.at[q - self.base, p, m, n], self.pr.at[q - self.base, p, self.chip, n], (c * 2 + self.core, self.h))
 
     def to_chips(self, i):
-        q = self.order[i]
         if self.square:
             near = ((0, self.xn), (1, self.yn))
-            return [self.to_chip(i, m, (n + m) % 2, q, c) for n in range(2) for m, c in near]
-        return [self.to_chip(i, j, None, q, c) for j, c in enumerate(self.cpeer)]
+            return [self.to_chip(i, m, (n + m) % 2, c) for n in range(2) for m, c in near]
+        return [self.to_chip(i, j, None, c) for j, c in enumerate(self.cpeer)]
+
+    def over(self, i, j, c):
+        item = self.items[i]
+        q, p = item
+        ref = self.blk(item, c)
+        return remote(ref, ref, self.cs.at[q - self.base, p, j], self.cr.at[q - self.base, p, c], (self.sib, self.h))
 
     def onward(self, i, n):
-        q = self.order[i]
+        item = self.items[i]
+        q, p = item
         c, to = (self.xn, self.yn) if n == 0 else (self.yn, self.xn)
-        ref = self.blk(q, c, n)
-        return remote(ref, ref, self.ds.at[i, n], self.dr.at[q, n], (to * 2 + self.core, self.h))
-
-    def got(self, q, c, part):
-        ref = self.blk(q, c, part)
+        ref = self.blk(item, c, n)
+        return remote(ref, ref, self.ds.at[q - self.base, p, n], self.dr.at[q - self.base, p, n], (to * 2 + self.core, self.h))
+
+    def spread_out(self, i):
+        def work():
+            for c in self.to_chips(i):
+                c.start()
+            self.over(i, 0, self.chip).start()
+
+        self.when(self.items[i], work)
+
+    def got(self, i, c, part):
+        item = self.items[i]
+        q, p = item
+        ref = self.blk(item, c, part)
         n = 0 if part is None else part
-        remote(ref, ref, self.ps.at[0, 0, 0], self.pr.at[q, c, n], (self.sib, self.h)).wait_recv()
+        remote(ref, ref, self.ps.at[q - self.base, p, 0, 0], self.pr.at[q - self.base, p, c, n], (self.sib, self.h)).wait_recv()
 
     def pass_on(self, i):
-        q = self.order[i]
-        if self.square:
-            for n, c in ((0, self.xn), (1, self.yn)):
-                self.got(q, c, n)
-                self.onward(i, n).start()
-            for n, c in ((1, self.xn), (0, self.yn)):
-                self.got(q, c, n)
-                self.over(i, 2 - n, q, c).start()
-        else:
-            for j, c in enumerate(self.cpeer):
-                self.got(q, c, None)
-                self.over(i, j + 1, q, c).start()
+        def work():
+            if self.square:
+                for n, c in ((0, self.xn), (1, self.yn)):
+                    self.got(i, c, n)
+                    self.onward(i, n).start()
+                for n, c in ((1, self.xn), (0, self.yn)):
+                    self.got(i, c, n)
+                    self.over(i, 2 - n, c).start()
+            else:
+                for j, c in enumerate(self.cpeer):
+                    self.got(i, c, None)
+                    self.over(i, j + 1, c).start()
+
+        self.when(self.items[i], work)
 
     def last_in(self, i):
-        if self.square:
-            q = self.order[i]
+        if not self.square:
+            return
+        item = self.items[i]
+        q, p = item
+
+        def work():
             for n in range(2):
-                ref = self.blk(q, self.diag, n)
-                remote(ref, ref, self.ds.at[0, 0], self.dr.at[q, n], (self.sib, self.h)).wait_recv()
-            self.over(i, 3, q, self.diag).start()
+                ref = self.blk(item, self.diag, n)
+                remote(ref, ref, self.ds.at[q - self.base, p, 0], self.dr.at[q - self.base, p, n], (self.sib, self.h)).wait_recv()
+            self.over(i, 3, self.diag).start()
+
+        self.when(item, work)
 
     def complete(self, i):
-        q = self.order[i]
-        for c in [self.chip] + self.cpeer:
-            ref = self.full.at[q, c * 2 + 1 - self.core].at[:, self.lanes]
-            remote(ref, ref, self.cs.at[0, 0], self.cr.at[q, c], (self.sib, self.h)).wait_recv()
+        item = self.items[i]
+        q, p = item
+
+        def work():
+            for c in [self.chip] + self.cpeer:
+                ref = self.blk(item, c, other=True)
+                remote(ref, ref, self.cs.at[q - self.base, p, 0], self.cr.at[q - self.base, p, c], (self.sib, self.h)).wait_recv()
+
+        self.when(item, work)
 
     def plan(self, columns):
-        n_h = self.n_h
-
-        def run(*steps):
-            def all_steps():
-                for step in steps:
-                    step()
-
-            return all_steps
-
-        plan = [lambda: self.z_in(1), lambda: self.spread_out(1)]
-        if n_h > 2:
-            plan.append(lambda: pl.when(self.inner)(lambda: self.z_in(2)))
-        plan.append(lambda: self.pass_on(0))
-        for i in range(2, n_h):
-            if i == 2:
-                plan.append(lambda: pl.when(jnp.logical_not(self.inner))(lambda: self.z_in(2)))
-            else:
-                plan.append(lambda i=i: self.z_in(i))
-            plan.append(lambda i=i: self.spread_out(i))
-            plan.append(run(lambda i=i: self.last_in(i - 2), lambda i=i: self.pass_on(i - 1)))
-            plan.append(run(lambda i=i: self.complete(i - 2), lambda i=i: columns(i - 2)))
-        plan.append(run(lambda: self.last_in(n_h - 2), lambda: self.pass_on(n_h - 1)))
-        plan.append(run(lambda: self.complete(n_h - 2), lambda: columns(n_h - 2)))
-        plan.append(run(lambda: self.last_in(n_h - 1), lambda: self.complete(n_h - 1), lambda: columns(n_h - 1)))
+        count, parts = len(self.items), len(self.parts)
+        plan = []
+        for i in range(count + 3):
+            if i < count:
+                plan.append(run_all(lambda i=i: self.z_in(i), lambda i=i: self.spread_out(i)))
+            if 1 <= i <= count:
+                plan.append(lambda i=i: self.pass_on(i - 1))
+            if 2 <= i <= count + 1:
+                plan.append(lambda i=i: self.last_in(i - 2))
+            if 3 <= i:
+                plan.append(lambda i=i: self.complete(i - 3))
+                if (i - 3) % parts == parts - 1 and columns is not None:
+                    plan.append(lambda i=i: columns(self.order[(i - 3) // parts]))
         return plan
 
     def finish(self):
-        self.z_done()
-        for i in range(self.n_h):
-            q = self.order[i]
+        for i in range(len(self.items)):
+            self.z_done(i)
             chips = [self.chip] + ([self.xn, self.yn, self.diag] if self.square else self.cpeer)
-            for c in self.to_chips(i):
-                c.wait_send()
-            for j, c in enumerate(chips):
-                self.over(i, j, q, c).wait_send()
-            if self.square:
-                for n in range(2):
-                    self.onward(i, n).wait_send()
-
-
-def gather_sems(n_s, n_h):
+
+            def work():
+                for c in self.to_chips(i):
+                    c.wait_send()
+                for j, c in enumerate(chips):
+                    self.over(i, j, c).wait_send()
+                if self.square:
+                    for n in range(2):
+                        self.onward(i, n).wait_send()
+
+            self.when(self.items[i], work)
+
+
+def gather_sems(n_s, count, parts):
     dma = pltpu.SemaphoreType.DMA
     n_c = n_s // 2
+    n = 2 if n_c == 4 else 1
     return [
-        dma((n_h, 2)), dma((n_h,)), dma((n_h, n_c, 2)), dma((n_h, n_c, 2)), dma((n_h, 2)), dma((n_h, 2)), dma((n_h, n_c)),
-        dma((n_h, n_c)),
+        dma((count, parts, 2)), dma((count, parts)), dma((count, parts, n_c, n)), dma((count, parts, n_c, n)),
+        dma((count, parts, 2)), dma((count, parts, 2)), dma((count, parts, n_c)), dma((count, parts, n_c)),
     ]
 
 
+def own_tiles(per_part, parts, width):
+    return [(per_part * q) // LANES for q in range(parts)] + [width // LANES]
+
+
+def payload_parts(per_part, parts, width):
+    first = own_tiles(per_part, parts, width)
+    counts = [first[q + 1] - first[q] for q in range(parts)]
+    common = max(counts[:-1])
+    mid = (common + 1) // 2
+    ranges = [(slice(0, mid * LANES), None), (slice(mid * LANES, common * LANES), None)]
+    if counts[-1] > common:
+        ranges.append((slice(common * LANES, counts[-1] * LANES), parts - 1))
+    return ranges, max(counts) * LANES
+
+
 def fore_kernel(
-    n_s, n_h, cph, oph, rin, rp, wi, wo,
+    n_s, n_h, cph, oph, rin, rp, wi, wo, wide_in,
     x, cot, w_in, w_out_t, flat, lengths,
     result, w_full_o, nlow_o, conv_in_o, conv_low_o, slope_o, raw, steps, decb, dec, dgate, hgrad, glow, dgain, lst, mst,
     dev2, hin_o, gin_o,
-    full, w_full, o_full, xh, shift_in, shift_out, nscr, conv_in, conv_low, slope, cf, gate, hst, gst, dev, into, csnd, incl_r,
-    excl_r, incl_t, excl_t, steps_t, inter_s, yb, el, eg, gg_scr, hin, gin, prm, gain, taps, heads, out_gain, spread,
-    xs_, xr_, us, ur, dws, dwr, outs, *gsems,
+    full, w_full, o_full, xh, shift_in, edge_out, edge_in, shift_out, nscr, conv_in, conv_low, slope, cf, gate, hst, gst, dev, into, csnd, incl_r,
+    excl_r, incl_t, excl_t, steps_t, inter_s, yb, el, eg, gg_scr, hin, gin, prm, gain, taps, heads, out_gain, spread, logs3, el_eg, cc2,
+    xs_, xr_, es_, er_, us, ur, dws, dwr, outs, *gsems,
 ):
     s = lax.axis_index("seq")
     h = lax.axis_index("head")
@@ -430,8 +483,12 @@
     sib = chip * 2 + (1 - core)
     cpeer = [lax.rem(chip + j, n_c) for j in range(1, n_c)]
     left = lengths[0] - h * rows
-    g_in = Gather(n_s, n_h, s, h, full, slice(0, wi), gsems[:8])
-    g_out = Gather(n_s, n_h, s, h, full, slice(wi, wi + wo), gsems[8:])
+    parts, _ = payload_parts(cph, n_h, WIDE)
+    sems = [gsems[8 * n : 8 * n + 8] for n in range(3)]
+    half_h = n_h // 2
+    g_high = Gather(n_s, n_h, s, h, full, half_h, n_h - half_h, parts, sems[0])
+    g_low = Gather(n_s, n_h, s, h, full, 0, half_h, parts[:2], sems[1])
+    g_out = Gather(n_s, n_h, s, h, full, 0, n_h, [(slice(wi, wi + wo), None)], sems[2])
     zpeer = [lax.rem(h + j, n_h) for j in range(1, n_h)]
     bar = pltpu.get_barrier_semaphore()
     for z in zpeer:
@@ -442,7 +499,19 @@
 
     shift_in[...] = jnp.zeros_like(shift_in)
     shift_in[0:rin, 0:cph] = w_in[...]
-    full[h, s, :, 0:wi] = pltpu.roll(shift_in[...], lax.rem(cph * h, LANES), 1).astype(BF16)
+    placed = pltpu.roll(shift_in[...], lax.rem(cph * h, LANES), 1)
+    shift_in[...] = placed
+    full[h, s, :, 0:wi] = placed[:, 0:wi].astype(BF16)
+    first_tile = own_tiles(cph, n_h, WIDE)
+    up = lax.rem(h + 1, n_h)
+    for q in range(n_h - 1):
+        at = (first_tile[q + 1] - first_tile[q]) * LANES
+
+        @pl.when(h == q)
+        def _():
+            edge_out[...] = shift_in[:, at : at + LANES].astype(BF16)
+
+    edge = remote(edge_out, edge_in, es_.at[0], er_.at[0], (s, up))
     shift_out[...] = jnp.zeros_like(shift_out)
     shift_out[0:rin, 0:oph] = w_out_t[...]
     turned = shift_out[...]
@@ -451,13 +520,25 @@
     full[h, s, :, wi:] = turned.astype(BF16)
     pl.semaphore_wait(bar, n_h + n_c - 1)
 
-    g_in.begin()
-    up = lax.rem(h + 1, n_h)
+
+    @pl.when(h < n_h - 1)
+    def _():
+        edge.start()
+
+    @pl.when(h > 0)
+    def _():
+        edge.wait_recv()
+        full[h, s, :, 0:LANES] += edge_in[...]
+
+    g_high.begin()
     halo = remote(x.at[rows - HALO : rows], xh, xs_.at[0], xr_.at[0], (s, up))
 
     @pl.when(h < n_h - 1)
     def _():
         halo.start()
+
+    high_plan = g_high.plan(lambda q: columns(q))
+    high_plan[0]()
 
     flat_rows(flat, prm, 0.0)
     unpack_rows(prm, rin, rp, gain, taps, heads, out_gain)
@@ -473,7 +554,7 @@
         norm_rows(x, pl.ds(at, 16), pl.ds(at + HALO, 16))
         return 0
 
-    lax.fori_loop(0, rows // 16, norm_body, 0)
+    lax.fori_loop(0, rows // 16, norm_body, 0, unroll=4)
 
     @pl.when(h > 0)
     def _():
@@ -517,28 +598,25 @@
             conv_low[:, at] = (total * sg).astype(BF16)
             slope[:, at] = sg * (1.0 + total * (1.0 - sg))
 
-    def columns(i):
-        q = g_in.order[i]
+    def tile_of(q, t):
         t0 = (cph * q) // LANES
-        lo = (cph * q + LANES - 1) // LANES
+        at = pl.ds(pl.multiple_of((t - t0) * LANES, LANES), LANES)
+        project(t, full[q, :, :, at].reshape(dp, LANES))
+
+    def columns(q):
         hi = jnp.where(q == n_h - 1, WIDE // LANES, (cph * (q + 1)) // LANES)
 
         def tile_body(t, _):
-            at = pl.ds(pl.multiple_of((t - t0) * LANES, LANES), LANES)
-            project(t, full[q, :, :, at].reshape(dp, LANES))
+            tile_of(q, t)
             return 0
 
-        lax.fori_loop(lo, hi, tile_body, 0)
-
-    for step in g_in.plan(columns):
+        lax.fori_loop((cph * q) // LANES, hi, tile_body, 0)
+
+    for step in high_plan[1:]:
         step()
+    g_low.begin()
     g_out.begin()
-    for q in range(1, n_h):
-        if (cph * q) % LANES:
-            tile, t0 = (cph * q) // LANES, (cph * (q - 1)) // LANES
-            at = (tile - t0) * LANES
-            project(tile, (full[q - 1, :, :, at : at + LANES] + full[q, :, :, 0:LANES]).reshape(dp, LANES))
-    for n, (src, dst) in enumerate(((w_full, w_full_o), (conv_in, conv_in_o), (conv_low, conv_low_o), (slope, slope_o))):
+    for n, (src, dst) in enumerate(((conv_in, conv_in_o), (conv_low, conv_low_o), (slope, slope_o))):
         leaving.append(leave(src, dst, n + 1))
         leaving[-1].start()
 
@@ -556,18 +634,23 @@
         incl_t[b] = incl.T
         excl_t[b] = excl.T
         steps_t[b] = st.T
-        wide = split(jnp.concatenate([jnp.exp(total - incl) * st, jnp.exp(excl) * st], axis=0))
+        logs3[b] = jnp.concatenate(split3(jnp.concatenate([incl, excl], axis=0)), axis=1)
+        el_eg[b] = stacked(jnp.concatenate([jnp.exp(incl), jnp.exp(total - excl)], axis=0))
+        wide = stacked(jnp.concatenate([jnp.exp(total - incl) * st, jnp.exp(excl) * st], axis=0))
         bc = conv_low[at, INNER:].astype(F32)
         bt = bc.T[:STATE].astype(BF16)
         bt2 = jnp.concatenate([bt, bt], axis=1)
-        c_low = half_masks(pltpu.roll(bc, STATE, 1))[0].astype(BF16)
-        inter_s[b] = nt(c_low, bc.astype(BF16))
+        cb = pltpu.roll(bc, STATE, 1)
+        c_low = half_masks(cb)[0].astype(BF16)
+        inter_s[b] = nt(c_low, bc.astype(BF16)) * (1.0 + (iota((SPAN, SPAN), 0) == iota((SPAN, SPAN), 1)).astype(F32))
+        cc = cb[:, :STATE].astype(BF16)
+        cc2[b] = jnp.concatenate([cc, cc], axis=1)
         tot = jnp.broadcast_to(jnp.exp(total), (8, LANES))
         for g in range(INNER // 256):
             cols = slice(g * 256, (g + 1) * 256)
             sp = spread[:, cols]
             xs = conv_low[at, cols].astype(F32)
-            w = nn(wide[0], sp) + nn(wide[1], sp)
+            w = halves_sum(nn(wide, sp))
             for n, dst in ((0, hst), (1, gst)):
                 hi, lo = split(w[n * SPAN : (n + 1) * SPAN] * xs)
                 dst[b, :, cols] = nn(bt2, jnp.concatenate([hi, lo], axis=0))
@@ -586,7 +669,6 @@
 
     row = iota((SPAN, SPAN), 0)
     col = iota((SPAN, SPAN), 1)
-    twice = 1.0 + (row == col).astype(F32)
     skip8 = jnp.broadcast_to(heads[2:3, :], (8, LANES))
 
     def pair_body(pair, _):
@@ -595,11 +677,11 @@
         hot = (iota((LANES, 2 * LANES), 0) == 2 * pair + iota((LANES, 2 * LANES), 1) // LANES).astype(BF16)
         hot3 = jnp.concatenate([hot, hot, hot], axis=0)
         skip = expand(skip8, spread[:, cols])[0:1]
+        wide_all = nn(logs3[...].reshape(blocks * 2 * SPAN, 3 * LANES), hot3)
         for b in range(blocks):
             at = slice(b * SPAN, (b + 1) * SPAN)
-            both = jnp.concatenate([incl_r[b], excl_r[b]], axis=0)
-            wide = nn(jnp.concatenate(split3(both), axis=1), hot3)
-            inter = inter_s[b] * twice
+            wide = wide_all[b * 2 * SPAN : (b + 1) * 2 * SPAN]
+            inter = inter_s[b]
             xs = conv_low[at, cols]
             mix = []
             for n in range(2):
@@ -614,15 +696,33 @@
             x0, x1 = half_masks(xs)
             y = nn_split(jnp.concatenate(mix, axis=1), jnp.concatenate([x0, x1], axis=0))
             yb[at, cols] = y + skip * xs.astype(F32)
-        chain.at(pair)
-        for n, step in enumerate(out_plan):
-            pl.when(pair == n * 12 // len(out_plan))(step)
+        chain.at(pair, 3)
+        for n, step in enumerate(behind):
+            pl.when(pair == n * pairs_n // len(behind))(step)
         return 0
 
-    out_plan = g_out.plan(lambda i: None)
-    lax.fori_loop(0, HEADS // 2, pair_body, 0)
-    for k in range(HEADS // 2, chain.steps()):
-        chain.at(k)
+    low_plan = g_low.plan(None)
+    out_plan = g_out.plan(None)
+    behind = []
+    for n in range(max(len(low_plan), len(out_plan))):
+        behind += low_plan[n : n + 1] + out_plan[n : n + 1]
+    pairs_n = HEADS // 2
+    lax.fori_loop(0, pairs_n, pair_body, 0)
+
+    def gate_tiles(q):
+        def tile_body(t, _):
+            tile_of(q, t)
+            chain.at(pairs_n + t, 3)
+            return 0
+
+        lax.fori_loop((cph * q) // LANES, (cph * (q + 1)) // LANES, tile_body, 0)
+
+    for q in range(half_h):
+        gate_tiles(q)
+    for t in range((cph * half_h) // LANES, max(chain.steps(3) - pairs_n, 0)):
+        chain.at(pairs_n + t, 3)
+    leaving.append(leave(w_full, w_full_o, 4))
+    leaving[-1].start()
 
     for tile in range(INNER // LANES):
         parts = []
@@ -649,17 +749,14 @@
         cols = slice(g * 256, (g + 1) * 256)
         sp = spread[:, cols]
         gg_scr[:, cols] = nn(bgrad, o_full[:, cols])
+        wide_all = nn(el_eg[...].reshape(blocks * 4 * SPAN, LANES), sp)
         for b in range(blocks):
             at = slice(b * SPAN, (b + 1) * SPAN)
-            incl = incl_r[b]
-            hi, lo = split(jnp.concatenate([jnp.exp(incl), jnp.exp(incl[SPAN - 1 : SPAN] - excl_r[b])], axis=0))
-            wide = nn(hi, sp) + nn(lo, sp)
+            wide = halves_sum(wide_all[b * 4 * SPAN : (b + 1) * 4 * SPAN])
             el[at, cols] = wide[0:SPAN]
             eg[at, cols] = wide[SPAN:]
-            cc = pltpu.roll(conv_low[at, INNER:].astype(F32), STATE, 1)[:, :STATE].astype(BF16)
-            cc2 = jnp.concatenate([cc, cc], axis=1)
-            yf = nn(cc2, jnp.concatenate(split(hin[b, :, cols]), axis=0))
-            yg = nn(cc2, jnp.concatenate(split(gin[b + 1, :, cols]), axis=0))
+            yf = nn(cc2[b], stacked(hin[b, :, cols]))
+            yg = nn(cc2[b], stacked(gin[b + 1, :, cols]))
             yb[at, cols] += wide[0:SPAN] * yf + wide[SPAN:] * yg
     dgain[...] = jnp.zeros_like(dgain)
 
@@ -682,7 +779,7 @@
         dgate[at, :] = (dg * hv * (sg * (1.0 + z * (1.0 - sg)))).astype(BF16)
         return 0
 
-    lax.fori_loop(0, rows // 16, gate_body, 0)
+    lax.fori_loop(0, rows // 16, gate_body, 0, unroll=2)
     for g in range(dp // 256):
         cols = slice(g * 256, (g + 1) * 256)
         branch = nt(glow[...], o_full[cols, :])
@@ -714,8 +811,14 @@
     def _():
         halo.wait_send()
 
-    g_in.finish()
+    g_high.finish()
+    g_low.finish()
     g_out.finish()
+
+    @pl.when(h < n_h - 1)
+    def _():
+        edge.wait_send()
+
     for c in leaving:
         c.wait()
 
@@ -726,7 +829,8 @@
     oph = w_out_t.shape[1]
     rows, dp = x.shape
     blocks = rows // SPAN
-    wi = tile_count(cph, n_h) * LANES
+    parts, wi = payload_parts(cph, n_h, WIDE)
+    wide_in = max(tile_count(cph, n_h) * LANES, wi)
     wo = tile_count(oph, n_h) * LANES
     dma = pltpu.SemaphoreType.DMA
     vm = pl.BlockSpec(memory_space=pltpu.VMEM)
@@ -761,7 +865,7 @@
         (entries, hbm),
     ]
     return pl.pallas_call(
-        functools.partial(fore_kernel, n_s, n_h, cph, oph, rin, rp, wi, wo),
+        functools.partial(fore_kernel, n_s, n_h, cph, oph, rin, rp, wi, wo, wide_in),
         out_shape=tuple(o for o, _ in outs),
         in_specs=[vm, vm, vm, vm, vm, sm],
         out_specs=tuple(p for _, p in outs),
@@ -770,7 +874,9 @@
             vb(dp, WIDE),
             vb(dp, INNER),
             vb(HALO, dp),
-            vf(rp, wi),
+            vf(rp, wide_in),
+            vb(rp, LANES),
+            vb(rp, LANES),
             vf(rp, wo),
             vb(rows + HALO, dp),
             vb(rows + HALO, CONV_CH),
@@ -796,12 +902,19 @@
             vf(8, LANES),
             vf(1, INNER),
             vb(LANES, INNER),
+            vb(blocks, 2 * SPAN, 3 * LANES),
+            vb(blocks, 4 * SPAN, LANES),
+            vb(blocks, SPAN, LANES),
+            dma((1,)),
+            dma((1,)),
             dma((1,)),
             dma((1,)),
         ]
         + [dma((CHAIN_PARTS,))] * 4
         + [dma((7,))]
-        + gather_sems(n_s, n_h) * 2,
+        + gather_sems(n_s, n_h - n_h // 2, len(parts))
+        + gather_sems(n_s, n_h // 2, 2)
+        + gather_sems(n_s, n_h, 1),
         compiler_params=pltpu.CompilerParams(
             collective_id=1, has_side_effects=True, vmem_limit_bytes=FORE_VMEM
         ),
@@ -811,7 +924,7 @@
 
 FORE_VMEM = 63 << 20
 SMALL = 10696
-FLAT_ROWS = 88
+FLAT_ROWS = 128
 TAPS_ROWS = CONV_CH // LANES
 HEAD_ROW = D // LANES + (CONV + 1) * TAPS_ROWS
 
@@ -823,7 +936,10 @@
 X_CHUNK = INNER // CHUNK
 SLOTS = 4
 THIRD = 6
+THIRD_LATE = 3
 HOP = 2
+EARLY = N_OUT + X_CHUNK
+LATE = HEADS // 2 + 3
 
 
 def rear_kernel(
@@ -834,11 +950,11 @@
     params_new,
     w_full, slope, conv_in, hin, gin, lst, mst, prm, sec_rows, gain, taps, heads, spread,
     adj, csnd, nt_p, bt_p, pg, ng, dpre, halo, dfs, cfs, incl_r, excl_r, incl_t, excl_t, q_t, at_f, at_g, back_f, back_g,
-    red, cross, dbc, dheads, dtaps, ngain, inter_s,
+    logs3, steps2, terms2, bb2, cc2, red, cross, dbc, dheads, dtaps, ngain, inter_s,
     sb, r0, vs, pbi, r1i, acci, r2i, pbo, r1o, acco, r2o, win,
-    sz, spl, z1, p1, z2, p2, line,
+    sz, szin, spl, sout, z1, p1, z2, p2, line,
     us, ur, ds, dr, hs, hr, s0s, s0r, s1s, s1r, s2s, s2r, o0s, o0r, o1s, o1r, o2s, o2r,
-    load, szs, szr, sps, spr, z1s, z1r, p1s, p1r, z2s, z2r, p2s, p2r,
+    load, sos, sor, szs, szr, sps, spr, z1s, z1r, p1s, p1r, z2s, z2r, p2s, p2r,
 ):
     s = lax.axis_index("seq")
     h = lax.axis_index("head")
@@ -895,7 +1011,14 @@
         part = pg[:, cols]
         sb[lax.rem(i, 2), :, 0:CHUNK] = nn(nt_p[1 - core], part)
         over_in(i).start()
-        ng[...] += nt(part, w_full[:, cols])
+
+    def normed_part(first, size, part, fresh):
+        third = dp // 3 // LANES * LANES if dp % (3 * LANES) == 0 else dp // 4
+        at = slice(part * third, (part + 1) * third)
+        v = nt(pg[:, first : first + size], w_full[at, first : first + size])
+        ng[:, at] = v if fresh else ng[:, at] + v
+
+    normed_parts = 3 if dp % (3 * LANES) == 0 else 4
 
     def second_in(i):
         cols = pl.ds(pl.multiple_of(i * CHUNK, CHUNK), CHUNK)
@@ -904,7 +1027,7 @@
         vs[:, :, 0:CHUNK] = (mine + r0[lax.rem(i, SLOTS), :, 0:CHUNK]).reshape(n_c, rp, CHUNK)
         for j, k in enumerate(cpeer):
             pbi[i, j] = vs[k, :, 0:CHUNK].astype(BF16)
-            remote(pbi.at[i, j], r1i.at[i, chip], s1s.at[i, j], s1r.at[i, chip], (2 * k + core, h)).start()
+            remote(pbi.at[i, j], r1i.at[i, n_c - 2 - j], s1s.at[i, j], s1r.at[i, n_c - 2 - j], (2 * k + core, h)).start()
         acci[i] = vs[chip, :, 0:CHUNK]
 
     def owners(i, wide, per):
@@ -915,8 +1038,8 @@
     def third_in(i):
         total = acci[i]
         for j, k in enumerate(cpeer):
-            remote(pbi.at[i, j], r1i.at[i, k], s1s.at[i, j], s1r.at[i, k], (2 * k + core, h)).wait_recv()
-            total = total + r1i[i, k].astype(F32)
+            remote(pbi.at[i, j], r1i.at[i, j], s1s.at[i, j], s1r.at[i, j], (2 * k + core, h)).wait_recv()
+            total = total + r1i[i, j].astype(F32)
         acci[i] = total
 
     def links(i, wide, per, acc, rec, snd, rcv):
@@ -961,7 +1084,7 @@
 
     def drain_in(i):
         for j, k in enumerate(cpeer):
-            remote(pbi.at[i, j], r1i.at[i, chip], s1s.at[i, j], s1r.at[i, chip], (2 * k + core, h)).wait_send()
+            remote(pbi.at[i, j], r1i.at[i, n_c - 2 - j], s1s.at[i, j], s1r.at[i, n_c - 2 - j], (2 * k + core, h)).wait_send()
         drain_z(i, *in_stream)
 
     def first_out(i):
@@ -980,60 +1103,61 @@
         vs[...] = (mine + r0[lax.rem(i, SLOTS)]).reshape(n_c, rp, OUT_CHUNK)
         for j, k in enumerate(cpeer):
             pbo[i, j] = vs[k].astype(BF16)
-            remote(pbo.at[i, j], r1o.at[i, chip], o1s.at[i, j], o1r.at[i, chip], (2 * k + core, h)).start()
+            remote(pbo.at[i, j], r1o.at[i, n_c - 2 - j], o1s.at[i, j], o1r.at[i, n_c - 2 - j], (2 * k + core, h)).start()
         acco[i] = vs[chip]
 
     def third_out(i):
         total = acco[i]
         for j, k in enumerate(cpeer):
-            remote(pbo.at[i, j], r1o.at[i, k], o1s.at[i, j], o1r.at[i, k], (2 * k + core, h)).wait_recv()
-            total = total + r1o[i, k].astype(F32)
+            remote(pbo.at[i, j], r1o.at[i, j], o1s.at[i, j], o1r.at[i, j], (2 * k + core, h)).wait_recv()
+            total = total + r1o[i, j].astype(F32)
         acco[i] = total
 
     def drain_out(i):
         for j, k in enumerate(cpeer):
-            remote(pbo.at[i, j], r1o.at[i, chip], o1s.at[i, j], o1r.at[i, chip], (2 * k + core, h)).wait_send()
+            remote(pbo.at[i, j], r1o.at[i, n_c - 2 - j], o1s.at[i, j], o1r.at[i, n_c - 2 - j], (2 * k + core, h)).wait_send()
         drain_z(i, *out_stream)
 
     def among(k, first, count):
         return jnp.logical_and(k >= first, k < first + count)
 
-    def stage_at(k):
-        @pl.when(k < N_OUT)
-        def _():
-            first_out(k)
-
-        @pl.when(jnp.logical_and(k >= N_OUT, k < N_OUT + N_IN))
-        def _():
-            first_in(k - N_OUT)
-
-        @pl.when(jnp.logical_and(k >= 1, k < N_OUT + 1))
-        def _():
-            second_out(k - 1)
-
-        @pl.when(jnp.logical_and(k >= N_OUT + 1, k < N_OUT + N_IN + 1))
-        def _():
-            second_in(k - 1 - N_OUT)
-
-        @pl.when(among(k, THIRD, N_OUT))
-        def _():
-            third_out(k - THIRD)
-
-        @pl.when(among(k, N_OUT + THIRD, N_IN))
-        def _():
-            third_in(k - THIRD - N_OUT)
-
-        for way, lag in ((0, THIRD + HOP * h), (1, THIRD + HOP * (n_h - 1 - h))):
-
-            @pl.when(among(k, lag, N_OUT))
-            def _():
-                along(k - lag, way, *out_stream)
-
-            @pl.when(among(k, N_OUT + lag, N_IN))
-            def _():
-                along(k - lag - N_OUT, way, *in_stream)
-
-    last_stage = N_OUT + N_IN - 1 + THIRD + HOP * (n_h - 2)
+    def early_at(t):
+        return among(t, 0, EARLY), t
+
+    def late_at(t):
+        spaced = LATE + 2 * (X_CHUNK - 2)
+        last = t > spaced
+        item = jnp.where(last, EARLY + X_CHUNK - 2 + t - spaced, EARLY + (t - LATE) // 2)
+        ok = jnp.logical_or(last, (t - LATE) % 2 == 0)
+        return jnp.logical_and(among(t, LATE, spaced + 3 - LATE), ok), item
+
+    def tick(t, phase):
+        def stage(at, lag, on_out, on_in):
+            ok, item = at(t - lag)
+            if on_out is not None:
+                pl.when(jnp.logical_and(ok, item < N_OUT))(lambda: on_out(item))
+                ok = jnp.logical_and(ok, item >= N_OUT)
+            pl.when(ok)(lambda: on_in(item - N_OUT))
+
+        if phase == 0:
+            stage(early_at, 1, second_out, second_in)
+        if phase < 2:
+            stage(early_at, THIRD, third_out if phase == 0 else None, third_in)
+        if phase > 0:
+            stage(late_at, 1, None, second_in)
+            stage(late_at, THIRD_LATE, None, third_in)
+        for at, third, last in ((early_at, THIRD, 2), (late_at, THIRD_LATE, 3)):
+            if at is late_at and phase == 0:
+                continue
+            for way, far in ((0, h), (1, n_h - 1 - h)):
+                stage(
+                    at,
+                    third + HOP * far,
+                    (lambda i, way=way: along(i, way, *out_stream)) if at is early_at else None,
+                    lambda i, way=way: along(i, way, *in_stream),
+                )
+
+    last_tick = LATE + 2 * (X_CHUNK - 2) + 2 + THIRD_LATE + HOP * (n_h - 2)
 
     keep_row = (iota((rows, 1), 0) < left).astype(F32)
     for src, dst in ((nlow[...], nt_p), ((cot[...].astype(F32) * keep_row).astype(BF16), bt_p)):
@@ -1044,7 +1168,6 @@
     flat_rows(second_i, sec_rows, 1.0)
     unpack_rows(prm, rin, rp, gain, taps, heads, None)
     fill_spread(spread)
-    ng[...] = jnp.zeros_like(ng)
     dheads[...] = jnp.zeros_like(dheads)
     dtaps[...] = jnp.zeros_like(dtaps)
     rates = -jnp.exp(heads[1:2, :])
@@ -1060,9 +1183,18 @@
         excl_r[b] = excl
         incl_t[b] = incl.T
         excl_t[b] = excl.T
+        logs3[b] = jnp.concatenate(split3(jnp.concatenate([incl, excl], axis=0)), axis=1)
+        st = steps[at, :]
+        steps2[b] = stacked(st)
+        terms2[b] = stacked(
+            jnp.concatenate([st, jnp.exp(incl), jnp.exp(total - excl), jnp.exp(total - incl), jnp.exp(excl)], axis=0)
+        )
         bc = conv_low[at, INNER:].astype(F32)
         cb = pltpu.roll(bc, STATE, 1)
         inter_s[b] = nt(half_masks(bc)[0].astype(BF16), cb.astype(BF16))
+        bb, cc = bc[:, :STATE].astype(BF16), cb[:, :STATE].astype(BF16)
+        bb2[b] = jnp.concatenate([bb, bb], axis=1)
+        cc2[b] = jnp.concatenate([cc, cc], axis=1)
 
     def pair_body(pair, _):
         cols = pl.ds(pl.multiple_of(pair * LANES, LANES), LANES)
@@ -1070,16 +1202,17 @@
         later = col >= row
         hot = (iota((LANES, 2 * LANES), 0) == 2 * pair + iota((LANES, 2 * LANES), 1) // LANES).astype(BF16)
         hot3 = jnp.concatenate([hot, hot, hot], axis=0)
+        wide_all = nn(logs3[...].reshape(blocks * 2 * SPAN, 3 * LANES), hot3)
+        step_all = nn(steps2[...].reshape(blocks * 2 * SPAN, LANES), sp)
         for b in range(blocks):
             at = slice(b * SPAN, (b + 1) * SPAN)
-            both = jnp.concatenate([incl_r[b], excl_r[b]], axis=0)
-            wide = nn(jnp.concatenate(split3(both), axis=1), hot3)
+            both = slice(b * 2 * SPAN, (b + 1) * 2 * SPAN)
+            wide = wide_all[both]
             inter = inter_s[b]
             inter2 = inter * twice
-            hi, lo = split(steps[at, :])
             xs = conv_low[at, cols].astype(F32)
             dyl = hgrad[at, cols]
-            xh, xl = split((nn(hi, sp) + nn(lo, sp)) * xs)
+            xh, xl = split(halves_sum(step_all[both]) * xs)
             xhs = half_masks(xh)
             xls = half_masks(xl)
             dy2 = jnp.concatenate([dyl, dyl], axis=1)
@@ -1096,7 +1229,7 @@
                 decay = jnp.exp(gap)
                 kern.append(inter2 * decay)
                 weigh = nt(jnp.concatenate([xhs[n], xls[n]], axis=1), dy2) * decay
-                qt = qt + weigh * twice
+                qt = qt + weigh
                 pairs = weigh * inter
                 above = jnp.where(col > row, pairs, 0.0)
                 below = jnp.where(col < row, pairs, 0.0)
@@ -1110,10 +1243,11 @@
             dpre[at, cols] = nn_split(jnp.concatenate(kern, axis=1), jnp.concatenate(dys, axis=0))
         chain.at(pair)
 
-        @pl.when(pair < N_OUT + X_CHUNK)
-        def _():
-            stage_at(pair)
-
+        pl.when(pair < N_OUT)(lambda: first_out(pair))
+        pl.when(among(pair, N_OUT, X_CHUNK))(lambda: first_in(pair - N_OUT))
+        tick(pair, 0)
+        for part in range(normed_parts):
+            pl.when(pair == N_OUT + 2 + part)(lambda part=part: normed_part(0, INNER, part, True))
         return 0
 
     pairs_n = HEADS // 2
@@ -1174,29 +1308,16 @@
         zero_state = jnp.zeros((STATE, CHUNK), BF16)
         for b in range(blocks):
             at = slice(b * SPAN, (b + 1) * SPAN)
-            incl, excl = incl_r[b], excl_r[b]
-            total = incl[SPAN - 1 : SPAN]
-            st = steps[at, :]
-            terms = jnp.concatenate(
-                [st, jnp.exp(incl), jnp.exp(total - excl), jnp.exp(total - incl), jnp.exp(excl)], axis=0
-            )
-            hi, lo = split(terms)
-            wide = nn(hi, sp) + nn(lo, sp)
+            wide = halves_sum(nn(terms2[b], sp))
             st_e, el, eg, tl, ex = [wide[n * SPAN : (n + 1) * SPAN] for n in range(5)]
-            bc = conv_low[at, INNER:].astype(F32)
-            cb = pltpu.roll(bc, STATE, 1)
-            bb = bc[:, :STATE].astype(BF16)
-            cc = cb[:, :STATE].astype(BF16)
-            bb2 = jnp.concatenate([bb, bb], axis=1)
-            cc2 = jnp.concatenate([cc, cc], axis=1)
             xs = conv_low[at, cols].astype(F32)
             dy = hgrad[at, cols].astype(F32)
             xst = st_e * xs
             parts = [split(v) for v in (hin[b, :, cols], gin[b + 1, :, cols], ls[b], ms[b])]
-            into_f = el * nn(cc2, jnp.concatenate(parts[0], axis=0))
-            into_g = eg * nn(cc2, jnp.concatenate(parts[1], axis=0))
-            out_f = tl * nn(bb2, jnp.concatenate(parts[2], axis=0))
-            out_g = ex * nn(bb2, jnp.concatenate(parts[3], axis=0))
+            into_f = el * nn(cc2[b], jnp.concatenate(parts[0], axis=0))
+            into_g = eg * nn(cc2[b], jnp.concatenate(parts[1], axis=0))
+            out_f = tl * nn(bb2[b], jnp.concatenate(parts[2], axis=0))
+            out_g = ex * nn(bb2[b], jnp.concatenate(parts[3], axis=0))
             dxu = dpre[at, cols] + out_f + out_g
             dpre[at, cols] = (st_e * dxu + skip * dy) * slope[at, cols]
             stack = jnp.concatenate([dy * into_f - xst * out_f, dy * into_g - xst * out_g, xs * dxu, xs * dy], axis=0)
@@ -1204,27 +1325,34 @@
             pair_f = jnp.sum(ls[b] * hin[b + 1, :, cols], axis=0, keepdims=True)
             pair_g = jnp.sum(ms[b] * gin[b, :, cols], axis=0, keepdims=True)
             cross[b] += fold(jnp.broadcast_to(pair_f + pair_g, (8, CHUNK)), sp)
-            lefts, rights = [], []
+            acc_bc = dbc[b]
             for scaled, (sh, sl), low in (
                 (xst * tl, parts[2], True),
                 (xst * ex, parts[3], True),
                 (el * dy, parts[0], False),
                 (eg * dy, parts[1], False),
             ):
-                ah, al = split(scaled)
-                for a, v in ((ah, sh), (al, sh), (ah, sl)):
-                    lefts.append(a)
-                    rights.append(jnp.concatenate([v, zero_state] if low else [zero_state, v], axis=0))
-            dbc[b] += nt(jnp.concatenate(lefts, axis=1), jnp.concatenate(rights, axis=1))
+                place = lambda v, low=low: jnp.concatenate([v, zero_state] if low else [zero_state, v], axis=0)
+                two = stacked(scaled)
+                acc_bc = acc_bc + halves_sum(nt(two, place(sh))) + nt(two[:SPAN], place(sl))
+            dbc[b] = acc_bc
 
     def group_body(g, _):
         group_compute(g)
         halo_send(g, CHUNK)
+        tick(pairs_n + 2 * g, 1)
 
         @pl.when(g >= 1)
         def _():
             conv_back(g - 1, CHUNK)
-            stage_at(N_OUT + X_CHUNK + g - 1)
+            first_in(X_CHUNK + g - 1)
+
+        tick(pairs_n + 2 * g + 1, 1)
+
+        @pl.when(g == 4)
+        def _():
+            for part in range(normed_parts):
+                normed_part(INNER, 4 * CHUNK, part, False)
 
         return 0
 
@@ -1234,12 +1362,13 @@
         at = slice(b * SPAN, (b + 1) * SPAN)
         bc = conv_low[at, INNER:].astype(F32)
         cb_lo, cb_hi = half_masks(pltpu.roll(bc, STATE, 1))
-        qt = q_t[b]
+        qt = q_t[b] * twice
         d = dbc[b] + nn_split(qt, cb_lo.astype(BF16)) + nn_split(qt.T, cb_hi.astype(BF16))
         dpre[at, INNER:] = d * slope[at, INNER:]
     halo_send(X_CHUNK, LANES)
     conv_back(X_CHUNK - 1, CHUNK)
-    stage_at(N_OUT + 2 * X_CHUNK - 1)
+    first_in(2 * X_CHUNK - 1)
+    tick(pairs_n + 2 * X_CHUNK, 2)
     for b in range(blocks):
         at = slice(b * SPAN, (b + 1) * SPAN)
         st = steps[at, :]
@@ -1255,8 +1384,11 @@
         dheads[1:2, :] += jnp.sum(da * st, axis=0, keepdims=True) * rates
         dheads[2:3, :] += jnp.sum(rd[3 * SPAN :], axis=0, keepdims=True)
     conv_back(X_CHUNK, LANES)
-    stage_at(N_OUT + N_IN - 1)
-    stage_at(N_OUT + N_IN)
+    first_in(N_IN - 1)
+    tick(pairs_n + 2 * X_CHUNK + 1, 2)
+    for part in range(normed_parts):
+        normed_part(INNER + 4 * CHUNK, 3 * CHUNK, part, False)
+    tick(pairs_n + 2 * X_CHUNK + 2, 2)
 
     ngain[...] = jnp.zeros_like(ngain)
 
@@ -1273,7 +1405,7 @@
         grad_x[at, :] = cot[at, :].astype(F32) + r * (gg - unit * mean)
         return 0
 
-    lax.fori_loop(0, rows // 16, norm_body, 0)
+    lax.fori_loop(0, rows // 16, norm_body, 0, unroll=4)
 
     sends = []
 
@@ -1314,13 +1446,22 @@
     t = HEAD_ROW + INNER // LANES
     sz[h, t : t + 1, :] = jnp.where(lane1 < turn, before, 0.0)
     sz[h, t + 1 :, :] = jnp.zeros((FLAT_ROWS - t - 1, LANES), F32)
-    start(sz, h, zpeer, True, szs, szr)
-
-    def stage_body(k, _):
-        stage_at(k)
+
+    def tick_body(t, _):
+        tick(t, 2)
         return 0
 
-    lax.fori_loop(N_OUT + N_IN + 1, last_stage + 1, stage_body, 0)
+    lax.fori_loop(pairs_n + 2 * X_CHUNK + 3, last_tick + 1, tick_body, 0)
+    share = FLAT_ROWS // n_h
+    part = pl.ds(pl.multiple_of(share * h, 8), share)
+
+    def share_out(j, q):
+        rows_of = pl.ds(pl.multiple_of(share * q, 8), share)
+        return remote(sz.at[h, rows_of], szin.at[h], szs.at[j], szr.at[h], (s, q))
+
+    for j, q in enumerate(zpeer):
+        share_out(j, q).start()
+    szin[h] = sz[h, part]
 
     def window(slots, dst, wide, per, acc, rec, snd, rcv):
         c0 = (per * h) // wide
@@ -1370,7 +1511,7 @@
     for i in range(n_ci + n_ro):
         p1[s, i : i + 1, :] = line[0:1, i * LANES : (i + 1) * LANES]
     start(p1, s, speer, False, p1s, p1r)
-    spl[s] = arrive(sz, zpeer, True, szs, szr)
+    spl[s] = arrive(szin, zpeer, True, szs, szr)
     start(spl, s, speer, False, sps, spr)
     sums = arrive(z1, zpeer, True, z1s, z1r)
     line_r = DECAY * row_in[...].reshape(1, rin) + decay_keep * (sums[0:1, 0:rin] / PROJ + EPS_SQUARE)
@@ -1404,15 +1545,19 @@
     z2[h] = note
     start(z2, h, zpeer, True, z2s, z2r)
 
-    g = arrive(spl, speer, False, sps, spr)
+    sout[h] = arrive(spl, speer, False, sps, spr)
+    start(sout, h, zpeer, True, sos, sor)
+    p2[s] = arrive(z2, zpeer, True, z2s, z2r)
+    start(p2, s, speer, False, p2s, p2r)
+    mean_out = p2[s, 0:1, 2:3] / INNER
+    for j, p in enumerate(zpeer):
+        remote(sout.at[p], sout.at[p], sos.at[j], sor.at[p], (s, p)).wait_recv()
+    g = jnp.concatenate([sout[q] for q in range(n_h)], axis=0)
     sec = DECAY * sec_rows[...] + decay_keep * (g * g + EPS_SQUARE)
     u = g * lax.rsqrt(sec)
     spread_small = jnp.sqrt(jnp.sum(u * u, keepdims=True) / SMALL)
     par = prm[...] - LEARN_SMALL * u / jnp.maximum(1.0, spread_small / CLIP_RMS)
 
-    p2[s] = arrive(z2, zpeer, True, z2s, z2r)
-    start(p2, s, speer, False, p2s, p2r)
-    mean_out = p2[s, 0:1, 2:3] / INNER
     whole, rest = SMALL // LANES, SMALL % LANES
     for v, dst in ((g, small), (sec, second_new), (par, params_new)):
         for i in range(whole):
@@ -1446,6 +1591,8 @@
     clip_out = jnp.maximum(1.0, jnp.sqrt(sums[0:1, 1:2] * mean_out / (INNER * D)) / CLIP_RMS)
     w_in_new[...] = w_in[...] - u_in * (LEARN_RATE * jnp.sqrt(mean_in) / clip_in)
     w_out_new[...] = w_out_t[...] - u_out * (LEARN_RATE * jnp.sqrt(mean_out) / clip_out)
+    for j, q in enumerate(zpeer):
+        share_out(j, q).wait_send()
     for c in sends:
         c.wait_send()
 
@@ -1518,6 +1665,11 @@
             vf(rows + 8, CHUNK),
             vf(rows + HALO, CHUNK),
             tables, tables, tables, tables, tables, tables, tables, tables, tables,
+            vb(blocks, 2 * SPAN, 3 * LANES),
+            vb(blocks, 2 * SPAN, LANES),
+            vb(blocks, 10 * SPAN, LANES),
+            vb(blocks, SPAN, LANES),
+            vb(blocks, SPAN, LANES),
             vf(blocks, 4 * SPAN, LANES),
             vf(blocks, 8, LANES),
             tables,
@@ -1529,16 +1681,18 @@
             vf(SLOTS, half, OUT_CHUNK),
             vf(n_c, rp, OUT_CHUNK),
             vb(N_IN, n_c - 1, rp, CHUNK),
-            vb(N_IN, n_c, rp, CHUNK),
+            vb(N_IN, n_c - 1, rp, CHUNK),
             vf(N_IN, rp, CHUNK),
             vf(N_IN, 2, 2, rp, CHUNK),
             vb(N_OUT, n_c - 1, rp, OUT_CHUNK),
-            vb(N_OUT, n_c, rp, OUT_CHUNK),
+            vb(N_OUT, n_c - 1, rp, OUT_CHUNK),
             vf(N_OUT, rp, OUT_CHUNK),
             vf(N_OUT, out_dup, 2, rp, OUT_CHUNK),
             vf(rp, in_slots * CHUNK),
             vf(n_h, FLAT_ROWS, LANES),
-            vf(n_s, FLAT_ROWS, LANES),
+            vf(n_h, FLAT_ROWS // n_h, LANES),
+            vf(n_s, FLAT_ROWS // n_h, LANES),
+            vf(n_h, FLAT_ROWS // n_h, LANES),
             vf(n_h, 8, LANES),
             vf(n_s, n_rows, LANES),
             vf(n_h, 8, LANES),
@@ -1549,7 +1703,7 @@
         + [dma((X_CHUNK + 1,))] * 2
         + [dma((N_IN,)), dma((N_IN,)), dma((N_IN, n_c)), dma((N_IN, n_c)), dma((N_IN, 2, 2)), dma((N_IN, 2, 2))]
         + [dma((N_OUT,)), dma((N_OUT,)), dma((N_OUT, n_c)), dma((N_OUT, n_c)), dma((N_OUT, out_dup, 2)), dma((N_OUT, out_dup, 2))]
-        + [dma((8,))]
+        + [dma((8,)), dma((n_h,)), dma((n_h,))]
         + [dma((n_h,)), dma((n_h,)), dma((n_s,)), dma((n_s,))] * 3,
         compiler_params=pltpu.CompilerParams(
             collective_id=2, has_side_effects=True, vmem_limit_bytes=REAR_VMEM
@@ -1558,7 +1712,25 @@
     )(*args)
 
 
-REAR_VMEM = 63 << 20
+REAR_VMEM = (63 << 20) + (1 << 19)
+
+
+def results_kernel(*refs):
+    count = len(refs) // 2
+    for n in range(count):
+        refs[count + n][...] = refs[n][...]
+
+
+def results(*arrays):
+    vm = pl.BlockSpec(memory_space=pltpu.VMEM)
+    return pl.pallas_call(
+        results_kernel,
+        out_shape=tuple(jax.ShapeDtypeStruct(a.shape, a.dtype) for a in arrays),
+        in_specs=[vm] * len(arrays),
+        out_specs=(vm,) * len(arrays),
+        compiler_params=pltpu.CompilerParams(vmem_limit_bytes=63 << 20),
+        name="results",
+    )(*arrays)
 
 
 def on_device(
@@ -1600,6 +1772,13 @@
         x, cot, small_params, lengths, w_full, nlow, dgate, glow, conv_low, hgrad, steps, raw, slope, conv_in, hin, gin, lst, mst,
         dev2, decb, dec, og_part, w_in, w_out_t, row_in, col_in, row_out, col_out, small_second,
     )
+    (
+        result, grad_x, grad_in, row_in_new, col_in_new, w_in_new, grad_out, row_out_new, col_out_new, w_out_new, small,
+        second_new, params_new,
+    ) = results(
+        result, grad_x, grad_in, row_in_new, col_in_new, w_in_new, grad_out, row_out_new, col_out_new, w_out_new, small,
+        second_new, params_new,
+    )
     return (
         cut(result, 1), cut(grad_x, 1), grad_in, row_in_new, col_in_new, w_in_new, grad_out.T, row_out_new, col_out_new,
         w_out_new.T, small, second_new, params_new,

time: 228 us -> 205 us (0.90)
  Pallas kernels: 217 us -> 204 us
  local copies, waits for them, and re-layouts: 9.51 us -> 0 us
    pallas_call x1, Pallas kernels: 116 us -> 106 us  [rear(): pl.pallas_call(functools.partial(rear_kernel, n_s, n_h, cph, oph, rin, rp...]
    unnamed x39 -> x0, local copies, waits for them, and re-layouts: 9.51 us -> none
    pallas_call x1, Pallas kernels: 101 us -> 94.6 us  [fore(): pl.pallas_call(functools.partial(fore_kernel, n_s, n_h, cph, oph, rin, rp...]
    pallas_call x0 -> x1, Pallas kernels: none -> 3.4 us  [results(): pl.pallas_call(results_kernel, out_shape=tuple((jax.ShapeDtypeStruct(a.sh...]
where the time goes in v4:
time: 205 us
  Pallas kernels  204 us (100%)
    pallas_call x1, Pallas kernels, rear(): pl.pallas_call(functools.partial(rear_kernel, n_s, n_h, cph, oph, rin, rp...  106 us
    pallas_call x1, Pallas kernels, fore(): pl.pallas_call(functools.partial(fore_kernel, n_s, n_h, cph, oph, rin, rp...  94.6 us

profile of v4, /device:TPU:0, one launch (start us, length us, event | category | flops | bytes accessed | tf_op | source)
XLA Modules:
  0.0 205.1 jit_solution(1997054579775609041)
XLA Ops:
  1.3 94.6 %fore.1 = (bf16[384,768]{1,0:T(8,128)(2,1)}, bf16[768,3328]{1,0:T(8,128)(2,1)}, bf16[384,768]{1,0:T(8,128)(2,1)}, bf16[400,1664]{1,0:T(8,128)(2,1)}, bf16[384,16...) custom-call(bf16[384,768]{1,0:T(8,128)(2,1)} %x.3, ...), custom_call_target="tpu_custom_call" | custom-call | tf_op jit(solution)/shard_map/fore/pallas_call | solution.py:867
  95.9 105.6 %rear.1 = (f32[384,768]{1,0:T(8,128)}, f32[96,806]{1,0:T(8,128)}, f32[96]{0:T(128)}, f32[806]{0:T(1024)}, f32[96,806]{1,0:T(8,128)}, /*index=5*/f32[96,384]{1,0:...) custom-call(bf16[384,768]{1,0:T(8,128)(2,1)} %x.3, ...), custom_call_target="tpu_custom_call" | custom-call | tf_op jit(solution)/shard_map/rear/pallas_call | solution.py:1625
  201.5 3.4 %results.1 = (bf16[384,768]{1,0:T(8,128)(2,1)}, f32[384,768]{1,0:T(8,128)}, f32[96,806]{1,0:T(8,128)}, f32[96]{0:T(128)}, f32[806]{0:T(1024)}, /*index=5*/f32[96...) custom-call(bf16[384,768]{1,0:T(8,128)(2,1)} %get-tuple-element.57.r, ...), custom_call_target="tpu_custom_call" | custom-call | tf_op jit(solution)/shard_map/results/pallas_call | solution.py:1726

commit v5 on v4

--- a/solution.py
+++ b/solution.py
@@ -111,7 +111,7 @@
     return incl, incl - logs, incl[SPAN - 1 : SPAN]
 
 
-CHAIN_PARTS = 4
+CHAIN_PARTS = 6
 
 
 class Chain:
@@ -125,23 +125,25 @@
         self.last = (h == n_h - 1, h == 0)
 
     def link(self, d, c):
-        width = STATE // CHAIN_PARTS
+        width = INNER // CHAIN_PARTS
         at = pl.ds(c * width, width)
         snd, rcv = self.sems[d]
-        return remote(self.snd.at[d, at], self.out.at[d, at], snd.at[c], rcv.at[c], (self.s, self.next[d]))
-
-    def begin(self):
+        return remote(self.snd.at[d, :, at], self.out.at[d, :, at], snd.at[c], rcv.at[c], (self.s, self.next[d]))
+
+    def begin(self, parts):
+        width = INNER // CHAIN_PARTS
         for d in range(2):
 
             @pl.when(self.first[d])
             def _():
-                self.out[d] = jnp.zeros((STATE, INNER), F32)
-                self.snd[d] = self.dev[d]
-                for c in range(CHAIN_PARTS):
+                for c in parts:
+                    at = slice(c * width, (c + 1) * width)
+                    self.out[d, :, at] = jnp.zeros((STATE, width), F32)
+                    self.snd[d, :, at] = self.dev[d, :, at]
                     self.link(d, c).start()
 
     def step(self, d, c):
-        width = STATE // CHAIN_PARTS
+        width = INNER // CHAIN_PARTS
         at = slice(c * width, (c + 1) * width)
 
         @pl.when(jnp.logical_not(self.first[d]))
@@ -150,7 +152,7 @@
 
         @pl.when(self.inner)
         def _():
-            self.snd[d, at] = self.out[d, at] * self.dec[0:1] + self.dev[d, at]
+            self.snd[d, :, at] = self.out[d, :, at] * self.dec[0:1, at] + self.dev[d, :, at]
             self.link(d, c).start()
 
     def at(self, k, stride=2):
@@ -245,7 +247,8 @@
 
 
 class Gather:
-    def __init__(self, n_s, n_h, s, h, full, base, count, parts, sems):
+    def __init__(self, n_s, n_h, s, h, full, base, count, parts, sems, gap=3):
+        self.gap = gap
         self.n_s, self.n_h, self.s, self.h, self.full = n_s, n_h, s, h, full
         self.base, self.count, self.parts = base, count, parts
         self.zs, self.zr, self.ps, self.pr, self.ds, self.dr, self.cs, self.cr = sems
@@ -293,8 +296,8 @@
         q, p = item
         return remote(ref, ref, self.zs.at[q - self.base, p, way], self.zr.at[q - self.base, p], (self.s, to))
 
-    def begin(self):
-        for p in range(len(self.parts)):
+    def begin(self, chosen=None):
+        for p in range(len(self.parts)) if chosen is None else chosen:
             item = (self.h, p)
             mine = jnp.logical_and(self.h >= self.base, self.h < self.base + self.count)
             if self.parts[p][1] is not None:
@@ -407,18 +410,19 @@
 
     def plan(self, columns):
         count, parts = len(self.items), len(self.parts)
+        gap = self.gap
         plan = []
-        for i in range(count + 3):
+        for i in range(count + 3 * gap):
             if i < count:
                 plan.append(run_all(lambda i=i: self.z_in(i), lambda i=i: self.spread_out(i)))
-            if 1 <= i <= count:
-                plan.append(lambda i=i: self.pass_on(i - 1))
-            if 2 <= i <= count + 1:
-                plan.append(lambda i=i: self.last_in(i - 2))
-            if 3 <= i:
-                plan.append(lambda i=i: self.complete(i - 3))
-                if (i - 3) % parts == parts - 1 and columns is not None:
-                    plan.append(lambda i=i: columns(self.order[(i - 3) // parts]))
+            if gap <= i < count + gap:
+                plan.append(lambda i=i: self.pass_on(i - gap))
+            if 2 * gap <= i < count + 2 * gap:
+                plan.append(lambda i=i: self.last_in(i - 2 * gap))
+        for i in range(count):
+            plan.append(lambda i=i: self.complete(i))
+            if i % parts == parts - 1 and columns is not None:
+                plan.append(lambda i=i: columns(self.order[i // parts]))
         return plan
 
     def finish(self):
@@ -457,7 +461,7 @@
     counts = [first[q + 1] - first[q] for q in range(parts)]
     common = max(counts[:-1])
     mid = (common + 1) // 2
-    ranges = [(slice(0, mid * LANES), None), (slice(mid * LANES, common * LANES), None)]
+    ranges = [(slice(mid * LANES, common * LANES), None), (slice(0, mid * LANES), None)]
     if counts[-1] > common:
         ranges.append((slice(common * LANES, counts[-1] * LANES), parts - 1))
     return ranges, max(counts) * LANES
@@ -469,7 +473,7 @@
     result, w_full_o, nlow_o, conv_in_o, conv_low_o, slope_o, raw, steps, decb, dec, dgate, hgrad, glow, dgain, lst, mst,
     dev2, hin_o, gin_o,
     full, w_full, o_full, xh, shift_in, edge_out, edge_in, shift_out, nscr, conv_in, conv_low, slope, cf, gate, hst, gst, dev, into, csnd, incl_r,
-    excl_r, incl_t, excl_t, steps_t, inter_s, yb, el, eg, gg_scr, hin, gin, prm, gain, taps, heads, out_gain, spread, logs3, el_eg, cc2,
+    excl_r, incl_t, excl_t, steps_t, inter_s, yb, el, eg, gg_scr, hin, gin, prm, gain, taps, heads, out_gain, spread, logs3, el_eg, cc2, tot2, wfg, bts,
     xs_, xr_, es_, er_, us, ur, dws, dwr, outs, *gsems,
 ):
     s = lax.axis_index("seq")
@@ -525,12 +529,14 @@
     def _():
         edge.start()
 
+    g_high.begin([0])
+
     @pl.when(h > 0)
     def _():
         edge.wait_recv()
         full[h, s, :, 0:LANES] += edge_in[...]
 
-    g_high.begin()
+    g_high.begin(range(1, len(parts)))
     halo = remote(x.at[rows - HALO : rows], xh, xs_.at[0], xr_.at[0], (s, up))
 
     @pl.when(h < n_h - 1)
@@ -612,10 +618,11 @@
 
         lax.fori_loop((cph * q) // LANES, hi, tile_body, 0)
 
-    for step in high_plan[1:]:
+    for n, step in enumerate(high_plan[1:]):
         step()
-    g_low.begin()
-    g_out.begin()
+        if n == 9:
+            g_low.begin()
+            g_out.begin()
     for n, (src, dst) in enumerate(((conv_in, conv_in_o), (conv_low, conv_low_o), (slope, slope_o))):
         leaving.append(leave(src, dst, n + 1))
         leaving[-1].start()
@@ -645,27 +652,32 @@
         inter_s[b] = nt(c_low, bc.astype(BF16)) * (1.0 + (iota((SPAN, SPAN), 0) == iota((SPAN, SPAN), 1)).astype(F32))
         cc = cb[:, :STATE].astype(BF16)
         cc2[b] = jnp.concatenate([cc, cc], axis=1)
-        tot = jnp.broadcast_to(jnp.exp(total), (8, LANES))
-        for g in range(INNER // 256):
-            cols = slice(g * 256, (g + 1) * 256)
-            sp = spread[:, cols]
+        tot2[b] = stacked(jnp.broadcast_to(jnp.exp(total), (8, LANES)))
+        wfg[b] = wide
+        bts[b] = bt2
+    chain = Chain(n_h, s, h, dev, dec, into, csnd, us, ur, dws, dwr)
+    for g in range(CHAIN_PARTS):
+        cols = slice(g * 256, (g + 1) * 256)
+        sp = spread[:, cols]
+        weights_all = nn(wfg[...].reshape(blocks * 4 * SPAN, LANES), sp)
+        totals = nn(tot2[...].reshape(blocks * 16, LANES), sp)
+        for b in range(blocks):
+            at = slice(b * SPAN, (b + 1) * SPAN)
             xs = conv_low[at, cols].astype(F32)
-            w = halves_sum(nn(wide, sp))
+            w = halves_sum(weights_all[b * 4 * SPAN : (b + 1) * 4 * SPAN])
             for n, dst in ((0, hst), (1, gst)):
-                hi, lo = split(w[n * SPAN : (n + 1) * SPAN] * xs)
-                dst[b, :, cols] = nn(bt2, jnp.concatenate([hi, lo], axis=0))
-            decb[b, :, cols] = expand(tot, sp)
-    hv, gv, dv = hst[0], gst[blocks - 1], decb[0]
-    for b in range(1, blocks):
-        hv = hv * decb[b, 0:1, :] + hst[b]
-        dv = dv * decb[b]
-    for b in range(blocks - 2, -1, -1):
-        gv = gv * decb[b, 0:1, :] + gst[b]
-    dev[0] = hv
-    dev[1] = gv
-    dec[...] = dv
-    chain = Chain(n_h, s, h, dev, dec, into, csnd, us, ur, dws, dwr)
-    chain.begin()
+                dst[b, :, cols] = nn(bts[b], stacked(w[n * SPAN : (n + 1) * SPAN] * xs))
+            decb[b, :, cols] = halves_sum(totals[b * 16 : (b + 1) * 16])
+        hv, gv, dv = hst[0, :, cols], gst[blocks - 1, :, cols], decb[0, :, cols]
+        for b in range(1, blocks):
+            hv = hv * decb[b, 0:1, cols] + hst[b, :, cols]
+            dv = dv * decb[b, :, cols]
+        for b in range(blocks - 2, -1, -1):
+            gv = gv * decb[b, 0:1, cols] + gst[b, :, cols]
+        dev[0, :, cols] = hv
+        dev[1, :, cols] = gv
+        dec[:, cols] = dv
+        chain.begin([g])
 
     row = iota((SPAN, SPAN), 0)
     col = iota((SPAN, SPAN), 1)
@@ -703,16 +715,20 @@
 
     low_plan = g_low.plan(None)
     out_plan = g_out.plan(None)
+    pairs_n = HEADS // 2
+    gates_n = INNER // LANES
     behind = []
     for n in range(max(len(low_plan), len(out_plan))):
         behind += low_plan[n : n + 1] + out_plan[n : n + 1]
-    pairs_n = HEADS // 2
+    out_plan = []
     lax.fori_loop(0, pairs_n, pair_body, 0)
 
     def gate_tiles(q):
         def tile_body(t, _):
             tile_of(q, t)
             chain.at(pairs_n + t, 3)
+            for n, step in enumerate(out_plan):
+                pl.when(t == n * gates_n // len(out_plan))(step)
             return 0
 
         lax.fori_loop((cph * q) // LANES, (cph * (q + 1)) // LANES, tile_body, 0)
@@ -905,6 +921,9 @@
             vb(blocks, 2 * SPAN, 3 * LANES),
             vb(blocks, 4 * SPAN, LANES),
             vb(blocks, SPAN, LANES),
+            vb(blocks, 16, LANES),
+            vb(blocks, 4 * SPAN, LANES),
+            vb(blocks, STATE, 2 * SPAN),
             dma((1,)),
             dma((1,)),
             dma((1,)),
@@ -951,10 +970,10 @@
     w_full, slope, conv_in, hin, gin, lst, mst, prm, sec_rows, gain, taps, heads, spread,
     adj, csnd, nt_p, bt_p, pg, ng, dpre, halo, dfs, cfs, incl_r, excl_r, incl_t, excl_t, q_t, at_f, at_g, back_f, back_g,
     logs3, steps2, terms2, bb2, cc2, red, cross, dbc, dheads, dtaps, ngain, inter_s,
-    sb, r0, vs, pbi, r1i, acci, r2i, pbo, r1o, acco, r2o, win,
+    sb, r0, vs, pbi, r1i, acci, r2i, pbo, r1o, acco, r2o, win, zb, r2b,
     sz, szin, spl, sout, z1, p1, z2, p2, line,
     us, ur, ds, dr, hs, hr, s0s, s0r, s1s, s1r, s2s, s2r, o0s, o0r, o1s, o1r, o2s, o2r,
-    load, sos, sor, szs, szr, sps, spr, z1s, z1r, p1s, p1r, z2s, z2r, p2s, p2r,
+    load, zbs, zbr, sos, sor, szs, szr, sps, spr, z1s, z1r, p1s, p1r, z2s, z2r, p2s, p2r,
 ):
     s = lax.axis_index("seq")
     h = lax.axis_index("head")
@@ -976,10 +995,7 @@
         pl.semaphore_signal(bar, inc=1, device_id=(s, z), device_id_type=MESH)
     for p in speer:
         pl.semaphore_signal(bar, inc=1, device_id=(p, h), device_id_type=MESH)
-    pl.semaphore_wait(bar, n_h + n_s - 2)
-
     chain = Chain(n_h, s, h, dev, dec, adj, csnd, us, ur, ds, dr)
-    chain.begin()
     pairs_of = (
         (dgate_i, pg.at[:, 0:INNER]), (w_full_i, w_full), (slope_i, slope), (hin_i, hin), (gin_i, gin), (lst_i, lst), (mst_i, mst),
         (conv_in_i, conv_in),
@@ -988,6 +1004,12 @@
     for c in loads:
         c.start()
     left = lengths[0] - h * rows
+    flat_rows(flat, prm, 0.0)
+    flat_rows(second_i, sec_rows, 1.0)
+    unpack_rows(prm, rin, rp, gain, taps, heads, None)
+    fill_spread(spread)
+    pl.semaphore_wait(bar, n_h + n_s - 2)
+    chain.begin(range(CHAIN_PARTS))
 
     def over_in(i):
         own = pl.ds(0, CHUNK)
@@ -1072,6 +1094,21 @@
                 rec[i, n, way] += acc[i]
                 make(rec.at[i, n, way]).start()
 
+    def straight(i):
+        z = i - X_CHUNK
+        zb[z] = acci[i].astype(BF16)
+        for n, q, real in straight_to(i):
+            pl.when(real)(lambda n=n, q=q: remote(zb.at[z], r2b.at[h, z], zbs.at[z, n], zbr.at[h, z], (s, q)).start())
+
+    def straight_to(i):
+        one, two = owners(i, CHUNK, cph)
+        return ((0, one, one != h), (1, two, jnp.logical_and(two != one, two != h)))
+
+    def drain_straight(i):
+        z = i - X_CHUNK
+        for n, q, real in straight_to(i):
+            pl.when(real)(lambda n=n, q=q: remote(zb.at[z], r2b.at[h, z], zbs.at[z, n], zbr.at[h, z], (s, q)).wait_send())
+
     def drain_z(i, *stream):
         for _, sends_it, _, make, n in links(i, *stream):
 
@@ -1085,7 +1122,8 @@
     def drain_in(i):
         for j, k in enumerate(cpeer):
             remote(pbi.at[i, j], r1i.at[i, n_c - 2 - j], s1s.at[i, j], s1r.at[i, n_c - 2 - j], (2 * k + core, h)).wait_send()
-        drain_z(i, *in_stream)
+        pl.when(i < X_CHUNK)(lambda: drain_z(i, *in_stream))
+        pl.when(i >= X_CHUNK)(lambda: drain_straight(i))
 
     def first_out(i):
         @pl.when(i >= 2)
@@ -1145,29 +1183,22 @@
             stage(early_at, THIRD, third_out if phase == 0 else None, third_in)
         if phase > 0:
             stage(late_at, 1, None, second_in)
-            stage(late_at, THIRD_LATE, None, third_in)
-        for at, third, last in ((early_at, THIRD, 2), (late_at, THIRD_LATE, 3)):
-            if at is late_at and phase == 0:
-                continue
-            for way, far in ((0, h), (1, n_h - 1 - h)):
-                stage(
-                    at,
-                    third + HOP * far,
-                    (lambda i, way=way: along(i, way, *out_stream)) if at is early_at else None,
-                    lambda i, way=way: along(i, way, *in_stream),
-                )
-
-    last_tick = LATE + 2 * (X_CHUNK - 2) + 2 + THIRD_LATE + HOP * (n_h - 2)
+            stage(late_at, THIRD_LATE, None, lambda i: (third_in(i), straight(i))[0])
+        for way, far in ((0, h), (1, n_h - 1 - h)):
+            stage(
+                early_at,
+                THIRD + HOP * far,
+                lambda i, way=way: along(i, way, *out_stream),
+                lambda i, way=way: along(i, way, *in_stream),
+            )
+
+    last_tick = max(LATE + 2 * (X_CHUNK - 2) + 2 + THIRD_LATE, EARLY - 1 + THIRD + HOP * (n_h - 2))
 
     keep_row = (iota((rows, 1), 0) < left).astype(F32)
     for src, dst in ((nlow[...], nt_p), ((cot[...].astype(F32) * keep_row).astype(BF16), bt_p)):
         turned = src.T
         for q in range(n_s):
             dst[q % 2, (q // 2) * rp : (q // 2 + 1) * rp, :] = turned[q * rp : (q + 1) * rp]
-    flat_rows(flat, prm, 0.0)
-    flat_rows(second_i, sec_rows, 1.0)
-    unpack_rows(prm, rin, rp, gain, taps, heads, None)
-    fill_spread(spread)
     dheads[...] = jnp.zeros_like(dheads)
     dtaps[...] = jnp.zeros_like(dtaps)
     rates = -jnp.exp(heads[1:2, :])
@@ -1471,12 +1502,23 @@
             at = slice(c * wide, (c + 1) * wide)
             dst[:, at] = acc[index]
             n = jnp.where(owners(index, wide, per)[0] == h, 0, 1) if rec.shape[1] > 1 else 0
+            held = jnp.minimum(index, rec.shape[0] - 1)
             for way, there in ((0, h > 0), (1, h < n_h - 1)):
 
-                @pl.when(jnp.logical_and(c0 + c < c1, there))
+                @pl.when(jnp.logical_and(jnp.logical_and(c0 + c < c1, index < rec.shape[0]), there))
                 def _():
-                    remote(acc.at[index], rec.at[index, n, way], snd.at[0, 0, 0], rcv.at[index, n, way], (s, up)).wait_recv()
-                    dst[:, at] += rec[index, n, way]
+                    remote(acc.at[index], rec.at[held, n, way], snd.at[0, 0, 0], rcv.at[held, n, way], (s, up)).wait_recv()
+                    dst[:, at] += rec[held, n, way]
+
+            if rec.shape[0] == acc.shape[0]:
+                continue
+            late = jnp.maximum(index - X_CHUNK, 0)
+
+            @pl.when(jnp.logical_and(c0 + c < c1, index >= X_CHUNK))
+            def _():
+                for z in zpeer:
+                    remote(zb.at[late], r2b.at[z, late], zbs.at[0, 0], zbr.at[z, late], (s, z)).wait_recv()
+                    dst[:, at] += r2b[z, late].astype(F32)
 
     wi = in_slots * CHUNK
     window(in_slots, win, *in_stream)
@@ -1683,12 +1725,14 @@
             vb(N_IN, n_c - 1, rp, CHUNK),
             vb(N_IN, n_c - 1, rp, CHUNK),
             vf(N_IN, rp, CHUNK),
-            vf(N_IN, 2, 2, rp, CHUNK),
+            vf(X_CHUNK, 2, 2, rp, CHUNK),
             vb(N_OUT, n_c - 1, rp, OUT_CHUNK),
             vb(N_OUT, n_c - 1, rp, OUT_CHUNK),
             vf(N_OUT, rp, OUT_CHUNK),
             vf(N_OUT, out_dup, 2, rp, OUT_CHUNK),
             vf(rp, in_slots * CHUNK),
+            vb(N_IN - X_CHUNK, rp, CHUNK),
+            vb(n_h, N_IN - X_CHUNK, rp, CHUNK),
             vf(n_h, FLAT_ROWS, LANES),
             vf(n_h, FLAT_ROWS // n_h, LANES),
             vf(n_s, FLAT_ROWS // n_h, LANES),
@@ -1701,9 +1745,9 @@
         ]
         + [dma((CHAIN_PARTS,))] * 4
         + [dma((X_CHUNK + 1,))] * 2
-        + [dma((N_IN,)), dma((N_IN,)), dma((N_IN, n_c)), dma((N_IN, n_c)), dma((N_IN, 2, 2)), dma((N_IN, 2, 2))]
+        + [dma((N_IN,)), dma((N_IN,)), dma((N_IN, n_c)), dma((N_IN, n_c)), dma((X_CHUNK, 2, 2)), dma((X_CHUNK, 2, 2))]
         + [dma((N_OUT,)), dma((N_OUT,)), dma((N_OUT, n_c)), dma((N_OUT, n_c)), dma((N_OUT, out_dup, 2)), dma((N_OUT, out_dup, 2))]
-        + [dma((8,)), dma((n_h,)), dma((n_h,))]
+        + [dma((8,)), dma((N_IN - X_CHUNK, 2)), dma((n_h, N_IN - X_CHUNK)), dma((n_h,)), dma((n_h,))]
         + [dma((n_h,)), dma((n_h,)), dma((n_s,)), dma((n_s,))] * 3,
         compiler_params=pltpu.CompilerParams(
             collective_id=2, has_side_effects=True, vmem_limit_bytes=REAR_VMEM

time: 205 us -> 186 us (0.907)
  Pallas kernels: 204 us -> 184 us
    pallas_call x1, Pallas kernels: 106 us -> 93.5 us  [rear(): pl.pallas_call(functools.partial(rear_kernel, n_s, n_h, cph, oph, rin, rp...]
    pallas_call x1, Pallas kernels: 94.6 us -> 87.2 us  [fore(): pl.pallas_call(functools.partial(fore_kernel, n_s, n_h, cph, oph, rin, rp...]
where the time goes in v5:
time: 186 us
  Pallas kernels  184 us (99%)
    pallas_call x1, Pallas kernels, rear(): pl.pallas_call(functools.partial(rear_kernel, n_s, n_h, cph, oph, rin, rp...  93.5 us
    pallas_call x1, Pallas kernels, fore(): pl.pallas_call(functools.partial(fore_kernel, n_s, n_h, cph, oph, rin, rp...  87.2 us

profile of v5, /device:TPU:0, one launch (start us, length us, event | category | flops | bytes accessed | tf_op | source)
XLA Modules:
  0.0 185.6 jit_solution(10719045324854712475)
XLA Ops:
  1.3 87.2 %fore.1 = (bf16[384,768]{1,0:T(8,128)(2,1)}, bf16[768,3328]{1,0:T(8,128)(2,1)}, bf16[384,768]{1,0:T(8,128)(2,1)}, bf16[400,1664]{1,0:T(8,128)(2,1)}, bf16[384,16...) custom-call(bf16[384,768]{1,0:T(8,128)(2,1)} %x.3, ...), custom_call_target="tpu_custom_call" | custom-call | tf_op jit(solution)/shard_map/fore/pallas_call | solution.py:883
  88.5 93.5 %rear.1 = (f32[384,768]{1,0:T(8,128)}, f32[96,806]{1,0:T(8,128)}, f32[96]{0:T(128)}, f32[806]{0:T(1024)}, f32[96,806]{1,0:T(8,128)}, /*index=5*/f32[96,384]{1,0:...) custom-call(bf16[384,768]{1,0:T(8,128)(2,1)} %x.3, ...), custom_call_target="tpu_custom_call" | custom-call | tf_op jit(solution)/shard_map/rear/pallas_call | solution.py:1667
  182.0 3.4 %results.1 = (bf16[384,768]{1,0:T(8,128)(2,1)}, f32[384,768]{1,0:T(8,128)}, f32[96,806]{1,0:T(8,128)}, f32[96]{0:T(128)}, f32[806]{0:T(1024)}, /*index=5*/f32[96...) custom-call(bf16[384,768]{1,0:T(8,128)(2,1)} %get-tuple-element.57.r, ...), custom_call_target="tpu_custom_call" | custom-call | tf_op jit(solution)/shard_map/results/pallas_call | solution.py:1770

commit v6 on v5

--- a/solution.py
+++ b/solution.py
@@ -724,14 +724,22 @@
     lax.fori_loop(0, pairs_n, pair_body, 0)
 
     def gate_tiles(q):
-        def tile_body(t, _):
-            tile_of(q, t)
+        t0, t1 = (cph * q) // LANES, (cph * (q + 1)) // LANES
+
+        def two_tiles(n, _):
+            t = t0 + 2 * n
+            here = pl.ds(pl.multiple_of(t * LANES, LANES), 2 * LANES)
+            weights = full[q, :, :, pl.ds(pl.multiple_of(2 * n * LANES, LANES), 2 * LANES)].reshape(dp, 2 * LANES)
+            w_full[:, here] = weights
+            gate[:, here] = nn(nscr[HALO:, :], weights).astype(BF16)
             chain.at(pairs_n + t, 3)
-            for n, step in enumerate(out_plan):
-                pl.when(t == n * gates_n // len(out_plan))(step)
+            chain.at(pairs_n + t + 1, 3)
             return 0
 
-        lax.fori_loop((cph * q) // LANES, (cph * (q + 1)) // LANES, tile_body, 0)
+        lax.fori_loop(0, (t1 - t0) // 2, two_tiles, 0)
+        if (t1 - t0) % 2:
+            tile_of(q, t1 - 1)
+            chain.at(pairs_n + t1 - 1, 3)
 
     for q in range(half_h):
         gate_tiles(q)
@@ -795,7 +803,7 @@
         dgate[at, :] = (dg * hv * (sg * (1.0 + z * (1.0 - sg)))).astype(BF16)
         return 0
 
-    lax.fori_loop(0, rows // 16, gate_body, 0, unroll=2)
+    lax.fori_loop(0, rows // 16, gate_body, 0, unroll=4)
     for g in range(dp // 256):
         cols = slice(g * 256, (g + 1) * 256)
         branch = nt(glow[...], o_full[cols, :])
@@ -956,7 +964,7 @@
 SLOTS = 4
 THIRD = 6
 THIRD_LATE = 3
-HOP = 2
+HOP = 4
 EARLY = N_OUT + X_CHUNK
 LATE = HEADS // 2 + 3
 
@@ -1478,11 +1486,6 @@
     sz[h, t : t + 1, :] = jnp.where(lane1 < turn, before, 0.0)
     sz[h, t + 1 :, :] = jnp.zeros((FLAT_ROWS - t - 1, LANES), F32)
 
-    def tick_body(t, _):
-        tick(t, 2)
-        return 0
-
-    lax.fori_loop(pairs_n + 2 * X_CHUNK + 3, last_tick + 1, tick_body, 0)
     share = FLAT_ROWS // n_h
     part = pl.ds(pl.multiple_of(share * h, 8), share)
 
@@ -1520,30 +1523,38 @@
                     remote(zb.at[late], r2b.at[z, late], zbs.at[0, 0], zbr.at[z, late], (s, z)).wait_recv()
                     dst[:, at] += r2b[z, late].astype(F32)
 
-    wi = in_slots * CHUNK
-    window(in_slots, win, *in_stream)
-    g_in = pltpu.roll(win[...], lax.rem(wi - lax.rem(cph * h, CHUNK), wi), 1)[0:rin, :cph]
+    def tick_body(t, _):
+        tick(t, 2)
+        return 0
+
+    lax.fori_loop(pairs_n + 2 * X_CHUNK + 3, last_tick + 1, tick_body, 0)
     window(1, win, *out_stream)
     g_out = win[0:rin, 0:OUT_CHUNK]
     if oph != OUT_CHUNK:
         g_out = pltpu.roll(g_out, lax.rem(OUT_CHUNK - lax.rem(oph * h, OUT_CHUNK), OUT_CHUNK), 1)[:, :oph]
+    grad_out[...] = g_out
+    fill = jnp.zeros((LANES - rin, LANES), F32)
+
+    def row_sums(squares):
+        wide = jnp.broadcast_to(jnp.sum(squares, axis=1, keepdims=True), (rin, LANES))
+        return jnp.concatenate([wide, fill], axis=0).T[0:8]
+
+    sq_out = g_out * g_out
+    line_out = row_sums(sq_out)
+    rs_out = jnp.sum(sq_out, axis=0, keepdims=True)
+    spl[s] = arrive(szin, zpeer, True, szs, szr)
+    start(spl, s, speer, False, sps, spr)
+    wi = in_slots * CHUNK
+    window(in_slots, win, *in_stream)
+    g_in = pltpu.roll(win[...], lax.rem(wi - lax.rem(cph * h, CHUNK), wi), 1)[0:rin, :cph]
     grad_in[...] = g_in
-    grad_out[...] = g_out
 
     decay_keep = 1.0 - DECAY
     sq_in = g_in * g_in
-    sq_out = g_out * g_out
-    fill = jnp.zeros((LANES - rin, LANES), F32)
-    line_in = jnp.concatenate(
-        [jnp.broadcast_to(jnp.sum(sq_in, axis=1, keepdims=True), (rin, LANES)), fill], axis=0
-    ).T[0:8]
-    line_out = jnp.concatenate(
-        [jnp.broadcast_to(jnp.sum(sq_out, axis=1, keepdims=True), (rin, LANES)), fill], axis=0
-    ).T[0:8]
+    line_in = row_sums(sq_in)
     z1[h] = jnp.where(iota((8, LANES), 0) == 0, line_in, line_out)
     start(z1, h, zpeer, True, z1s, z1r)
     cs_in = jnp.sum(sq_in, axis=0, keepdims=True)
-    rs_out = jnp.sum(sq_out, axis=0, keepdims=True)
     n_ci = -(-cph // LANES)
     n_ro = -(-oph // LANES)
     line[...] = jnp.zeros_like(line)
@@ -1553,8 +1564,6 @@
     for i in range(n_ci + n_ro):
         p1[s, i : i + 1, :] = line[0:1, i * LANES : (i + 1) * LANES]
     start(p1, s, speer, False, p1s, p1r)
-    spl[s] = arrive(szin, zpeer, True, szs, szr)
-    start(spl, s, speer, False, sps, spr)
     sums = arrive(z1, zpeer, True, z1s, z1r)
     line_r = DECAY * row_in[...].reshape(1, rin) + decay_keep * (sums[0:1, 0:rin] / PROJ + EPS_SQUARE)
     line_c = DECAY * col_out[...].reshape(1, rin) + decay_keep * (sums[1:2, 0:rin] / INNER + EPS_SQUARE)
@@ -1572,8 +1581,8 @@
     )
     col_in_new[...] = line_ci.reshape(cph)
     row_out_new[...] = line_ro.reshape(oph)
-    u_in = g_in * lax.rsqrt(up_r * line_ci)
-    u_out = g_out * lax.rsqrt(up_c * line_ro)
+    u_in = g_in * (lax.rsqrt(up_r) * lax.rsqrt(line_ci))
+    u_out = g_out * (lax.rsqrt(up_c) * lax.rsqrt(line_ro))
     lane = iota((8, LANES), 1)
     values = (
         jnp.sum(u_in * u_in, keepdims=True),

time: 186 us -> 179 us (0.962)
  Pallas kernels: 184 us -> 178 us
    pallas_call x1, Pallas kernels: 93.5 us -> 90 us  [rear(): pl.pallas_call(functools.partial(rear_kernel, n_s, n_h, cph, oph, rin, rp...]
    pallas_call x1, Pallas kernels: 87.2 us -> 84.3 us  [fore(): pl.pallas_call(functools.partial(fore_kernel, n_s, n_h, cph, oph, rin, rp...]
where the time goes in v6:
time: 179 us
  Pallas kernels  178 us (99%)
    pallas_call x1, Pallas kernels, rear(): pl.pallas_call(functools.partial(rear_kernel, n_s, n_h, cph, oph, rin, rp...  90 us
    pallas_call x1, Pallas kernels, fore(): pl.pallas_call(functools.partial(fore_kernel, n_s, n_h, cph, oph, rin, rp...  84.3 us

profile of v6, /device:TPU:0, one launch (start us, length us, event | category | flops | bytes accessed | tf_op | source)
XLA Modules:
  0.0 179.2 jit_solution(6608519783124990939)
XLA Ops:
  1.3 84.3 %fore.1 = (bf16[384,768]{1,0:T(8,128)(2,1)}, bf16[768,3328]{1,0:T(8,128)(2,1)}, bf16[384,768]{1,0:T(8,128)(2,1)}, bf16[400,1664]{1,0:T(8,128)(2,1)}, bf16[384,16...) custom-call(bf16[384,768]{1,0:T(8,128)(2,1)} %x.3, ...), custom_call_target="tpu_custom_call" | custom-call | tf_op jit(solution)/shard_map/fore/pallas_call | solution.py:891
  85.6 90.0 %rear.1 = (f32[384,768]{1,0:T(8,128)}, f32[96,806]{1,0:T(8,128)}, f32[96]{0:T(128)}, f32[806]{0:T(1024)}, f32[96,806]{1,0:T(8,128)}, /*index=5*/f32[96,384]{1,0:...) custom-call(bf16[384,768]{1,0:T(8,128)(2,1)} %x.3, ...), custom_call_target="tpu_custom_call" | custom-call | tf_op jit(solution)/shard_map/rear/pallas_call | solution.py:1676
  175.6 3.4 %results.1 = (bf16[384,768]{1,0:T(8,128)(2,1)}, f32[384,768]{1,0:T(8,128)}, f32[96,806]{1,0:T(8,128)}, f32[96]{0:T(128)}, f32[806]{0:T(1024)}, /*index=5*/f32[96...) custom-call(bf16[384,768]{1,0:T(8,128)(2,1)} %get-tuple-element.57.r, ...), custom_call_target="tpu_custom_call" | custom-call | tf_op jit(solution)/shard_map/results/pallas_call | solution.py:1779
